TPU v7x, 256 devices: a whole 4x4x8 slice. The times are simulated.
256 devices in a mesh: section: 8 (over z), expert: 32 (over x, y, core).
Axes of the slice: x: 4, y: 4, z: 8, core: 2. Of those that a mesh axis runs over, the one named last changes fastest.
Arguments:
- tokens_a: bfloat16 [8, 4096, 2048], P('section', 'expert'), may hold values from -6 to 6
- routes_a: int32 [8, 4096, 8], P('section', 'expert'), may hold values from 0 to 31, all different within a row; in each aligned block of 128 rows (0 to 127, 128 to 255, ..., all dimensions but the last counted through in order) at most 40 rows name the same one
- gates_a: float32 [8, 4096, 8], P('section', 'expert'), may hold values from 0.05 to 0.5
- w_gate: bfloat16 [8, 32, 2048, 768], P('section', 'expert'), may hold values from -0.125 to 0.125
- w_up: bfloat16 [8, 32, 2048, 768], P('section', 'expert'), may hold values from -0.125 to 0.125
- w_down: bfloat16 [8, 32, 768, 2048], P('section', 'expert'), may hold values from -0.21875 to 0.21875
Outputs:
- next_input: bfloat16 [8, 4096, 2048], P('section', 'expert')
Inputs may be any that keep to these rules, and one draw needn't show every extreme that they name: `routes_a`: each row names 8 different experts; in each aligned block of 128 rows (the tokens of one device) no expert is named by more than 40 rows, a bound that some block reaches.
All inputs are finite; a program needn't handle non-finite values.
Results may differ from a plain program's by a relative error of at most 0.0075.
Values may be sent and summed in bfloat16 or wider, within the bound.
No kernel may reach another device: no remote copies, remote signals or barrier semaphores. Data moves between devices by JAX's collectives and lax.ppermute only.
A program may use at most 128 MiB of HBM per device.

v0:
```python
import jax
import jax.numpy as jnp
from jax import lax
from jax.sharding import PartitionSpec as P

EXPERTS = 32
CAP = 40


def shifted(block, axis, distance):
    devices = range(lax.axis_size(axis))
    route = [((i - distance) % len(devices), i) for i in devices]
    return lax.ppermute(block, axis, route)


def routing_tables(routes, gates, count, capacity):
    tok, top = routes.shape
    flat = routes.reshape(-1)
    onehot = (flat[:, None] == jnp.arange(count, dtype=jnp.int32)[None, :]).astype(jnp.int32)
    before = jnp.cumsum(onehot, axis=0) - onehot
    slot = jnp.sum(before * onehot, axis=1).reshape(tok, top)
    target = routes * capacity + slot
    columns = jnp.arange(count * capacity, dtype=jnp.int32)
    hits = target[:, :, None] == columns[None, None, :]
    spread = jnp.any(hits, axis=1).astype(jnp.bfloat16).T
    weights = jnp.sum(jnp.where(hits, gates[:, :, None], 0.0), axis=1)
    return (spread, weights)


def expert_forward(rows, w_gate, w_up, w_down):
    pre_g = jnp.einsum("lrd,ldf->lrf", rows, w_gate, preferred_element_type=jnp.float32)
    pre_u = jnp.einsum("lrd,ldf->lrf", rows, w_up, preferred_element_type=jnp.float32)
    hidden = (jax.nn.silu(pre_g) * pre_u).astype(jnp.bfloat16)
    return jnp.einsum("lrf,lfd->lrd", hidden, w_down, preferred_element_type=jnp.float32).astype(
        jnp.bfloat16
    )


def on_device(tokens_a, routes_a, gates_a, w_gate, w_up, w_down):
    count = EXPERTS
    capacity = CAP
    width = tokens_a.shape[2]
    own_a = tokens_a[0]
    spread_a, weights_a = routing_tables(routes_a[0], gates_a[0], count, capacity)
    send_a = jnp.dot(spread_a, own_a, preferred_element_type=jnp.float32).astype(jnp.bfloat16)
    rows_a = lax.all_to_all(
        send_a.reshape(count, capacity, width), "expert", split_axis=0, concat_axis=1, tiled=True
    )
    expert_out = expert_forward(rows_a, w_gate[0], w_up[0], w_down[0])
    back_a = lax.all_to_all(expert_out, "expert", split_axis=1, concat_axis=0, tiled=True)
    mixed_a = jnp.dot(
        weights_a, back_a.reshape(count * capacity, width), preferred_element_type=jnp.float32
    )
    layer_a = (own_a.astype(jnp.float32) + mixed_a).astype(jnp.bfloat16)
    return shifted(layer_a[None], "section", 1)


def solution(mesh):
    in_specs = (
        P("section", "expert", None),
        P("section", "expert", None),
        P("section", "expert", None),
        P("section", "expert", None, None),
        P("section", "expert", None, None),
        P("section", "expert", None, None),
    )
    out_specs = P("section", "expert", None)
    return jax.shard_map(
        on_device, mesh=mesh, in_specs=in_specs, out_specs=out_specs, check_vma=False
    )
```

profile of v0, /device:TPU:8, one launch (start us, length us, event | category | flops | bytes accessed | tf_op | source)
XLA Modules:
  0.0 296.5 jit_solution(7432188182627963781)
XLA Ops:
  0.0 0.0 copy-start
  0.0 0.9 copy.29
  0.9 0.1 eq.42
  1.0 0.1 eq.38
  1.1 9.0 %reduce-window.6 = s32[32,8,128]{2,1,0:T(8,128)S(1)} reduce-window(s32[32,8,128]{2,1,0:T(8,128)S(1)} %fusion.23, s32[]{:T(128)} %constant.6.clone.1), window={size=1x1x128 pad=0_0x0_0x127_0}, to_apply=%region_0.0 | reduce-window | flops 4161536 | bytes 262148 | tf_op jit(solution)/shard_map/reduce-window
  10.2 0.1 slice.8
  10.3 0.1 copy.32
  10.4 0.1 copy.33
  10.5 0.1 broadcast_add_fusion
  10.7 0.1 reshape.78
  10.8 1.6 fusion.4
  12.4 2.6 convolution_convert_fusion.1
  15.0 0.0 copy-start.3
  15.0 68.1 %all_to_all.8 = bf16[32,40,2048]{2,1,0:T(8,128)(2,1)S(1)} all-to-all(bf16[32,40,2048]{2,1,0:T(8,128)(2,1)S(1)} %bitcast.59), channel_id=1, replica_groups=mesh['section'=8,'expert'=32] {'expert'}, dimensions={0} | all-to-all | bytes 10485760 | tf_op jit(solution)/shard_map/all_to_all | solution.py:46
  83.1 0.0 copy-done.3
  83.1 4.2 %fusion.8 = f32[1280,768]{1,0:T(8,128)S(1)} fusion(bf16[1280,2048]{1,0:T(8,128)(2,1)S(1)} %bitcast.61, bf16[1,1,2048,768]{3,2,1,0:T(8,128)(2,1)S(1)} %copy-done.3), kind=kOutput, calls=%fused_computation.13 | convolution fusion | flops 4026531840 | bytes 12320768 | tf_op jit(solution)/shard_map/lrd,ldf->lrf/dot_general | solution.py:31
  87.4 0.0 copy-done.4
  87.4 4.6 %fusion.5 = bf16[1280,768]{1,0:T(8,128)(2,1)S(1)} fusion(bf16[1280,2048]{1,0:T(8,128)(2,1)S(1)} %bitcast.62, f32[1280,768]{1,0:T(8,128)S(1)} %fusion.8, bf16[1,1,2048,768]{3,2,1,0:T(8,128)(2,1)S(1)} %copy-done.4), kind=kOutput, calls=%fused_computation.10 | convolution fusion | flops 4032430080 | bytes 14286848 | tf_op jit(solution)/shard_map/lrd,ldf->lrf/dot_general | solution.py:32
  92.0 4.5 %fusion = bf16[1,1280,2048]{2,1,0:T(8,128)(2,1)S(1)} fusion(bf16[1280,768]{1,0:T(8,128)(2,1)S(1)} %fusion.5, bf16[1,1,768,2048]{3,2,1,0:T(8,128)(2,1)S(1)} %copy-done), kind=kOutput, calls=%fused_computation.2 | convolution fusion | flops 4029153280 | bytes 10354688 | tf_op jit(solution)/shard_map/lrf,lfd->lrd/dot_general | solution.py:34
  96.5 30.5 %copy.50 = bf16[1,1280,2048]{2,0,1:T(2,128)(2,1)} copy(bf16[1,1280,2048]{2,1,0:T(8,128)(2,1)S(1)} %fusion) | data formatting | bytes 10485760 | tf_op jit(solution)/shard_map/convert_element_type | solution.py:34
  127.0 0.5 broadcast.28
  127.5 33.1 %reduce = bf16[1280,2048]{1,0:T(8,128)(2,1)} reduce(bf16[1280,1,2048]{2,1,0:T(2,128)(2,1)} %bitcast.58, bf16[]{:T(256)} %broadcast.28), dimensions={1}, to_apply=%bitcast.57.reduce_sub_computation | reduce | bytes 10485762
  160.6 13.1 %reshape.85 = bf16[32,2,40960]{2,1,0:T(2,128)(2,1)} reshape(bf16[1280,2048]{1,0:T(8,128)(2,1)} %reduce) | data formatting | bytes 10485760
  173.7 6.1 %all-to-all-start.1 = ((bf16[32,2,40960]{2,1,0:T(2,128)(2,1)}), bf16[32,2,40960]{2,1,0:T(2,128)(2,1)}, u32[]{:S(2)}, u32[]{:S(2)}) async-start(bf16[32,2,40960]{2,1,0:T(2,128)(2,1)} %reshape.85), calls=%async_computation.1 | async-start | bytes 10485760 | tf_op jit(solution)/shard_map/all_to_all | solution.py:50
  179.8 0.1 copy.34
  179.9 1.7 select_reduce_fusion
  181.6 68.3 %all-to-all-done.1 = bf16[32,2,40960]{2,1,0:T(2,128)(2,1)} async-done(((bf16[32,2,40960]{2,1,0:T(2,128)(2,1)}), bf16[32,2,40960]{2,1,0:T(2,128)(2,1)}, u32[]{:S(2)}, u32[]{:S(2)}) %all-to-all-start.1) | async-done | bytes 5242912 | tf_op jit(solution)/shard_map/all_to_all | solution.py:50
  249.9 20.7 %reshape.86 = bf16[1280,1,2048]{2,1,0:T(2,128)(2,1)} reshape(bf16[32,2,40960]{2,1,0:T(2,128)(2,1)} %all-to-all-done.1) | data formatting | bytes 10485760
  270.6 7.4 %fusion.16 = bf16[1,128,2048]{2,1,0:T(8,128)(2,1)S(1)} fusion(bf16[128,1280]{1,0:T(8,128)(2,1)S(1)} %select_reduce_fusion, bf16[1,1280,2048]{2,0,1:T(2,128)(2,1)} %bitcast.60, bf16[1,128,2048]{2,1,0:T(8,128)(2,1)} %param.6), kind=kOutput, calls=%fused_computation.17 | convolution fusion | flops 671875072 | bytes 6619136 | tf_op jit(solution)/shard_map/dot_general | solution.py:51
  278.0 2.0 collective-permute-start
  280.0 15.7 %collective-permute-done = bf16[1,128,2048]{2,1,0:T(8,128)(2,1)S(1)} collective-permute-done((bf16[1,128,2048]{2,1,0:T(8,128)(2,1)S(1)}, bf16[1,128,2048]{2,1,0:T(8,128)(2,1)S(1)}, u32[]{:S(2)}, u32[]{:S(2)}) %collective-permute-start) | collective-permute-done | bytes 524320 | tf_op jit(solution)/shard_map/ppermute | solution.py:13
  295.7 0.8 copy.52
  (11 shorter events, 0.1 us)
Async XLA Ops:
  0.0 92.0 %copy-start = (bf16[1,1,768,2048]{3,2,1,0:T(8,128)(2,1)S(1)}, bf16[1,1,768,2048]{3,2,1,0:T(8,128)(2,1)}, u32[]{:S(2)}) copy-start(bf16[1,1,768,2048]{3,2,1,0:T(8,128)(2,1)} %param.11) | copy-start | bytes 9437188
  15.0 68.1 %copy-start.3 = (bf16[1,1,2048,768]{3,2,1,0:T(8,128)(2,1)S(1)}, bf16[1,1,2048,768]{3,2,1,0:T(8,128)(2,1)}, u32[]{:S(2)}) copy-start(bf16[1,1,2048,768]{3,2,1,0:T(8,128)(2,1)} %param.9) | copy-start | bytes 9437188
  83.1 4.3 %copy-start.4 = (bf16[1,1,2048,768]{3,2,1,0:T(8,128)(2,1)S(1)}, bf16[1,1,2048,768]{3,2,1,0:T(8,128)(2,1)}, u32[]{:S(2)}) copy-start(bf16[1,1,2048,768]{3,2,1,0:T(8,128)(2,1)} %param.10) | copy-start | bytes 9437188
  173.7 6.1 %copy-start.2 = (f32[1,128,8]{1,2,0:T(8,128)S(1)}, f32[1,128,8]{1,2,0:T(8,128)}, u32[]{:S(2)}) copy-start(f32[1,128,8]{1,2,0:T(8,128)} %param.8) | copy-start | bytes 12292
  173.7 76.2 %all-to-all-start.1 = ((bf16[32,2,40960]{2,1,0:T(2,128)(2,1)}), bf16[32,2,40960]{2,1,0:T(2,128)(2,1)}, u32[]{:S(2)}, u32[]{:S(2)}) async-start(bf16[32,2,40960]{2,1,0:T(2,128)(2,1)} %reshape.85), calls=%async_computation.1 | async-start | bytes 10485760 | tf_op jit(solution)/shard_map/all_to_all | solution.py:50
  270.6 25.9 %copy-start.1 = (bf16[1,1,768,2048]{3,2,1,0:T(8,128)(2,1)S(1)}, bf16[1,1,768,2048]{3,2,1,0:T(8,128)(2,1)}, u32[]{:S(2)}) copy-start(bf16[1,1,768,2048]{3,2,1,0:T(8,128)(2,1)} %param.11) | copy-start | bytes 9437188
  278.0 17.7 %collective-permute-start = (bf16[1,128,2048]{2,1,0:T(8,128)(2,1)S(1)}, bf16[1,128,2048]{2,1,0:T(8,128)(2,1)S(1)}, u32[]{:S(2)}, u32[]{:S(2)}) collective-permute-start(bf16[1,128,2048]{2,1,0:T(8,128)(2,1)S(1)} %fusion.16), channel_id=1, source_target_pairs={{224,0},{0,32},{32,64},{64,96},{96,128},{128,160},{160,192},{192,2... | collective-permute-start | bytes 1572872 | tf_op jit(solution)/shard_map/ppermute | solution.py:13
where the time goes:
time: 297 us; the launch traced here: 296 us
  waiting for transfers between devices  84 us (28%)
  blocking collectives  68.1 us (23%)
  local copies, waits for them, and re-layouts  67.2 us (23%)
  other arithmetic  45.6 us (15%)
  matrix products  23.4 us (8%)
  starting transfers between devices  8.1 us (3%)
    all_to_all x1, waiting for transfers between devices, on_device(): lax.all_to_all(expert_out, 'expert', split_axis=1, concat_axis=0, tiled=T...  68.3 us
    all_to_all x1, blocking collectives, on_device(): lax.all_to_all(send_a.reshape(count, capacity, width), 'expert', split_ax...  68.1 us
    unnamed x15, local copies, waits for them, and re-layouts  36 us
    unnamed x1, other arithmetic  33.1 us
    convert_element_type x1, local copies, waits for them, and re-layouts, expert_forward(): jnp.einsum('lrf,lfd->lrd', hidden, w_down, preferred_element_type=jnp.flo...  30.5 us
    ppermute x1, waiting for transfers between devices, shifted(): return lax.ppermute(block, axis, route)  15.7 us
    another operation x3, other arithmetic  9.15 us
    dot_general x1, matrix products, on_device(): jnp.dot(weights_a, back_a.reshape(count * capacity, width), preferred_ele...  7.43 us
  transfers between devices with their start and end apart: 2, of which 2 were waited for; matrix products, arithmetic and copies ran while one was open for 1% of the time, Pallas kernels for 0%

commit v1 on v0

v1 whole, which is shorter than its diff:
```python
import functools

import jax
import jax.numpy as jnp
from jax import lax
from jax.experimental import pallas as pl
from jax.experimental.pallas import tpu as pltpu
from jax.sharding import PartitionSpec as P

EXPERTS = 32
CAP = 40
SIDE = 4
TOK = 128
TOP = 8
D = 2048
FF = 768
HALF = 1024
TILE = 256
PAIR = 2 * CAP
TARGETS = [(d, flip) for d in (1, 3, 2, 0) for flip in (0, 1)]


def place(x, y, core):
    return ((x % SIDE) * SIDE + y % SIDE) * 2 + core % 2


def routes_of(step):
    return [
        (place(x, y, core), place(*step(x, y, core)))
        for x in range(SIDE)
        for y in range(SIDE)
        for core in range(2)
    ]


def gather_route(d):
    return routes_of(lambda x, y, core: (x + d, y, core) if core == 0 else (x, y + d, core))


def slot_route(d, flip):
    return routes_of(
        lambda x, y, core: (x, y + d, core + flip) if core == 0 else (x + d, y, core + flip)
    )


def back(route):
    return [(b, a) for a, b in route]


def target_experts():
    me = lax.axis_index("expert")
    x, y, core = me // (2 * SIDE), (me // 2) % SIDE, me % 2
    ids = [
        jnp.where(core == 0, place(x, y + d, core + flip), place(x + d, y, core + flip))
        for d, flip in TARGETS
    ]
    return jnp.stack(ids).astype(jnp.int32)


def tables_kernel(ids_ref, *refs):
    named_refs, spread, gather, slots = refs[0:4], refs[4], refs[5], refs[6]
    expert = lax.broadcasted_iota(jnp.int32, (EXPERTS, TOK), 0).astype(jnp.float32)
    earlier = lax.broadcasted_iota(jnp.int32, (TOK, TOK), 0) < lax.broadcasted_iota(
        jnp.int32, (TOK, TOK), 1
    )
    earlier = jnp.where(earlier, 1.0, 0.0).astype(jnp.bfloat16)
    for j, block in enumerate(named_refs):
        named = jnp.zeros((EXPERTS, TOK), jnp.float32)
        gate = jnp.zeros((EXPERTS, TOK), jnp.float32)
        for k in range(TOP):
            hit = expert == block[k : k + 1, :]
            named = named + jnp.where(hit, 1.0, 0.0)
            gate = gate + jnp.where(hit, block[TOP + k : TOP + k + 1, :], 0.0)
        before = jnp.dot(named.astype(jnp.bfloat16), earlier, preferred_element_type=jnp.float32)
        slots[j, 0:EXPERTS, :] = jnp.where(named > 0.0, before, -1.0)
        slots[j, EXPERTS : 2 * EXPERTS, :] = gate
    slot = lax.broadcasted_iota(jnp.int32, (CAP, TOK), 0).astype(jnp.float32)
    empty = jnp.zeros((CAP, TOK), jnp.float32)
    for pair in range(2):
        whole = []
        for i in range(len(TARGETS)):
            e = ids_ref[i]
            halves = []
            for j in (2 * pair, 2 * pair + 1):
                hit = slot == slots[j, pl.ds(e, 1), :]
                spread[j, i * CAP : (i + 1) * CAP, :] = jnp.where(hit, 1.0, 0.0)
                halves.append(jnp.where(hit, slots[j, pl.ds(e + EXPERTS, 1), :], 0.0))
            whole.append(jnp.concatenate([halves[0], empty], axis=1))
            whole.append(jnp.concatenate([empty, halves[1]], axis=1))
        gather[pair] = jnp.concatenate(whole, axis=0).T.astype(jnp.bfloat16)


VMEM = pl.BlockSpec(memory_space=pltpu.VMEM)
SMEM = pl.BlockSpec(memory_space=pltpu.SMEM)


def params(mib):
    return pltpu.CompilerParams(vmem_limit_bytes=mib << 20)


def slot_tables(ids, named):
    return pl.pallas_call(
        tables_kernel,
        out_shape=[
            jax.ShapeDtypeStruct((4, len(TARGETS) * CAP, TOK), jnp.float32),
            jax.ShapeDtypeStruct((2, 2 * TOK, len(TARGETS) * PAIR), jnp.bfloat16),
        ],
        in_specs=[SMEM] + [VMEM] * 4,
        out_specs=[VMEM] * 2,
        scratch_shapes=[pltpu.VMEM((4, 2 * EXPERTS, TOK), jnp.float32)],
        compiler_params=params(16),
        cost_estimate=pl.CostEstimate(flops=1 << 30, bytes_accessed=0, transcendentals=0),
        name="tables",
    )(ids, *named)


def fill_kernel(first, spread, *refs):
    tokens, outs = refs[0:4], refs[4:]
    rows = pl.ds(first * CAP, len(outs) * CAP)
    for t in range(D // TILE):
        cut = pl.ds(t * TILE, TILE)
        made = [
            jnp.dot(
                spread[j, rows, :].astype(jnp.bfloat16),
                tokens[j][:, cut],
                preferred_element_type=jnp.float32,
            )
            for j in range(4)
        ]
        for i, out in enumerate(outs):
            out[:, cut] = jnp.concatenate(
                [m[i * CAP : (i + 1) * CAP] for m in made], axis=0
            ).astype(jnp.bfloat16)


def fill_slots(spread, tokens, first, count):
    return pl.pallas_call(
        functools.partial(fill_kernel, first),
        out_shape=[jax.ShapeDtypeStruct((2 * PAIR, D), jnp.bfloat16)] * count,
        in_specs=[VMEM] * 5,
        out_specs=[VMEM] * count,
        compiler_params=params(16),
        cost_estimate=pl.CostEstimate(flops=1 << 30, bytes_accessed=0, transcendentals=0),
        name="fill",
    )(spread, *tokens)


def combine_kernel(half, *refs):
    weights, rows, outs, gathered = refs[0], refs[1:9], refs[9:13], refs[13]
    for pair in range(2):
        for t in range(HALF // (2 * TILE)):
            cut = pl.ds(t * 2 * TILE, 2 * TILE)
            source = pl.ds(half * HALF + t * 2 * TILE, 2 * TILE)
            for i in range(len(TARGETS)):
                gathered[i * PAIR : (i + 1) * PAIR, :] = rows[i][
                    pair * PAIR : (pair + 1) * PAIR, source
                ]
            mixed = jnp.dot(weights[pair], gathered[...], preferred_element_type=jnp.float32)
            outs[2 * pair][:, cut] = mixed[0:TOK].astype(jnp.bfloat16)
            outs[2 * pair + 1][:, cut] = mixed[TOK : 2 * TOK].astype(jnp.bfloat16)


def combine(weights, rows, half):
    return pl.pallas_call(
        functools.partial(combine_kernel, half),
        out_shape=[jax.ShapeDtypeStruct((TOK, HALF), jnp.bfloat16)] * 4,
        in_specs=[VMEM] * 9,
        out_specs=[VMEM] * 4,
        scratch_shapes=[pltpu.VMEM((len(TARGETS) * PAIR, 2 * TILE), jnp.bfloat16)],
        compiler_params=params(16),
        cost_estimate=pl.CostEstimate(flops=1 << 31, bytes_accessed=0, transcendentals=0),
        name="combine",
    )(weights, *rows)


def expert_kernel(*refs):
    n = (len(refs) - 4) // 2
    rows, (w_gate, w_up, w_down), outs, hidden = refs[:n], refs[n : n + 3], refs[n + 3 : -1], refs[-1]
    for f in range(FF // TILE):
        cut = pl.ds(f * TILE, TILE)
        block = jnp.concatenate([r[...] for r in rows], axis=0)
        pre_g = jnp.dot(block, w_gate[:, cut], preferred_element_type=jnp.float32)
        pre_u = jnp.dot(block, w_up[:, cut], preferred_element_type=jnp.float32)
        hidden[:, cut] = (pre_g / (1.0 + jnp.exp(-pre_g)) * pre_u).astype(jnp.bfloat16)
    for t in range(D // (2 * TILE)):
        cut = pl.ds(t * 2 * TILE, 2 * TILE)
        done = jnp.dot(hidden[...], w_down[:, cut], preferred_element_type=jnp.float32)
        at = 0
        for out in outs:
            out[:, cut] = done[at : at + out.shape[0]].astype(jnp.bfloat16)
            at += out.shape[0]


def expert_forward(rows, w_gate, w_up, w_down):
    total = sum(r.shape[0] for r in rows)
    return pl.pallas_call(
        expert_kernel,
        out_shape=[jax.ShapeDtypeStruct(r.shape, jnp.bfloat16) for r in rows],
        in_specs=[VMEM] * (len(rows) + 3),
        out_specs=[VMEM] * len(rows),
        scratch_shapes=[pltpu.VMEM((total, FF), jnp.bfloat16)],
        compiler_params=params(16),
        cost_estimate=pl.CostEstimate(flops=6 * total * D * FF, bytes_accessed=0, transcendentals=0),
        name="expert",
    )(*rows, w_gate, w_up, w_down)


def on_device(tokens_a, routes_a, gates_a, w_gate, w_up, w_down):
    own = tokens_a[0]
    send = functools.partial(lax.ppermute, axis_name="expert")
    steps = (1, 3, 2)
    named = jnp.concatenate([routes_a[0].astype(jnp.float32).T, gates_a[0].T])
    named = [named] + [send(named, perm=gather_route(d)) for d in steps]
    tokens = [own] + [send(own, perm=gather_route(d)) for d in steps]
    spread, weights = slot_tables(target_experts(), named)
    filled = fill_slots(spread, tokens, 0, 4) + fill_slots(spread, tokens, 4, 4)
    results = [None] * len(TARGETS)
    for n in (6, 0, 2, 4):
        arrived = [
            filled[i] if TARGETS[i] == (0, 0) else send(filled[i], perm=slot_route(*TARGETS[i]))
            for i in (n, n + 1)
        ]
        done = expert_forward(arrived, w_gate[0, 0], w_up[0, 0], w_down[0, 0])
        for i, out in zip((n, n + 1), done):
            results[i] = (
                out if TARGETS[i] == (0, 0) else send(out, perm=back(slot_route(*TARGETS[i])))
            )
    count = lax.axis_size("section")
    onward = [((i - 1) % count, i) for i in range(count)]
    moved = []
    for half in range(2):
        partial = combine(weights, results, half)
        mixed = own[:, half * HALF : (half + 1) * HALF].astype(jnp.float32)
        mixed = mixed + partial[0].astype(jnp.float32)
        for d, block in zip(steps, partial[1:]):
            mixed = mixed + send(block, perm=back(gather_route(d))).astype(jnp.float32)
        moved.append(lax.ppermute(mixed.astype(jnp.bfloat16), "section", onward))
    return jnp.concatenate(moved, axis=1)[None]


def solution(mesh):
    in_specs = (
        P("section", "expert", None),
        P("section", "expert", None),
        P("section", "expert", None),
        P("section", "expert", None, None),
        P("section", "expert", None, None),
        P("section", "expert", None, None),
    )
    out_specs = P("section", "expert", None)
    return jax.shard_map(
        on_device, mesh=mesh, in_specs=in_specs, out_specs=out_specs, check_vma=False
    )
```

time: 297 us -> 132 us (0.44)
  blocking collectives: 68.1 us -> 0 us
  local copies, waits for them, and re-layouts: 67.2 us -> 0.1 us
  starting transfers between devices: 8.1 us -> 52 us
  other arithmetic: 45.6 us -> 2.67 us
  waiting for transfers between devices: 84 us -> 58.3 us
  matrix products: 23.4 us -> 0 us
  Pallas kernels: 0 us -> 17.5 us
    all_to_all x1 -> x0, waiting for transfers between devices: 68.3 us -> none  [on_device(): lax.all_to_all(expert_out, 'expert', split_axis=1, concat_axis=0, tiled=T...]
    all_to_all x1 -> x0, blocking collectives: 68.1 us -> none  [on_device(): lax.all_to_all(send_a.reshape(count, capacity, width), 'expert', split_ax...]
    ppermute x1 -> x28, starting transfers between devices: 1.99 us -> 52 us  [the longest x7 21.9 us: on_device(): send(out, perm=back(slot_route(*TARGETS[i])))]
    ppermute x1 -> x28, waiting for transfers between devices: 15.7 us -> 58.3 us  [the longest x7 17.4 us: on_device(): send(out, perm=back(slot_route(*TARGETS[i])))]
    unnamed x15 -> x8, local copies, waits for them, and re-layouts: 36 us -> 0.02 us
    unnamed x1 -> x0, other arithmetic: 33.1 us -> none
    convert_element_type x1 -> x0, local copies, waits for them, and re-layouts: 30.5 us -> none  [expert_forward(): jnp.einsum('lrf,lfd->lrd', hidden, w_down, preferred_element_type=jnp.flo...]
    dot_general x5 -> x0, matrix products: 23.4 us -> none  [the longest x1 7.43 us: on_device(): jnp.dot(weights_a, back_a.reshape(count * capacity, width), preferred_ele...]
  transfers between devices with their start and end apart: 2 -> 28, of which waited for: 2 -> 13; matrix products, arithmetic and copies ran while one was open for 1% -> 1% of each run, Pallas kernels for 0% -> 12%
where the time goes in v1:
time: 132 us; the launch traced here: 131 us
  waiting for transfers between devices  58.3 us (44%)
  starting transfers between devices  52 us (39%)
  Pallas kernels  17.5 us (13%)
  other arithmetic  2.67 us (2%)
    ppermute x7, starting transfers between devices, on_device(): send(out, perm=back(slot_route(*TARGETS[i])))  21.9 us
    ppermute x7, waiting for transfers between devices, on_device(): send(out, perm=back(slot_route(*TARGETS[i])))  17.4 us
    ppermute x2, waiting for transfers between devices, on_device(): moved.append(lax.ppermute(mixed.astype(jnp.bfloat16), 'section', onward))  13.1 us
    pallas_call x4, Pallas kernels, expert_forward(): pl.pallas_call(expert_kernel, out_shape=[jax.ShapeDtypeStruct(r.shape, jn...  12.9 us
    ppermute x3, waiting for transfers between devices, on_device(): named = [named] + [send(named, perm=gather_route(d)) for d in steps]  10.2 us
    ppermute x6, starting transfers between devices, on_device(): mixed = mixed + send(block, perm=back(gather_route(d))).astype(jnp.float32)  9.28 us
    ppermute x6, waiting for transfers between devices, on_device(): mixed = mixed + send(block, perm=back(gather_route(d))).astype(jnp.float32)  8.78 us
    ppermute x7, waiting for transfers between devices, on_device(): send(filled[i], perm=slot_route(*TARGETS[i]))  8.77 us
  transfers between devices with their start and end apart: 28, of which 13 were waited for; matrix products, arithmetic and copies ran while one was open for 1% of the time, Pallas kernels for 12%

profile of v1, /device:TPU:8, one launch (start us, length us, event | category | flops | bytes accessed | tf_op | source)
XLA Modules:
  0.0 130.7 jit_solution(15825928573316644012)
XLA Ops:
  0.0 3.0 %collective-permute-start.5 = (bf16[128,2048]{1,0:T(8,128)(2,1)}, bf16[128,2048]{1,0:T(8,128)(2,1)S(1)}, u32[]{:S(2)}, u32[]{:S(2)}) collective-permute-start(bf16[128,2048]{1,0:T(8,128)(2,1)} %bitcast.21), channel_id=1, source_target_pairs={{0,16},{1,5},{2,18},{3,7},{4,20},{5,1},{6,22},{7,3},{8,24},{9,13},... | collective-permute-start | bytes 1572872 | tf_op jit(solution)/shard_map/ppermute | solution.py:214
  3.0 1.1 collective-permute-start.4
  7.1 2.6 %collective-permute-start.1 = (f32[16,128]{1,0:T(8,128)S(1)}, f32[16,128]{1,0:T(8,128)S(1)}, u32[]{:S(2)}, u32[]{:S(2)}) collective-permute-start(f32[16,128]{1,0:T(8,128)S(1)} %pad_maximum_fusion.refs_0_), channel_id=1, source_target_pairs={{0,24},{1,7},{2,26},{3,1},{4,28},{5,3},{6,30},{7,5},{8,0},{9,15},{... | collective-permute-start | bytes 24584 | tf_op jit(solution)/shard_map/ppermute | solution.py:213
  9.7 6.9 %collective-permute-done.2.refs_3_ = f32[16,128]{1,0:T(8,128)S(1)} collective-permute-done((f32[16,128]{1,0:T(8,128)S(1)}, f32[16,128]{1,0:T(8,128)S(1)}, u32[]{:S(2)}, u32[]{:S(2)}) %collective-permute-start.2) | collective-permute-done | bytes 8224 | tf_op jit(solution)/shard_map/ppermute | solution.py:213
  16.6 1.6 %collective-permute-start = (f32[16,128]{1,0:T(8,128)S(1)}, f32[16,128]{1,0:T(8,128)S(1)}, u32[]{:S(2)}, u32[]{:S(2)}) collective-permute-start(f32[16,128]{1,0:T(8,128)S(1)} %pad_maximum_fusion.refs_0_), channel_id=1, source_target_pairs={{0,8},{1,3},{2,10},{3,5},{4,12},{5,7},{6,14},{7,1},{8,16},{9,11},{... | collective-permute-start | bytes 24584 | tf_op jit(solution)/shard_map/ppermute | solution.py:213
  18.3 3.2 %collective-permute-done.refs_1_ = f32[16,128]{1,0:T(8,128)S(1)} collective-permute-done((f32[16,128]{1,0:T(8,128)S(1)}, f32[16,128]{1,0:T(8,128)S(1)}, u32[]{:S(2)}, u32[]{:S(2)}) %collective-permute-start) | collective-permute-done | bytes 8224 | tf_op jit(solution)/shard_map/ppermute | solution.py:213
  23.4 1.7 %collective-permute-start.6 = (bf16[160,2048]{1,0:T(8,128)(2,1)S(1)}, bf16[160,2048]{1,0:T(8,128)(2,1)S(1)}, u32[]{:S(2)}, u32[]{:S(2)}) collective-permute-start(bf16[160,2048]{1,0:T(8,128)(2,1)S(1)} %get-tuple-element.33), channel_id=1, source_target_pairs={{0,2},{1,9},{2,4},{3,11},{4,6},{5,13},{6,0},{7,15},{8,10},{9,17},{... | collective-permute-start | bytes 1966088 | tf_op jit(solution)/shard_map/ppermute | solution.py:220
  25.9 2.6 %collective-permute-start.11 = (bf16[160,2048]{1,0:T(8,128)(2,1)S(1)}, bf16[160,2048]{1,0:T(8,128)(2,1)S(1)}, u32[]{:S(2)}, u32[]{:S(2)}) collective-permute-start(bf16[160,2048]{1,0:T(8,128)(2,1)S(1)} %get-tuple-element.38), channel_id=1, source_target_pairs={{0,7},{1,24},{2,1},{3,26},{4,3},{5,28},{6,5},{7,30},{8,15},{9,0},{... | collective-permute-start | bytes 1966088 | tf_op jit(solution)/shard_map/ppermute | solution.py:220
  29.3 2.1 %collective-permute-start.14 = (bf16[160,2048]{1,0:T(8,128)(2,1)S(1)}, bf16[160,2048]{1,0:T(8,128)(2,1)S(1)}, u32[]{:S(2)}, u32[]{:S(2)}) collective-permute-start(bf16[160,2048]{1,0:T(8,128)(2,1)S(1)} %get-tuple-element.41), channel_id=1, source_target_pairs={{0,4},{1,17},{2,6},{3,19},{4,0},{5,21},{6,2},{7,23},{8,12},{9,25},... | collective-permute-start | bytes 1966088 | tf_op jit(solution)/shard_map/ppermute | solution.py:220
  31.4 2.8 %collective-permute-done.6.refs_0_ = bf16[160,2048]{1,0:T(8,128)(2,1)S(1)} collective-permute-done((bf16[160,2048]{1,0:T(8,128)(2,1)S(1)}, bf16[160,2048]{1,0:T(8,128)(2,1)S(1)}, u32[]{:S(2)}, u32[]{:S(2)}) %collective-permute-start.6) | collective-permute-done | bytes 655392 | tf_op jit(solution)/shard_map/ppermute | solution.py:220
  34.3 5.9 %collective-permute-done.7.refs_1_ = bf16[160,2048]{1,0:T(8,128)(2,1)S(1)} collective-permute-done((bf16[160,2048]{1,0:T(8,128)(2,1)S(1)}, bf16[160,2048]{1,0:T(8,128)(2,1)S(1)}, u32[]{:S(2)}, u32[]{:S(2)}) %collective-permute-start.7) | collective-permute-done | bytes 655392 | tf_op jit(solution)/shard_map/ppermute | solution.py:220
  40.2 1.2 collective-permute-start.18
  41.4 3.2 %expert.4 = (bf16[160,2048]{1,0:T(8,128)(2,1)S(1)}, bf16[160,2048]{1,0:T(8,128)(2,1)S(1)}) custom-call(bf16[160,2048]{1,0:T(8,128)(2,1)S(1)} %collective-permute-done.6.refs_0_, bf16[160,2048]{1,0:T(8,128)(2,1)S(1)} %collective-permute-done.7.refs_1_, bf16[2048,768]{1,0:T(8,128)(2,1)S(1)} %bitcast.27, bf16[2048,768]{1,0:T(8,128)(2,1)S(1)} %bitcast.31, ...), custom_call_target="tpu_custom_call" | custom-call | flops 3019898880 | tf_op jit(solution)/shard_map/expert/pallas_call | solution.py:196
  44.6 17.1 %collective-permute-start.8 = (bf16[160,2048]{1,0:T(8,128)(2,1)S(1)}, bf16[160,2048]{1,0:T(8,128)(2,1)S(1)}, u32[]{:S(2)}, u32[]{:S(2)}) collective-permute-start(bf16[160,2048]{1,0:T(8,128)(2,1)S(1)} %get-tuple-element.35), channel_id=1, source_target_pairs={{2,0},{9,1},{4,2},{11,3},{6,4},{13,5},{0,6},{15,7},{10,8},{17,9},{... | collective-permute-start | bytes 1966088 | tf_op jit(solution)/shard_map/ppermute | solution.py:226
  61.7 3.2 %expert.5 = (bf16[160,2048]{1,0:T(8,128)(2,1)S(1)}, bf16[160,2048]{1,0:T(8,128)(2,1)S(1)}) custom-call(bf16[160,2048]{1,0:T(8,128)(2,1)S(1)} %collective-permute-done.10.refs_0_, bf16[160,2048]{1,0:T(8,128)(2,1)S(1)} %collective-permute-done.11.refs_1_, bf16[2048,768]{1,0:T(8,128)(2,1)S(1)} %bitcast.28, bf16[2048,768]{1,0:T(8,128)(2,1)S(1)} %bitcast.32, ...), custom_call_target="tpu_custom_call" | custom-call | flops 3019898880 | tf_op jit(solution)/shard_map/expert/pallas_call | solution.py:196
  65.1 3.2 %expert.6 = (bf16[160,2048]{1,0:T(8,128)(2,1)S(1)}, bf16[160,2048]{1,0:T(8,128)(2,1)S(1)}) custom-call(bf16[160,2048]{1,0:T(8,128)(2,1)S(1)} %collective-permute-done.14.refs_0_, bf16[160,2048]{1,0:T(8,128)(2,1)S(1)} %collective-permute-done.15.refs_1_, bf16[2048,768]{1,0:T(8,128)(2,1)S(1)} %bitcast.29, bf16[2048,768]{1,0:T(8,128)(2,1)S(1)} %bitcast.33, ...), custom_call_target="tpu_custom_call" | custom-call | flops 3019898880 | tf_op jit(solution)/shard_map/expert/pallas_call | solution.py:196
  68.4 2.2 %collective-permute-start.16 = (bf16[160,2048]{1,0:T(8,128)(2,1)S(1)}, bf16[160,2048]{1,0:T(8,128)(2,1)S(1)}, u32[]{:S(2)}, u32[]{:S(2)}) collective-permute-start(bf16[160,2048]{1,0:T(8,128)(2,1)S(1)} %get-tuple-element.43), channel_id=1, source_target_pairs={{4,0},{17,1},{6,2},{19,3},{0,4},{21,5},{2,6},{23,7},{12,8},{25,9},... | collective-permute-start | bytes 1966088 | tf_op jit(solution)/shard_map/ppermute | solution.py:226
  70.5 3.2 %expert.7 = (bf16[160,2048]{1,0:T(8,128)(2,1)S(1)}, bf16[160,2048]{1,0:T(8,128)(2,1)S(1)}) custom-call(bf16[160,2048]{1,0:T(8,128)(2,1)S(1)} %get-tuple-element.45.refs_0_, bf16[160,2048]{1,0:T(8,128)(2,1)S(1)} %collective-permute-done.18.refs_1_, bf16[2048,768]{1,0:T(8,128)(2,1)S(1)} %bitcast.30, bf16[2048,768]{1,0:T(8,128)(2,1)S(1)} %bitcast.34, ...), custom_call_target="tpu_custom_call" | custom-call | flops 3019898880 | tf_op jit(solution)/shard_map/expert/pallas_call | solution.py:196
  73.7 2.6 %collective-permute-done.8.refs_1_ = bf16[160,2048]{1,0:T(8,128)(2,1)S(1)} collective-permute-done((bf16[160,2048]{1,0:T(8,128)(2,1)S(1)}, bf16[160,2048]{1,0:T(8,128)(2,1)S(1)}, u32[]{:S(2)}, u32[]{:S(2)}) %collective-permute-start.8) | collective-permute-done | bytes 655392 | tf_op jit(solution)/shard_map/ppermute | solution.py:226
  76.4 2.5 %collective-permute-start.19 = (bf16[160,2048]{1,0:T(8,128)(2,1)S(1)}, bf16[160,2048]{1,0:T(8,128)(2,1)S(1)}, u32[]{:S(2)}, u32[]{:S(2)}) collective-permute-start(bf16[160,2048]{1,0:T(8,128)(2,1)S(1)} %get-tuple-element.48), channel_id=1, source_target_pairs={{1,0},{0,1},{3,2},{2,3},{5,4},{4,5},{7,6},{6,7},{9,8},{8,9},{11,10... | collective-permute-start | bytes 1966088 | tf_op jit(solution)/shard_map/ppermute | solution.py:226
  78.9 3.6 %collective-permute-done.12.refs_3_ = bf16[160,2048]{1,0:T(8,128)(2,1)S(1)} collective-permute-done((bf16[160,2048]{1,0:T(8,128)(2,1)S(1)}, bf16[160,2048]{1,0:T(8,128)(2,1)S(1)}, u32[]{:S(2)}, u32[]{:S(2)}) %collective-permute-start.12) | collective-permute-done | bytes 655392 | tf_op jit(solution)/shard_map/ppermute | solution.py:226
  82.5 4.8 %collective-permute-done.16.refs_5_ = bf16[160,2048]{1,0:T(8,128)(2,1)S(1)} collective-permute-done((bf16[160,2048]{1,0:T(8,128)(2,1)S(1)}, bf16[160,2048]{1,0:T(8,128)(2,1)S(1)}, u32[]{:S(2)}, u32[]{:S(2)}) %collective-permute-start.16) | collective-permute-done | bytes 655392 | tf_op jit(solution)/shard_map/ppermute | solution.py:226
  87.4 6.3 %collective-permute-done.17.refs_6_ = bf16[160,2048]{1,0:T(8,128)(2,1)S(1)} collective-permute-done((bf16[160,2048]{1,0:T(8,128)(2,1)S(1)}, bf16[160,2048]{1,0:T(8,128)(2,1)S(1)}, u32[]{:S(2)}, u32[]{:S(2)}) %collective-permute-start.17) | collective-permute-done | bytes 655392 | tf_op jit(solution)/shard_map/ppermute | solution.py:226
  94.7 3.0 %collective-permute-start.24 = (bf16[128,1024]{1,0:T(8,128)(2,1)S(1)}, bf16[128,1024]{1,0:T(8,128)(2,1)S(1)}, u32[]{:S(2)}, u32[]{:S(2)}) collective-permute-start(bf16[128,1024]{1,0:T(8,128)(2,1)S(1)} %get-tuple-element.54), channel_id=1, source_target_pairs={{8,0},{3,1},{10,2},{5,3},{12,4},{7,5},{14,6},{1,7},{16,8},{11,9},{... | collective-permute-start | bytes 786440 | tf_op jit(solution)/shard_map/ppermute | solution.py:236
  97.7 1.6 %collective-permute-start.26 = (bf16[128,1024]{1,0:T(8,128)(2,1)S(1)}, bf16[128,1024]{1,0:T(8,128)(2,1)S(1)}, u32[]{:S(2)}, u32[]{:S(2)}) collective-permute-start(bf16[128,1024]{1,0:T(8,128)(2,1)S(1)} %get-tuple-element.56), channel_id=1, source_target_pairs={{16,0},{5,1},{18,2},{7,3},{20,4},{1,5},{22,6},{3,7},{24,8},{13,9},... | collective-permute-start | bytes 786440 | tf_op jit(solution)/shard_map/ppermute | solution.py:236
  100.3 1.8 %collective-permute-start.20 = (bf16[128,1024]{1,0:T(8,128)(2,1)S(1)}, bf16[128,1024]{1,0:T(8,128)(2,1)S(1)}, u32[]{:S(2)}, u32[]{:S(2)}) collective-permute-start(bf16[128,1024]{1,0:T(8,128)(2,1)S(1)} %get-tuple-element.50), channel_id=1, source_target_pairs={{8,0},{3,1},{10,2},{5,3},{12,4},{7,5},{14,6},{1,7},{16,8},{11,9},{... | collective-permute-start | bytes 786440 | tf_op jit(solution)/shard_map/ppermute | solution.py:236
  103.0 2.0 %collective-permute-start.22 = (bf16[128,1024]{1,0:T(8,128)(2,1)S(1)}, bf16[128,1024]{1,0:T(8,128)(2,1)S(1)}, u32[]{:S(2)}, u32[]{:S(2)}) collective-permute-start(bf16[128,1024]{1,0:T(8,128)(2,1)S(1)} %get-tuple-element.52), channel_id=1, source_target_pairs={{16,0},{5,1},{18,2},{7,3},{20,4},{1,5},{22,6},{3,7},{24,8},{13,9},... | collective-permute-start | bytes 786440 | tf_op jit(solution)/shard_map/ppermute | solution.py:236
  105.0 3.2 %collective-permute-done.25 = bf16[128,1024]{1,0:T(8,128)(2,1)S(1)} collective-permute-done((bf16[128,1024]{1,0:T(8,128)(2,1)S(1)}, bf16[128,1024]{1,0:T(8,128)(2,1)S(1)}, u32[]{:S(2)}, u32[]{:S(2)}) %collective-permute-start.25) | collective-permute-done | bytes 262176 | tf_op jit(solution)/shard_map/ppermute | solution.py:236
  109.0 4.7 %collective-permute-done.21 = bf16[128,1024]{1,0:T(8,128)(2,1)S(1)} collective-permute-done((bf16[128,1024]{1,0:T(8,128)(2,1)S(1)}, bf16[128,1024]{1,0:T(8,128)(2,1)S(1)}, u32[]{:S(2)}, u32[]{:S(2)}) %collective-permute-start.21) | collective-permute-done | bytes 262176 | tf_op jit(solution)/shard_map/ppermute | solution.py:236
  114.8 1.9 %collective-permute-start.27 = (bf16[128,1024]{1,0:T(8,128)(2,1)S(1)}, bf16[128,1024]{1,0:T(8,128)(2,1)S(1)}, u32[]{:S(2)}, u32[]{:S(2)}) collective-permute-start(bf16[128,1024]{1,0:T(8,128)(2,1)S(1)} %get-tuple-element.58), channel_id=1, source_target_pairs={{224,0},{0,32},{32,64},{64,96},{96,128},{128,160},{160,192},{192,2... | collective-permute-start | bytes 786440 | tf_op jit(solution)/shard_map/ppermute | solution.py:237
  116.8 9.2 %collective-permute-done.23 = bf16[128,1024]{1,0:T(8,128)(2,1)S(1)} collective-permute-done((bf16[128,1024]{1,0:T(8,128)(2,1)S(1)}, bf16[128,1024]{1,0:T(8,128)(2,1)S(1)}, u32[]{:S(2)}, u32[]{:S(2)}) %collective-permute-start.23) | collective-permute-done | bytes 262176 | tf_op jit(solution)/shard_map/ppermute | solution.py:237
  126.0 3.9 %collective-permute-done.27 = bf16[128,1024]{1,0:T(8,128)(2,1)S(1)} collective-permute-done((bf16[128,1024]{1,0:T(8,128)(2,1)S(1)}, bf16[128,1024]{1,0:T(8,128)(2,1)S(1)}, u32[]{:S(2)}, u32[]{:S(2)}) %collective-permute-start.27) | collective-permute-done | bytes 262176 | tf_op jit(solution)/shard_map/ppermute | solution.py:237
  (46 shorter events, 12.4 us)
Async XLA Ops:
  0.0 22.5 %copy-start = (bf16[1,128,2048]{2,1,0:T(8,128)(2,1)S(1)}, bf16[1,128,2048]{2,1,0:T(8,128)(2,1)}, u32[]{:S(2)}) copy-start(bf16[1,128,2048]{2,1,0:T(8,128)(2,1)} %param.6) | copy-start | bytes 1572868
  0.0 22.5 %collective-permute-start.5 = (bf16[128,2048]{1,0:T(8,128)(2,1)}, bf16[128,2048]{1,0:T(8,128)(2,1)S(1)}, u32[]{:S(2)}, u32[]{:S(2)}) collective-permute-start(bf16[128,2048]{1,0:T(8,128)(2,1)} %bitcast.21), channel_id=1, source_target_pairs={{0,16},{1,5},{2,18},{3,7},{4,20},{5,1},{6,22},{7,3},{8,24},{9,13},... | collective-permute-start | bytes 1572872 | tf_op jit(solution)/shard_map/ppermute | solution.py:214
  3.0 19.5 %collective-permute-start.4 = (bf16[128,2048]{1,0:T(8,128)(2,1)}, bf16[128,2048]{1,0:T(8,128)(2,1)S(1)}, u32[]{:S(2)}, u32[]{:S(2)}) collective-permute-start(bf16[128,2048]{1,0:T(8,128)(2,1)} %bitcast.22), channel_id=1, source_target_pairs={{0,24},{1,7},{2,26},{3,1},{4,28},{5,3},{6,30},{7,5},{8,0},{9,15},{... | collective-permute-start | bytes 1572872 | tf_op jit(solution)/shard_map/ppermute | solution.py:214
  4.2 18.3 %collective-permute-start.3 = (bf16[128,2048]{1,0:T(8,128)(2,1)}, bf16[128,2048]{1,0:T(8,128)(2,1)S(1)}, u32[]{:S(2)}, u32[]{:S(2)}) collective-permute-start(bf16[128,2048]{1,0:T(8,128)(2,1)} %bitcast.23), channel_id=1, source_target_pairs={{0,8},{1,3},{2,10},{3,5},{4,12},{5,7},{6,14},{7,1},{8,16},{9,11},{... | collective-permute-start | bytes 1572872 | tf_op jit(solution)/shard_map/ppermute | solution.py:214
  6.4 10.2 %collective-permute-start.2 = (f32[16,128]{1,0:T(8,128)S(1)}, f32[16,128]{1,0:T(8,128)S(1)}, u32[]{:S(2)}, u32[]{:S(2)}) collective-permute-start(f32[16,128]{1,0:T(8,128)S(1)} %pad_maximum_fusion.refs_0_), channel_id=1, source_target_pairs={{0,16},{1,5},{2,18},{3,7},{4,20},{5,1},{6,22},{7,3},{8,24},{9,13},... | collective-permute-start | bytes 24584 | tf_op jit(solution)/shard_map/ppermute | solution.py:213
  7.1 11.2 %collective-permute-start.1 = (f32[16,128]{1,0:T(8,128)S(1)}, f32[16,128]{1,0:T(8,128)S(1)}, u32[]{:S(2)}, u32[]{:S(2)}) collective-permute-start(f32[16,128]{1,0:T(8,128)S(1)} %pad_maximum_fusion.refs_0_), channel_id=1, source_target_pairs={{0,24},{1,7},{2,26},{3,1},{4,28},{5,3},{6,30},{7,5},{8,0},{9,15},{... | collective-permute-start | bytes 24584 | tf_op jit(solution)/shard_map/ppermute | solution.py:213
  16.6 4.9 %collective-permute-start = (f32[16,128]{1,0:T(8,128)S(1)}, f32[16,128]{1,0:T(8,128)S(1)}, u32[]{:S(2)}, u32[]{:S(2)}) collective-permute-start(f32[16,128]{1,0:T(8,128)S(1)} %pad_maximum_fusion.refs_0_), channel_id=1, source_target_pairs={{0,8},{1,3},{2,10},{3,5},{4,12},{5,7},{6,14},{7,1},{8,16},{9,11},{... | collective-permute-start | bytes 24584 | tf_op jit(solution)/shard_map/ppermute | solution.py:213
  21.5 19.9 %copy-start.3 = (bf16[1,1,768,2048]{3,2,1,0:T(8,128)(2,1)S(1)}, bf16[1,1,768,2048]{3,2,1,0:T(8,128)(2,1)}, u32[]{:S(2)}) copy-start(bf16[1,1,768,2048]{3,2,1,0:T(8,128)(2,1)} %param.11) | copy-start | bytes 9437188
  22.5 18.9 %copy-start.1 = (bf16[1,1,2048,768]{3,2,1,0:T(8,128)(2,1)S(1)}, bf16[1,1,2048,768]{3,2,1,0:T(8,128)(2,1)}, u32[]{:S(2)}) copy-start(bf16[1,1,2048,768]{3,2,1,0:T(8,128)(2,1)} %param.9) | copy-start | bytes 9437188
  22.5 18.9 %copy-start.2 = (bf16[1,1,2048,768]{3,2,1,0:T(8,128)(2,1)S(1)}, bf16[1,1,2048,768]{3,2,1,0:T(8,128)(2,1)}, u32[]{:S(2)}) copy-start(bf16[1,1,2048,768]{3,2,1,0:T(8,128)(2,1)} %param.10) | copy-start | bytes 9437188
  23.4 10.8 %collective-permute-start.6 = (bf16[160,2048]{1,0:T(8,128)(2,1)S(1)}, bf16[160,2048]{1,0:T(8,128)(2,1)S(1)}, u32[]{:S(2)}, u32[]{:S(2)}) collective-permute-start(bf16[160,2048]{1,0:T(8,128)(2,1)S(1)} %get-tuple-element.33), channel_id=1, source_target_pairs={{0,2},{1,9},{2,4},{3,11},{4,6},{5,13},{6,0},{7,15},{8,10},{9,17},{... | collective-permute-start | bytes 1966088 | tf_op jit(solution)/shard_map/ppermute | solution.py:220
  25.1 15.1 %collective-permute-start.7 = (bf16[160,2048]{1,0:T(8,128)(2,1)S(1)}, bf16[160,2048]{1,0:T(8,128)(2,1)S(1)}, u32[]{:S(2)}, u32[]{:S(2)}) collective-permute-start(bf16[160,2048]{1,0:T(8,128)(2,1)S(1)} %get-tuple-element.34), channel_id=1, source_target_pairs={{0,3},{1,8},{2,5},{3,10},{4,7},{5,12},{6,1},{7,14},{8,11},{9,16},{... | collective-permute-start | bytes 1966088 | tf_op jit(solution)/shard_map/ppermute | solution.py:220
  25.1 19.6 %collective-permute-start.10 = (bf16[160,2048]{1,0:T(8,128)(2,1)S(1)}, bf16[160,2048]{1,0:T(8,128)(2,1)S(1)}, u32[]{:S(2)}, u32[]{:S(2)}) collective-permute-start(bf16[160,2048]{1,0:T(8,128)(2,1)S(1)} %get-tuple-element.37), channel_id=1, source_target_pairs={{0,6},{1,25},{2,0},{3,27},{4,2},{5,29},{6,4},{7,31},{8,14},{9,1},{... | collective-permute-start | bytes 1966088 | tf_op jit(solution)/shard_map/ppermute | solution.py:220
  25.9 35.8 %collective-permute-start.11 = (bf16[160,2048]{1,0:T(8,128)(2,1)S(1)}, bf16[160,2048]{1,0:T(8,128)(2,1)S(1)}, u32[]{:S(2)}, u32[]{:S(2)}) collective-permute-start(bf16[160,2048]{1,0:T(8,128)(2,1)S(1)} %get-tuple-element.38), channel_id=1, source_target_pairs={{0,7},{1,24},{2,1},{3,26},{4,3},{5,28},{6,5},{7,30},{8,15},{9,0},{... | collective-permute-start | bytes 1966088 | tf_op jit(solution)/shard_map/ppermute | solution.py:220
  29.3 35.6 %collective-permute-start.14 = (bf16[160,2048]{1,0:T(8,128)(2,1)S(1)}, bf16[160,2048]{1,0:T(8,128)(2,1)S(1)}, u32[]{:S(2)}, u32[]{:S(2)}) collective-permute-start(bf16[160,2048]{1,0:T(8,128)(2,1)S(1)} %get-tuple-element.41), channel_id=1, source_target_pairs={{0,4},{1,17},{2,6},{3,19},{4,0},{5,21},{6,2},{7,23},{8,12},{9,25},... | collective-permute-start | bytes 1966088 | tf_op jit(solution)/shard_map/ppermute | solution.py:220
  34.3 30.8 %collective-permute-start.15 = (bf16[160,2048]{1,0:T(8,128)(2,1)S(1)}, bf16[160,2048]{1,0:T(8,128)(2,1)S(1)}, u32[]{:S(2)}, u32[]{:S(2)}) collective-permute-start(bf16[160,2048]{1,0:T(8,128)(2,1)S(1)} %get-tuple-element.42), channel_id=1, source_target_pairs={{0,5},{1,16},{2,7},{3,18},{4,1},{5,20},{6,3},{7,22},{8,13},{9,24},... | collective-permute-start | bytes 1966088 | tf_op jit(solution)/shard_map/ppermute | solution.py:220
  40.2 28.2 %collective-permute-start.18 = (bf16[160,2048]{1,0:T(8,128)(2,1)S(1)}, bf16[160,2048]{1,0:T(8,128)(2,1)S(1)}, u32[]{:S(2)}, u32[]{:S(2)}) collective-permute-start(bf16[160,2048]{1,0:T(8,128)(2,1)S(1)} %get-tuple-element.46), channel_id=1, source_target_pairs={{0,1},{1,0},{2,3},{3,2},{4,5},{5,4},{6,7},{7,6},{8,9},{9,8},{10,11... | collective-permute-start | bytes 1966088 | tf_op jit(solution)/shard_map/ppermute | solution.py:220
  44.6 31.7 %collective-permute-start.8 = (bf16[160,2048]{1,0:T(8,128)(2,1)S(1)}, bf16[160,2048]{1,0:T(8,128)(2,1)S(1)}, u32[]{:S(2)}, u32[]{:S(2)}) collective-permute-start(bf16[160,2048]{1,0:T(8,128)(2,1)S(1)} %get-tuple-element.35), channel_id=1, source_target_pairs={{2,0},{9,1},{4,2},{11,3},{6,4},{13,5},{0,6},{15,7},{10,8},{17,9},{... | collective-permute-start | bytes 1966088 | tf_op jit(solution)/shard_map/ppermute | solution.py:226
  61.7 14.7 %collective-permute-start.9 = (bf16[160,2048]{1,0:T(8,128)(2,1)S(1)}, bf16[160,2048]{1,0:T(8,128)(2,1)S(1)}, u32[]{:S(2)}, u32[]{:S(2)}) collective-permute-start(bf16[160,2048]{1,0:T(8,128)(2,1)S(1)} %get-tuple-element.36), channel_id=1, source_target_pairs={{3,0},{8,1},{5,2},{10,3},{7,4},{12,5},{1,6},{14,7},{11,8},{16,9},{... | collective-permute-start | bytes 1966088 | tf_op jit(solution)/shard_map/ppermute | solution.py:226
  64.9 17.6 %collective-permute-start.12 = (bf16[160,2048]{1,0:T(8,128)(2,1)S(1)}, bf16[160,2048]{1,0:T(8,128)(2,1)S(1)}, u32[]{:S(2)}, u32[]{:S(2)}) collective-permute-start(bf16[160,2048]{1,0:T(8,128)(2,1)S(1)} %get-tuple-element.39), channel_id=1, source_target_pairs={{6,0},{25,1},{0,2},{27,3},{2,4},{29,5},{4,6},{31,7},{14,8},{1,9},{... | collective-permute-start | bytes 1966088 | tf_op jit(solution)/shard_map/ppermute | solution.py:226
  65.0 17.5 %collective-permute-start.13 = (bf16[160,2048]{1,0:T(8,128)(2,1)S(1)}, bf16[160,2048]{1,0:T(8,128)(2,1)S(1)}, u32[]{:S(2)}, u32[]{:S(2)}) collective-permute-start(bf16[160,2048]{1,0:T(8,128)(2,1)S(1)} %get-tuple-element.40), channel_id=1, source_target_pairs={{7,0},{24,1},{1,2},{26,3},{3,4},{28,5},{5,6},{30,7},{15,8},{0,9},{... | collective-permute-start | bytes 1966088 | tf_op jit(solution)/shard_map/ppermute | solution.py:226
  68.4 19.0 %collective-permute-start.16 = (bf16[160,2048]{1,0:T(8,128)(2,1)S(1)}, bf16[160,2048]{1,0:T(8,128)(2,1)S(1)}, u32[]{:S(2)}, u32[]{:S(2)}) collective-permute-start(bf16[160,2048]{1,0:T(8,128)(2,1)S(1)} %get-tuple-element.43), channel_id=1, source_target_pairs={{4,0},{17,1},{6,2},{19,3},{0,4},{21,5},{2,6},{23,7},{12,8},{25,9},... | collective-permute-start | bytes 1966088 | tf_op jit(solution)/shard_map/ppermute | solution.py:226
  76.3 17.4 %collective-permute-start.17 = (bf16[160,2048]{1,0:T(8,128)(2,1)S(1)}, bf16[160,2048]{1,0:T(8,128)(2,1)S(1)}, u32[]{:S(2)}, u32[]{:S(2)}) collective-permute-start(bf16[160,2048]{1,0:T(8,128)(2,1)S(1)} %get-tuple-element.44), channel_id=1, source_target_pairs={{5,0},{16,1},{7,2},{18,3},{1,4},{20,5},{3,6},{22,7},{13,8},{24,9},... | collective-permute-start | bytes 1966088 | tf_op jit(solution)/shard_map/ppermute | solution.py:226
  76.4 17.4 %collective-permute-start.19 = (bf16[160,2048]{1,0:T(8,128)(2,1)S(1)}, bf16[160,2048]{1,0:T(8,128)(2,1)S(1)}, u32[]{:S(2)}, u32[]{:S(2)}) collective-permute-start(bf16[160,2048]{1,0:T(8,128)(2,1)S(1)} %get-tuple-element.48), channel_id=1, source_target_pairs={{1,0},{0,1},{3,2},{2,3},{5,4},{4,5},{7,6},{6,7},{9,8},{8,9},{11,10... | collective-permute-start | bytes 1966088 | tf_op jit(solution)/shard_map/ppermute | solution.py:226
  94.7 8.3 %collective-permute-start.24 = (bf16[128,1024]{1,0:T(8,128)(2,1)S(1)}, bf16[128,1024]{1,0:T(8,128)(2,1)S(1)}, u32[]{:S(2)}, u32[]{:S(2)}) collective-permute-start(bf16[128,1024]{1,0:T(8,128)(2,1)S(1)} %get-tuple-element.54), channel_id=1, source_target_pairs={{8,0},{3,1},{10,2},{5,3},{12,4},{7,5},{14,6},{1,7},{16,8},{11,9},{... | collective-permute-start | bytes 786440 | tf_op jit(solution)/shard_map/ppermute | solution.py:236
  97.7 10.4 %collective-permute-start.25 = (bf16[128,1024]{1,0:T(8,128)(2,1)S(1)}, bf16[128,1024]{1,0:T(8,128)(2,1)S(1)}, u32[]{:S(2)}, u32[]{:S(2)}) collective-permute-start(bf16[128,1024]{1,0:T(8,128)(2,1)S(1)} %get-tuple-element.55), channel_id=1, source_target_pairs={{24,0},{7,1},{26,2},{1,3},{28,4},{3,5},{30,6},{5,7},{0,8},{15,9},{... | collective-permute-start | bytes 786440 | tf_op jit(solution)/shard_map/ppermute | solution.py:236
  97.7 10.4 %collective-permute-start.26 = (bf16[128,1024]{1,0:T(8,128)(2,1)S(1)}, bf16[128,1024]{1,0:T(8,128)(2,1)S(1)}, u32[]{:S(2)}, u32[]{:S(2)}) collective-permute-start(bf16[128,1024]{1,0:T(8,128)(2,1)S(1)} %get-tuple-element.56), channel_id=1, source_target_pairs={{16,0},{5,1},{18,2},{7,3},{20,4},{1,5},{22,6},{3,7},{24,8},{13,9},... | collective-permute-start | bytes 786440 | tf_op jit(solution)/shard_map/ppermute | solution.py:236
  100.3 8.8 %collective-permute-start.20 = (bf16[128,1024]{1,0:T(8,128)(2,1)S(1)}, bf16[128,1024]{1,0:T(8,128)(2,1)S(1)}, u32[]{:S(2)}, u32[]{:S(2)}) collective-permute-start(bf16[128,1024]{1,0:T(8,128)(2,1)S(1)} %get-tuple-element.50), channel_id=1, source_target_pairs={{8,0},{3,1},{10,2},{5,3},{12,4},{7,5},{14,6},{1,7},{16,8},{11,9},{... | collective-permute-start | bytes 786440 | tf_op jit(solution)/shard_map/ppermute | solution.py:236
  102.0 11.7 %collective-permute-start.21 = (bf16[128,1024]{1,0:T(8,128)(2,1)S(1)}, bf16[128,1024]{1,0:T(8,128)(2,1)S(1)}, u32[]{:S(2)}, u32[]{:S(2)}) collective-permute-start(bf16[128,1024]{1,0:T(8,128)(2,1)S(1)} %get-tuple-element.51), channel_id=1, source_target_pairs={{24,0},{7,1},{26,2},{1,3},{28,4},{3,5},{30,6},{5,7},{0,8},{15,9},{... | collective-permute-start | bytes 786440 | tf_op jit(solution)/shard_map/ppermute | solution.py:236
  103.0 10.8 %collective-permute-start.22 = (bf16[128,1024]{1,0:T(8,128)(2,1)S(1)}, bf16[128,1024]{1,0:T(8,128)(2,1)S(1)}, u32[]{:S(2)}, u32[]{:S(2)}) collective-permute-start(bf16[128,1024]{1,0:T(8,128)(2,1)S(1)} %get-tuple-element.52), channel_id=1, source_target_pairs={{16,0},{5,1},{18,2},{7,3},{20,4},{1,5},{22,6},{3,7},{24,8},{13,9},... | collective-permute-start | bytes 786440 | tf_op jit(solution)/shard_map/ppermute | solution.py:236
  114.2 11.8 %collective-permute-start.23 = (bf16[128,1024]{1,0:T(8,128)(2,1)S(1)}, bf16[128,1024]{1,0:T(8,128)(2,1)S(1)}, u32[]{:S(2)}, u32[]{:S(2)}) collective-permute-start(bf16[128,1024]{1,0:T(8,128)(2,1)S(1)} %get-tuple-element.57), channel_id=1, source_target_pairs={{224,0},{0,32},{32,64},{64,96},{96,128},{128,160},{160,192},{192,2... | collective-permute-start | bytes 786440 | tf_op jit(solution)/shard_map/ppermute | solution.py:237
  114.8 15.1 %collective-permute-start.27 = (bf16[128,1024]{1,0:T(8,128)(2,1)S(1)}, bf16[128,1024]{1,0:T(8,128)(2,1)S(1)}, u32[]{:S(2)}, u32[]{:S(2)}) collective-permute-start(bf16[128,1024]{1,0:T(8,128)(2,1)S(1)} %get-tuple-element.58), channel_id=1, source_target_pairs={{224,0},{0,32},{32,64},{64,96},{96,128},{128,160},{160,192},{192,2... | collective-permute-start | bytes 786440 | tf_op jit(solution)/shard_map/ppermute | solution.py:237

commit v2 on v1

v2 whole, which is shorter than its diff:
```python
import functools

import jax
import jax.numpy as jnp
from jax import lax
from jax.experimental import pallas as pl
from jax.experimental.pallas import tpu as pltpu
from jax.sharding import PartitionSpec as P

EXPERTS = 32
CAP = 40
SIDE = 4
TOK = 128
TOP = 8
D = 2048
FF = 768
HALF = 1024
TILE = 256
PAIR = 2 * CAP
STEPS = (1, 3, 2)
TARGETS = [(d, flip) for d in (0, 1, 3, 2) for flip in (0, 1)]
VMEM = pl.BlockSpec(memory_space=pltpu.VMEM)
SMEM = pl.BlockSpec(memory_space=pltpu.SMEM)
ANY = pl.BlockSpec(memory_space=pl.ANY)


def place(x, y, core):
    return ((x % SIDE) * SIDE + y % SIDE) * 2 + core % 2


def routes_of(step):
    return [
        (place(x, y, core), place(*step(x, y, core)))
        for x in range(SIDE)
        for y in range(SIDE)
        for core in range(2)
    ]


def gather_route(d):
    return routes_of(lambda x, y, core: (x + d, y, core) if core == 0 else (x, y + d, core))


def slot_route(d, flip):
    return routes_of(
        lambda x, y, core: (x, y + d, core + flip) if core == 0 else (x + d, y, core + flip)
    )


def back(route):
    return [(b, a) for a, b in route]


def target_experts():
    me = lax.axis_index("expert")
    x, y, core = me // (2 * SIDE), (me // 2) % SIDE, me % 2
    ids = [
        jnp.where(core == 0, place(x, y + d, core + flip), place(x + d, y, core + flip))
        for d, flip in TARGETS
    ]
    return jnp.stack(ids).astype(jnp.int32)


def call(kernel, name, out_shape, args, scratch=(), after=(), flops=1 << 20):
    one = not isinstance(out_shape, list)
    count = 1 if one else len(out_shape)
    n = len(args)

    def body(*refs):
        kernel(*refs[:n], *refs[n + len(after) :])

    return pl.pallas_call(
        body,
        out_shape=out_shape,
        in_specs=[SMEM if a.dtype == jnp.int32 and a.ndim == 1 else VMEM for a in args]
        + [ANY] * len(after),
        out_specs=VMEM if one else [VMEM] * count,
        scratch_shapes=list(scratch),
        compiler_params=pltpu.CompilerParams(vmem_limit_bytes=16 << 20),
        cost_estimate=pl.CostEstimate(flops=flops, bytes_accessed=0, transcendentals=0),
        name=name,
    )(*args, *after)


def bf16(*shape):
    return jax.ShapeDtypeStruct(shape, jnp.bfloat16)


def f32(*shape):
    return jax.ShapeDtypeStruct(shape, jnp.float32)


def pack_kernel(own, routes, gates, packed, named, gated, sems):
    copies = [
        pltpu.make_async_copy(routes, named, sems.at[0]),
        pltpu.make_async_copy(gates, gated, sems.at[1]),
        pltpu.make_async_copy(own, packed.at[:, 0:D], sems.at[2]),
    ]
    for copy in copies:
        copy.start()
    packed[2 * TOP :, D:] = jnp.zeros((TOK - 2 * TOP, TOK), jnp.bfloat16)
    copies[0].wait()
    copies[1].wait()
    both = jnp.concatenate([named[...].astype(jnp.float32), gated[...]], axis=0)
    packed[0 : 2 * TOP, D:] = both.astype(jnp.bfloat16)
    copies[2].wait()


def slots_kernel(ids, *refs):
    blocks, (spread, slots) = refs[0:4], refs[4:]
    expert = lax.broadcasted_iota(jnp.int32, (EXPERTS, TOK), 0).astype(jnp.float32)
    earlier = lax.broadcasted_iota(jnp.int32, (TOK, TOK), 0) < lax.broadcasted_iota(
        jnp.int32, (TOK, TOK), 1
    )
    earlier = jnp.where(earlier, 1.0, 0.0).astype(jnp.bfloat16)
    slot = lax.broadcasted_iota(jnp.int32, (CAP, TOK), 0).astype(jnp.float32)
    for j in range(4):
        block = blocks[j][0 : 2 * TOP, D:].astype(jnp.float32)
        named = jnp.zeros((EXPERTS, TOK), jnp.float32)
        gate = jnp.zeros((EXPERTS, TOK), jnp.float32)
        for k in range(TOP):
            hit = expert == block[k : k + 1, :]
            named = named + jnp.where(hit, 1.0, 0.0)
            gate = gate + jnp.where(hit, block[TOP + k : TOP + k + 1, :], 0.0)
        before = jnp.dot(named.astype(jnp.bfloat16), earlier, preferred_element_type=jnp.float32)
        slots[j, 0:EXPERTS, :] = jnp.where(named > 0.0, before, -1.0)
        slots[j, EXPERTS : 2 * EXPERTS, :] = gate
        for i in range(len(TARGETS)):
            hit = slot == slots[j, pl.ds(ids[i], 1), :]
            spread[j, i * CAP : (i + 1) * CAP, :] = jnp.where(hit, 1.0, 0.0)


def weights_kernel(ids, slots, weights):
    slot = lax.broadcasted_iota(jnp.int32, (CAP, TOK), 0).astype(jnp.float32)
    empty = jnp.zeros((CAP, TOK), jnp.float32)
    for pair in range(2):
        whole = []
        for i in range(len(TARGETS)):
            halves = []
            for j in (2 * pair, 2 * pair + 1):
                hit = slot == slots[j, pl.ds(ids[i], 1), :]
                halves.append(jnp.where(hit, slots[j, pl.ds(ids[i] + EXPERTS, 1), :], 0.0))
            whole.append(jnp.concatenate([halves[0], empty], axis=1))
            whole.append(jnp.concatenate([empty, halves[1]], axis=1))
        weights[pair] = jnp.concatenate(whole, axis=0).T.astype(jnp.bfloat16)


def fill_kernel(first, spread, *refs):
    tokens, outs = refs[0:4], refs[4:]
    rows = pl.ds(first * CAP, len(outs) * CAP)
    for t in range(D // TILE):
        cut = pl.ds(t * TILE, TILE)
        made = [
            jnp.dot(
                spread[j, rows, :].astype(jnp.bfloat16),
                tokens[j][:, cut],
                preferred_element_type=jnp.float32,
            )
            for j in range(4)
        ]
        for i, out in enumerate(outs):
            out[:, cut] = jnp.concatenate(
                [m[i * CAP : (i + 1) * CAP] for m in made], axis=0
            ).astype(jnp.bfloat16)


def fill_slots(spread, tokens, first, count, after=()):
    kernel = functools.partial(fill_kernel, first)
    return call(kernel, "fill", [bf16(2 * PAIR, D)] * count, (spread, *tokens), after=after)


def expert_kernel(*refs):
    n = (len(refs) - 4) // 2
    rows, (w_gate, w_up, w_down), outs, hidden = refs[:n], refs[n : n + 3], refs[n + 3 : -1], refs[-1]
    for f in range(FF // TILE):
        cut = pl.ds(f * TILE, TILE)
        block = jnp.concatenate([r[...] for r in rows], axis=0)
        pre_g = jnp.dot(block, w_gate[:, cut], preferred_element_type=jnp.float32)
        pre_u = jnp.dot(block, w_up[:, cut], preferred_element_type=jnp.float32)
        hidden[:, cut] = (pre_g / (1.0 + jnp.exp(-pre_g)) * pre_u).astype(jnp.bfloat16)
    for t in range(D // (2 * TILE)):
        cut = pl.ds(t * 2 * TILE, 2 * TILE)
        done = jnp.dot(hidden[...], w_down[:, cut], preferred_element_type=jnp.float32)
        at = 0
        for out in outs:
            out[:, cut] = done[at : at + out.shape[0]].astype(jnp.bfloat16)
            at += out.shape[0]


def expert_forward(rows, weights, after=()):
    total = sum(r.shape[0] for r in rows)
    scratch = [pltpu.VMEM((total, FF), jnp.bfloat16)]
    outs = [bf16(*r.shape) for r in rows]
    flops = 6 * total * D * FF
    return call(expert_kernel, "expert", outs, (*rows, *weights), scratch, after, flops)


def combine_kernel(half, *refs):
    weights, rows, outs, gathered = refs[0], refs[1:9], refs[9:13], refs[13]
    for pair in range(2):
        for t in range(HALF // (2 * TILE)):
            cut = pl.ds(t * 2 * TILE, 2 * TILE)
            source = pl.ds(half * HALF + t * 2 * TILE, 2 * TILE)
            for i in range(len(TARGETS)):
                gathered[i * PAIR : (i + 1) * PAIR, :] = rows[i][
                    pair * PAIR : (pair + 1) * PAIR, source
                ]
            mixed = jnp.dot(weights[pair], gathered[...], preferred_element_type=jnp.float32)
            outs[2 * pair][:, cut] = mixed[0:TOK].astype(jnp.bfloat16)
            outs[2 * pair + 1][:, cut] = mixed[TOK : 2 * TOK].astype(jnp.bfloat16)


def combine(weights, rows, half, after=()):
    kernel = functools.partial(combine_kernel, half)
    scratch = [pltpu.VMEM((len(TARGETS) * PAIR, 2 * TILE), jnp.bfloat16)]
    return call(kernel, "combine", [bf16(TOK, HALF)] * 4, (weights, *rows), scratch, after)


def finish_kernel(half, own, *refs):
    blocks, out = refs[:4], refs[4]
    mixed = own[:, half * HALF : (half + 1) * HALF].astype(jnp.float32)
    for block in blocks:
        mixed = mixed + block[...].astype(jnp.float32)
    out[...] = mixed.astype(jnp.bfloat16)


def on_device(tokens_a, routes_a, gates_a, w_gate, w_up, w_down):
    own = tokens_a[0]
    expert = (w_gate[0, 0], w_up[0, 0], w_down[0, 0])
    ids = target_experts()

    def send(block, route):
        return lax.ppermute(block, "expert", route)

    packed = pl.pallas_call(
        pack_kernel,
        out_shape=bf16(TOK, D + TOK),
        in_specs=[ANY] * 3,
        out_specs=VMEM,
        scratch_shapes=[
            pltpu.VMEM((TOP, TOK), jnp.int32),
            pltpu.VMEM((TOP, TOK), jnp.float32),
            pltpu.SemaphoreType.DMA((3,)),
        ],
        compiler_params=pltpu.CompilerParams(vmem_limit_bytes=16 << 20),
        name="pack",
    )(own, routes_a[0].T, gates_a[0].T)
    tokens = [packed] + [send(packed, gather_route(d)) for d in STEPS]
    spread, slots = call(
        slots_kernel,
        "slots",
        [f32(4, len(TARGETS) * CAP, TOK), f32(4, 2 * EXPERTS, TOK)],
        (ids, *tokens),
    )

    def out(i, block):
        return send(block, slot_route(*TARGETS[i]))

    def home(i, block):
        return send(block, back(slot_route(*TARGETS[i])))

    results = [None] * len(TARGETS)
    near_rows = fill_slots(spread, tokens, 2, 4)
    near = [out(i + 2, block) for i, block in enumerate(near_rows)]
    far = fill_slots(spread, tokens, 6, 2, after=(near_rows[0],))
    far = [out(i + 6, block) for i, block in enumerate(far)]
    here = list(fill_slots(spread, tokens, 0, 2))
    here[1] = out(1, here[1])
    weights = call(weights_kernel, "weights", bf16(2, 2 * TOK, len(TARGETS) * PAIR), (ids, slots))
    after = ()
    for n, rows in ((2, near[0:2]), (4, near[2:4]), (6, far), (0, here)):
        done = expert_forward(rows, expert, after)
        results[n : n + 2] = [
            block if n + i == 0 else home(n + i, block) for i, block in enumerate(done)
        ]
    count = lax.axis_size("section")
    onward = [((i - 1) % count, i) for i in range(count)]
    moved, after = [], ()
    for half in range(2):
        partial = combine(weights, results, half, after)
        after = (partial[0],)
        arrived = [send(block, back(gather_route(d))) for d, block in zip(STEPS, partial[1:])]
        layer_a = call(
            functools.partial(finish_kernel, half),
            "finish",
            bf16(TOK, HALF),
            (packed, partial[0], *arrived),
        )
        moved.append(lax.ppermute(layer_a, "section", onward))
    return jnp.concatenate(moved, axis=1)[None]


def solution(mesh):
    in_specs = (
        P("section", "expert", None),
        P("section", "expert", None),
        P("section", "expert", None),
        P("section", "expert", None, None),
        P("section", "expert", None, None),
        P("section", "expert", None, None),
    )
    out_specs = P("section", "expert", None)
    return jax.shard_map(
        on_device, mesh=mesh, in_specs=in_specs, out_specs=out_specs, check_vma=False
    )
```

time: 132 us -> 115 us (0.87)
  starting transfers between devices: 52 us -> 33.1 us
  local copies, waits for them, and re-layouts: 0.1 us -> 2.51 us
  other arithmetic: 2.67 us -> 0.83 us
    ppermute x28 -> x25, starting transfers between devices: 52 us -> 33.1 us  [the longest x23 29.1 us: send(): return lax.ppermute(block, 'expert', route)]
    unnamed x8 -> x12, local copies, waits for them, and re-layouts: 0.02 us -> 2.43 us
    ppermute x28 -> x25, waiting for transfers between devices: 58.3 us -> 59.4 us  [the longest x23 51.2 us: send(): return lax.ppermute(block, 'expert', route)]
    pallas_call x9 -> x14, Pallas kernels: 17.5 us -> 18.6 us  [the longest x13 18.6 us: call(): pl.pallas_call(body, out_shape=out_shape, in_specs=[SMEM if a.dtype == jn...]
  transfers between devices with their start and end apart: 28 -> 25, of which waited for: 13 -> 14; matrix products, arithmetic and copies ran while one was open for 1% -> 0% of each run, Pallas kernels for 12% -> 13%
where the time goes in v2:
time: 115 us
  waiting for transfers between devices  59.4 us (52%)
  starting transfers between devices  33.1 us (29%)
  Pallas kernels  18.6 us (16%)
  local copies, waits for them, and re-layouts  2.51 us (2%)
    ppermute x23, waiting for transfers between devices, send(): return lax.ppermute(block, 'expert', route)  51.2 us
    ppermute x23, starting transfers between devices, send(): return lax.ppermute(block, 'expert', route)  29.1 us
    pallas_call x13, Pallas kernels, call(): pl.pallas_call(body, out_shape=out_shape, in_specs=[SMEM if a.dtype == jn...  18.6 us
    ppermute x2, waiting for transfers between devices, on_device(): moved.append(lax.ppermute(layer_a, 'section', onward))  8.29 us
    ppermute x2, starting transfers between devices, on_device(): moved.append(lax.ppermute(layer_a, 'section', onward))  4 us
    unnamed x12, local copies, waits for them, and re-layouts  2.43 us
  transfers between devices with their start and end apart: 25, of which 14 were waited for; matrix products, arithmetic and copies ran while one was open for 0% of the time, Pallas kernels for 13%

profile of v2, /device:TPU:8, one launch (start us, length us, event | category | flops | bytes accessed | tf_op | source)
XLA Modules:
  0.0 114.7 jit_solution(8564510904076280704)
XLA Ops:
  2.5 1.6 %collective-permute-start = (bf16[128,2176]{1,0:T(8,128)(2,1)S(1)}, bf16[128,2176]{1,0:T(8,128)(2,1)S(1)}, u32[]{:S(2)}, u32[]{:S(2)}) collective-permute-start(bf16[128,2176]{1,0:T(8,128)(2,1)S(1)} %pack.1.refs_1_.refs_0_), channel_id=1, source_target_pairs={{0,8},{1,3},{2,10},{3,5},{4,12},{5,7},{6,14},{7,1},{8,16},{9,11},{... | collective-permute-start | bytes 1671176 | tf_op jit(solution)/shard_map/ppermute | solution.py:233
  4.1 1.7 %collective-permute-start.1 = (bf16[128,2176]{1,0:T(8,128)(2,1)S(1)}, bf16[128,2176]{1,0:T(8,128)(2,1)S(1)}, u32[]{:S(2)}, u32[]{:S(2)}) collective-permute-start(bf16[128,2176]{1,0:T(8,128)(2,1)S(1)} %pack.1.refs_1_.refs_0_), channel_id=1, source_target_pairs={{0,24},{1,7},{2,26},{3,1},{4,28},{5,3},{6,30},{7,5},{8,0},{9,15},{... | collective-permute-start | bytes 1671176 | tf_op jit(solution)/shard_map/ppermute | solution.py:233
  5.8 1.8 %collective-permute-start.2 = (bf16[128,2176]{1,0:T(8,128)(2,1)S(1)}, bf16[128,2176]{1,0:T(8,128)(2,1)S(1)}, u32[]{:S(2)}, u32[]{:S(2)}) collective-permute-start(bf16[128,2176]{1,0:T(8,128)(2,1)S(1)} %pack.1.refs_1_.refs_0_), channel_id=1, source_target_pairs={{0,16},{1,5},{2,18},{3,7},{4,20},{5,1},{6,22},{7,3},{8,24},{9,13},... | collective-permute-start | bytes 1671176 | tf_op jit(solution)/shard_map/ppermute | solution.py:233
  7.7 5.6 %collective-permute-done.refs_2_ = bf16[128,2176]{1,0:T(8,128)(2,1)S(1)} collective-permute-done((bf16[128,2176]{1,0:T(8,128)(2,1)S(1)}, bf16[128,2176]{1,0:T(8,128)(2,1)S(1)}, u32[]{:S(2)}, u32[]{:S(2)}) %collective-permute-start) | collective-permute-done | bytes 557088 | tf_op jit(solution)/shard_map/ppermute | solution.py:233
  13.3 5.5 %collective-permute-done.1.refs_3_ = bf16[128,2176]{1,0:T(8,128)(2,1)S(1)} collective-permute-done((bf16[128,2176]{1,0:T(8,128)(2,1)S(1)}, bf16[128,2176]{1,0:T(8,128)(2,1)S(1)}, u32[]{:S(2)}, u32[]{:S(2)}) %collective-permute-start.1) | collective-permute-done | bytes 557088 | tf_op jit(solution)/shard_map/ppermute | solution.py:233
  18.9 1.4 %collective-permute-done.2.refs_4_ = bf16[128,2176]{1,0:T(8,128)(2,1)S(1)} collective-permute-done((bf16[128,2176]{1,0:T(8,128)(2,1)S(1)}, bf16[128,2176]{1,0:T(8,128)(2,1)S(1)}, u32[]{:S(2)}, u32[]{:S(2)}) %collective-permute-start.2) | collective-permute-done | bytes 557088 | tf_op jit(solution)/shard_map/ppermute | solution.py:233
  22.5 2.4 %collective-permute-start.13 = (bf16[160,2048]{1,0:T(8,128)(2,1)S(1)}, bf16[160,2048]{1,0:T(8,128)(2,1)S(1)}, u32[]{:S(2)}, u32[]{:S(2)}) collective-permute-start(bf16[160,2048]{1,0:T(8,128)(2,1)S(1)} %get-tuple-element.45), channel_id=1, source_target_pairs={{0,4},{1,17},{2,6},{3,19},{4,0},{5,21},{6,2},{7,23},{8,12},{9,25},... | collective-permute-start | bytes 1966088 | tf_op jit(solution)/shard_map/ppermute | solution.py:233
  25.1 1.7 %collective-permute-start.10 = (bf16[160,2048]{1,0:T(8,128)(2,1)S(1)}, bf16[160,2048]{1,0:T(8,128)(2,1)S(1)}, u32[]{:S(2)}, u32[]{:S(2)}) collective-permute-start(bf16[160,2048]{1,0:T(8,128)(2,1)S(1)} %get-tuple-element.42), channel_id=1, source_target_pairs={{0,7},{1,24},{2,1},{3,26},{4,3},{5,28},{6,5},{7,30},{8,15},{9,0},{... | collective-permute-start | bytes 1966088 | tf_op jit(solution)/shard_map/ppermute | solution.py:233
  28.8 6.0 %collective-permute-done.13.refs_0_ = bf16[160,2048]{1,0:T(8,128)(2,1)S(1)} collective-permute-done((bf16[160,2048]{1,0:T(8,128)(2,1)S(1)}, bf16[160,2048]{1,0:T(8,128)(2,1)S(1)}, u32[]{:S(2)}, u32[]{:S(2)}) %collective-permute-start.13) | collective-permute-done | bytes 655392 | tf_op jit(solution)/shard_map/ppermute | solution.py:233
  35.2 4.8 %collective-permute-done.14.refs_1_ = bf16[160,2048]{1,0:T(8,128)(2,1)S(1)} collective-permute-done((bf16[160,2048]{1,0:T(8,128)(2,1)S(1)}, bf16[160,2048]{1,0:T(8,128)(2,1)S(1)}, u32[]{:S(2)}, u32[]{:S(2)}) %collective-permute-start.14) | collective-permute-done | bytes 655392 | tf_op jit(solution)/shard_map/ppermute | solution.py:233
  40.0 1.6 %collective-permute-start.3 = (bf16[160,2048]{1,0:T(8,128)(2,1)S(1)}, bf16[160,2048]{1,0:T(8,128)(2,1)S(1)}, u32[]{:S(2)}, u32[]{:S(2)}) collective-permute-start(bf16[160,2048]{1,0:T(8,128)(2,1)S(1)} %get-tuple-element.34), channel_id=1, source_target_pairs={{0,1},{1,0},{2,3},{3,2},{4,5},{5,4},{6,7},{7,6},{8,9},{9,8},{10,11... | collective-permute-start | bytes 1966088 | tf_op jit(solution)/shard_map/ppermute | solution.py:233
  41.6 3.2 %expert.7 = (bf16[160,2048]{1,0:T(8,128)(2,1)S(1)}, bf16[160,2048]{1,0:T(8,128)(2,1)S(1)}) custom-call(bf16[160,2048]{1,0:T(8,128)(2,1)S(1)} %collective-permute-done.13.refs_0_, bf16[160,2048]{1,0:T(8,128)(2,1)S(1)} %collective-permute-done.14.refs_1_, bf16[2048,768]{1,0:T(8,128)(2,1)S(1)} %bitcast.23, bf16[2048,768]{1,0:T(8,128)(2,1)S(1)} %bitcast.27, ...), custom_call_target="tpu_custom_call" | custom-call | flops 3019898880 | tf_op jit(solution)/shard_map/expert/pallas_call | solution.py:72
  44.8 2.2 %collective-permute-done.10.refs_1_ = bf16[160,2048]{1,0:T(8,128)(2,1)S(1)} collective-permute-done((bf16[160,2048]{1,0:T(8,128)(2,1)S(1)}, bf16[160,2048]{1,0:T(8,128)(2,1)S(1)}, u32[]{:S(2)}, u32[]{:S(2)}) %collective-permute-start.10) | collective-permute-done | bytes 655392 | tf_op jit(solution)/shard_map/ppermute | solution.py:233
  47.0 1.2 %collective-permute-start.15 = (bf16[160,2048]{1,0:T(8,128)(2,1)S(1)}, bf16[160,2048]{1,0:T(8,128)(2,1)S(1)}, u32[]{:S(2)}, u32[]{:S(2)}) collective-permute-start(bf16[160,2048]{1,0:T(8,128)(2,1)S(1)} %get-tuple-element.47), channel_id=1, source_target_pairs={{4,0},{17,1},{6,2},{19,3},{0,4},{21,5},{2,6},{23,7},{12,8},{25,9},... | collective-permute-start | bytes 1966088 | tf_op jit(solution)/shard_map/ppermute | solution.py:233
  48.3 7.4 %collective-permute-done.9.refs_0_ = bf16[160,2048]{1,0:T(8,128)(2,1)S(1)} collective-permute-done((bf16[160,2048]{1,0:T(8,128)(2,1)S(1)}, bf16[160,2048]{1,0:T(8,128)(2,1)S(1)}, u32[]{:S(2)}, u32[]{:S(2)}) %collective-permute-start.9) | collective-permute-done | bytes 655392 | tf_op jit(solution)/shard_map/ppermute | solution.py:233
  55.7 3.2 %expert.6 = (bf16[160,2048]{1,0:T(8,128)(2,1)S(1)}, bf16[160,2048]{1,0:T(8,128)(2,1)S(1)}) custom-call(bf16[160,2048]{1,0:T(8,128)(2,1)S(1)} %collective-permute-done.9.refs_0_, bf16[160,2048]{1,0:T(8,128)(2,1)S(1)} %collective-permute-done.10.refs_1_, bf16[2048,768]{1,0:T(8,128)(2,1)S(1)} %bitcast.24, bf16[2048,768]{1,0:T(8,128)(2,1)S(1)} %bitcast.28, ...), custom_call_target="tpu_custom_call" | custom-call | flops 3019898880 | tf_op jit(solution)/shard_map/expert/pallas_call | solution.py:72
  59.6 2.9 %collective-permute-start.12 = (bf16[160,2048]{1,0:T(8,128)(2,1)S(1)}, bf16[160,2048]{1,0:T(8,128)(2,1)S(1)}, u32[]{:S(2)}, u32[]{:S(2)}) collective-permute-start(bf16[160,2048]{1,0:T(8,128)(2,1)S(1)} %get-tuple-element.44), channel_id=1, source_target_pairs={{7,0},{24,1},{1,2},{26,3},{3,4},{28,5},{5,6},{30,7},{15,8},{0,9},{... | collective-permute-start | bytes 1966088 | tf_op jit(solution)/shard_map/ppermute | solution.py:233
  62.5 3.2 %expert.5 = (bf16[160,2048]{1,0:T(8,128)(2,1)S(1)}, bf16[160,2048]{1,0:T(8,128)(2,1)S(1)}) custom-call(bf16[160,2048]{1,0:T(8,128)(2,1)S(1)} %collective-permute-done.5.refs_0_, bf16[160,2048]{1,0:T(8,128)(2,1)S(1)} %collective-permute-done.6.refs_1_, bf16[2048,768]{1,0:T(8,128)(2,1)S(1)} %bitcast.25, bf16[2048,768]{1,0:T(8,128)(2,1)S(1)} %bitcast.29, ...), custom_call_target="tpu_custom_call" | custom-call | flops 3019898880 | tf_op jit(solution)/shard_map/expert/pallas_call | solution.py:72
  66.2 3.2 %expert.4 = (bf16[160,2048]{1,0:T(8,128)(2,1)S(1)}, bf16[160,2048]{1,0:T(8,128)(2,1)S(1)}) custom-call(bf16[160,2048]{1,0:T(8,128)(2,1)S(1)} %get-tuple-element.33.refs_0_, bf16[160,2048]{1,0:T(8,128)(2,1)S(1)} %collective-permute-done.3.refs_1_, bf16[2048,768]{1,0:T(8,128)(2,1)S(1)} %bitcast.26, bf16[2048,768]{1,0:T(8,128)(2,1)S(1)} %bitcast.30, ...), custom_call_target="tpu_custom_call" | custom-call | flops 3019898880 | tf_op jit(solution)/shard_map/expert/pallas_call | solution.py:72
  69.5 1.9 %collective-permute-start.8 = (bf16[160,2048]{1,0:T(8,128)(2,1)S(1)}, bf16[160,2048]{1,0:T(8,128)(2,1)S(1)}, u32[]{:S(2)}, u32[]{:S(2)}) collective-permute-start(bf16[160,2048]{1,0:T(8,128)(2,1)S(1)} %get-tuple-element.40), channel_id=1, source_target_pairs={{3,0},{8,1},{5,2},{10,3},{7,4},{12,5},{1,6},{14,7},{11,8},{16,9},{... | collective-permute-start | bytes 1966088 | tf_op jit(solution)/shard_map/ppermute | solution.py:233
  72.5 10.3 %collective-permute-done.11.refs_5_ = bf16[160,2048]{1,0:T(8,128)(2,1)S(1)} collective-permute-done((bf16[160,2048]{1,0:T(8,128)(2,1)S(1)}, bf16[160,2048]{1,0:T(8,128)(2,1)S(1)}, u32[]{:S(2)}, u32[]{:S(2)}) %collective-permute-start.11) | collective-permute-done | bytes 655392 | tf_op jit(solution)/shard_map/ppermute | solution.py:233
  82.8 1.2 %collective-permute-done.12.refs_6_ = bf16[160,2048]{1,0:T(8,128)(2,1)S(1)} collective-permute-done((bf16[160,2048]{1,0:T(8,128)(2,1)S(1)}, bf16[160,2048]{1,0:T(8,128)(2,1)S(1)}, u32[]{:S(2)}, u32[]{:S(2)}) %collective-permute-start.12) | collective-permute-done | bytes 655392 | tf_op jit(solution)/shard_map/ppermute | solution.py:233
  85.1 2.3 %collective-permute-start.17 = (bf16[128,1024]{1,0:T(8,128)(2,1)S(1)}, bf16[128,1024]{1,0:T(8,128)(2,1)S(1)}, u32[]{:S(2)}, u32[]{:S(2)}) collective-permute-start(bf16[128,1024]{1,0:T(8,128)(2,1)S(1)} %get-tuple-element.50), channel_id=1, source_target_pairs={{8,0},{3,1},{10,2},{5,3},{12,4},{7,5},{14,6},{1,7},{16,8},{11,9},{... | collective-permute-start | bytes 786440 | tf_op jit(solution)/shard_map/ppermute | solution.py:233
  87.4 2.1 %collective-permute-start.19 = (bf16[128,1024]{1,0:T(8,128)(2,1)S(1)}, bf16[128,1024]{1,0:T(8,128)(2,1)S(1)}, u32[]{:S(2)}, u32[]{:S(2)}) collective-permute-start(bf16[128,1024]{1,0:T(8,128)(2,1)S(1)} %get-tuple-element.52), channel_id=1, source_target_pairs={{16,0},{5,1},{18,2},{7,3},{20,4},{1,5},{22,6},{3,7},{24,8},{13,9},... | collective-permute-start | bytes 786440 | tf_op jit(solution)/shard_map/ppermute | solution.py:233
  90.4 1.9 %collective-permute-start.21 = (bf16[128,1024]{1,0:T(8,128)(2,1)S(1)}, bf16[128,1024]{1,0:T(8,128)(2,1)S(1)}, u32[]{:S(2)}, u32[]{:S(2)}) collective-permute-start(bf16[128,1024]{1,0:T(8,128)(2,1)S(1)} %get-tuple-element.54), channel_id=1, source_target_pairs={{8,0},{3,1},{10,2},{5,3},{12,4},{7,5},{14,6},{1,7},{16,8},{11,9},{... | collective-permute-start | bytes 786440 | tf_op jit(solution)/shard_map/ppermute | solution.py:233
  92.6 2.0 %collective-permute-start.23 = (bf16[128,1024]{1,0:T(8,128)(2,1)S(1)}, bf16[128,1024]{1,0:T(8,128)(2,1)S(1)}, u32[]{:S(2)}, u32[]{:S(2)}) collective-permute-start(bf16[128,1024]{1,0:T(8,128)(2,1)S(1)} %get-tuple-element.56), channel_id=1, source_target_pairs={{16,0},{5,1},{18,2},{7,3},{20,4},{1,5},{22,6},{3,7},{24,8},{13,9},... | collective-permute-start | bytes 786440 | tf_op jit(solution)/shard_map/ppermute | solution.py:233
  94.6 3.2 %collective-permute-done.18.refs_3_ = bf16[128,1024]{1,0:T(8,128)(2,1)S(1)} collective-permute-done((bf16[128,1024]{1,0:T(8,128)(2,1)S(1)}, bf16[128,1024]{1,0:T(8,128)(2,1)S(1)}, u32[]{:S(2)}, u32[]{:S(2)}) %collective-permute-start.18) | collective-permute-done | bytes 262176 | tf_op jit(solution)/shard_map/ppermute | solution.py:233
  98.0 2.0 %collective-permute-start.20 = (bf16[128,1024]{1,0:T(8,128)(2,1)S(1)}, bf16[128,1024]{1,0:T(8,128)(2,1)S(1)}, u32[]{:S(2)}, u32[]{:S(2)}) collective-permute-start(bf16[128,1024]{1,0:T(8,128)(2,1)S(1)} %finish.2), channel_id=1, source_target_pairs={{224,0},{0,32},{32,64},{64,96},{96,128},{128,160},{160,192},{192,2... | collective-permute-start | bytes 786440 | tf_op jit(solution)/shard_map/ppermute | solution.py:289
  100.0 3.4 %collective-permute-done.22.refs_3_ = bf16[128,1024]{1,0:T(8,128)(2,1)S(1)} collective-permute-done((bf16[128,1024]{1,0:T(8,128)(2,1)S(1)}, bf16[128,1024]{1,0:T(8,128)(2,1)S(1)}, u32[]{:S(2)}, u32[]{:S(2)}) %collective-permute-start.22) | collective-permute-done | bytes 262176 | tf_op jit(solution)/shard_map/ppermute | solution.py:233
  103.6 2.0 %collective-permute-start.24 = (bf16[128,1024]{1,0:T(8,128)(2,1)S(1)}, bf16[128,1024]{1,0:T(8,128)(2,1)S(1)}, u32[]{:S(2)}, u32[]{:S(2)}) collective-permute-start(bf16[128,1024]{1,0:T(8,128)(2,1)S(1)} %finish.3), channel_id=1, source_target_pairs={{224,0},{0,32},{32,64},{64,96},{96,128},{128,160},{160,192},{192,2... | collective-permute-start | bytes 786440 | tf_op jit(solution)/shard_map/ppermute | solution.py:289
  105.6 5.3 %collective-permute-done.20 = bf16[128,1024]{1,0:T(8,128)(2,1)S(1)} collective-permute-done((bf16[128,1024]{1,0:T(8,128)(2,1)S(1)}, bf16[128,1024]{1,0:T(8,128)(2,1)S(1)}, u32[]{:S(2)}, u32[]{:S(2)}) %collective-permute-start.20) | collective-permute-done | bytes 262176 | tf_op jit(solution)/shard_map/ppermute | solution.py:289
  110.9 3.0 %collective-permute-done.24 = bf16[128,1024]{1,0:T(8,128)(2,1)S(1)} collective-permute-done((bf16[128,1024]{1,0:T(8,128)(2,1)S(1)}, bf16[128,1024]{1,0:T(8,128)(2,1)S(1)}, u32[]{:S(2)}, u32[]{:S(2)}) %collective-permute-start.24) | collective-permute-done | bytes 262176 | tf_op jit(solution)/shard_map/ppermute | solution.py:289
  (46 shorter events, 13.3 us)
Async XLA Ops:
  0.0 1.0 copy-start
  1.0 0.7 copy-start.1
  1.7 0.7 copy-start.2
  2.5 10.8 %collective-permute-start = (bf16[128,2176]{1,0:T(8,128)(2,1)S(1)}, bf16[128,2176]{1,0:T(8,128)(2,1)S(1)}, u32[]{:S(2)}, u32[]{:S(2)}) collective-permute-start(bf16[128,2176]{1,0:T(8,128)(2,1)S(1)} %pack.1.refs_1_.refs_0_), channel_id=1, source_target_pairs={{0,8},{1,3},{2,10},{3,5},{4,12},{5,7},{6,14},{7,1},{8,16},{9,11},{... | collective-permute-start | bytes 1671176 | tf_op jit(solution)/shard_map/ppermute | solution.py:233
  4.1 14.8 %collective-permute-start.1 = (bf16[128,2176]{1,0:T(8,128)(2,1)S(1)}, bf16[128,2176]{1,0:T(8,128)(2,1)S(1)}, u32[]{:S(2)}, u32[]{:S(2)}) collective-permute-start(bf16[128,2176]{1,0:T(8,128)(2,1)S(1)} %pack.1.refs_1_.refs_0_), channel_id=1, source_target_pairs={{0,24},{1,7},{2,26},{3,1},{4,28},{5,3},{6,30},{7,5},{8,0},{9,15},{... | collective-permute-start | bytes 1671176 | tf_op jit(solution)/shard_map/ppermute | solution.py:233
  5.8 14.5 %collective-permute-start.2 = (bf16[128,2176]{1,0:T(8,128)(2,1)S(1)}, bf16[128,2176]{1,0:T(8,128)(2,1)S(1)}, u32[]{:S(2)}, u32[]{:S(2)}) collective-permute-start(bf16[128,2176]{1,0:T(8,128)(2,1)S(1)} %pack.1.refs_1_.refs_0_), channel_id=1, source_target_pairs={{0,16},{1,5},{2,18},{3,7},{4,20},{5,1},{6,22},{7,3},{8,24},{9,13},... | collective-permute-start | bytes 1671176 | tf_op jit(solution)/shard_map/ppermute | solution.py:233
  20.3 21.3 %copy-start.5 = (bf16[1,1,768,2048]{3,2,1,0:T(8,128)(2,1)S(1)}, bf16[1,1,768,2048]{3,2,1,0:T(8,128)(2,1)}, u32[]{:S(2)}) copy-start(bf16[1,1,768,2048]{3,2,1,0:T(8,128)(2,1)} %param.11) | copy-start | bytes 9437188
  21.9 19.7 %copy-start.3 = (bf16[1,1,2048,768]{3,2,1,0:T(8,128)(2,1)S(1)}, bf16[1,1,2048,768]{3,2,1,0:T(8,128)(2,1)}, u32[]{:S(2)}) copy-start(bf16[1,1,2048,768]{3,2,1,0:T(8,128)(2,1)} %param.9) | copy-start | bytes 9437188
  21.9 19.7 %copy-start.4 = (bf16[1,1,2048,768]{3,2,1,0:T(8,128)(2,1)S(1)}, bf16[1,1,2048,768]{3,2,1,0:T(8,128)(2,1)}, u32[]{:S(2)}) copy-start(bf16[1,1,2048,768]{3,2,1,0:T(8,128)(2,1)} %param.10) | copy-start | bytes 9437188
  22.5 12.3 %collective-permute-start.13 = (bf16[160,2048]{1,0:T(8,128)(2,1)S(1)}, bf16[160,2048]{1,0:T(8,128)(2,1)S(1)}, u32[]{:S(2)}, u32[]{:S(2)}) collective-permute-start(bf16[160,2048]{1,0:T(8,128)(2,1)S(1)} %get-tuple-element.45), channel_id=1, source_target_pairs={{0,4},{1,17},{2,6},{3,19},{4,0},{5,21},{6,2},{7,23},{8,12},{9,25},... | collective-permute-start | bytes 1966088 | tf_op jit(solution)/shard_map/ppermute | solution.py:233
  24.8 15.2 %collective-permute-start.14 = (bf16[160,2048]{1,0:T(8,128)(2,1)S(1)}, bf16[160,2048]{1,0:T(8,128)(2,1)S(1)}, u32[]{:S(2)}, u32[]{:S(2)}) collective-permute-start(bf16[160,2048]{1,0:T(8,128)(2,1)S(1)} %get-tuple-element.46), channel_id=1, source_target_pairs={{0,5},{1,16},{2,7},{3,18},{4,1},{5,20},{6,3},{7,22},{8,13},{9,24},... | collective-permute-start | bytes 1966088 | tf_op jit(solution)/shard_map/ppermute | solution.py:233
  25.1 21.9 %collective-permute-start.10 = (bf16[160,2048]{1,0:T(8,128)(2,1)S(1)}, bf16[160,2048]{1,0:T(8,128)(2,1)S(1)}, u32[]{:S(2)}, u32[]{:S(2)}) collective-permute-start(bf16[160,2048]{1,0:T(8,128)(2,1)S(1)} %get-tuple-element.42), channel_id=1, source_target_pairs={{0,7},{1,24},{2,1},{3,26},{4,3},{5,28},{6,5},{7,30},{8,15},{9,0},{... | collective-permute-start | bytes 1966088 | tf_op jit(solution)/shard_map/ppermute | solution.py:233
  26.7 29.0 %collective-permute-start.9 = (bf16[160,2048]{1,0:T(8,128)(2,1)S(1)}, bf16[160,2048]{1,0:T(8,128)(2,1)S(1)}, u32[]{:S(2)}, u32[]{:S(2)}) collective-permute-start(bf16[160,2048]{1,0:T(8,128)(2,1)S(1)} %get-tuple-element.41), channel_id=1, source_target_pairs={{0,6},{1,25},{2,0},{3,27},{4,2},{5,29},{6,4},{7,31},{8,14},{9,1},{... | collective-permute-start | bytes 1966088 | tf_op jit(solution)/shard_map/ppermute | solution.py:233
  27.8 31.1 %collective-permute-start.5 = (bf16[160,2048]{1,0:T(8,128)(2,1)S(1)}, bf16[160,2048]{1,0:T(8,128)(2,1)S(1)}, u32[]{:S(2)}, u32[]{:S(2)}) collective-permute-start(bf16[160,2048]{1,0:T(8,128)(2,1)S(1)} %get-tuple-element.37.refs_5_), channel_id=1, source_target_pairs={{0,2},{1,9},{2,4},{3,11},{4,6},{5,13},{6,0},{7,15},{8,10},{9,17},{... | collective-permute-start | bytes 1966088 | tf_op jit(solution)/shard_map/ppermute | solution.py:233
  34.7 24.9 %collective-permute-start.6 = (bf16[160,2048]{1,0:T(8,128)(2,1)S(1)}, bf16[160,2048]{1,0:T(8,128)(2,1)S(1)}, u32[]{:S(2)}, u32[]{:S(2)}) collective-permute-start(bf16[160,2048]{1,0:T(8,128)(2,1)S(1)} %get-tuple-element.38), channel_id=1, source_target_pairs={{0,3},{1,8},{2,5},{3,10},{4,7},{5,12},{6,1},{7,14},{8,11},{9,16},{... | collective-permute-start | bytes 1966088 | tf_op jit(solution)/shard_map/ppermute | solution.py:233
  40.0 25.8 %collective-permute-start.3 = (bf16[160,2048]{1,0:T(8,128)(2,1)S(1)}, bf16[160,2048]{1,0:T(8,128)(2,1)S(1)}, u32[]{:S(2)}, u32[]{:S(2)}) collective-permute-start(bf16[160,2048]{1,0:T(8,128)(2,1)S(1)} %get-tuple-element.34), channel_id=1, source_target_pairs={{0,1},{1,0},{2,3},{3,2},{4,5},{5,4},{6,7},{7,6},{8,9},{9,8},{10,11... | collective-permute-start | bytes 1966088 | tf_op jit(solution)/shard_map/ppermute | solution.py:233
  47.0 22.4 %collective-permute-start.15 = (bf16[160,2048]{1,0:T(8,128)(2,1)S(1)}, bf16[160,2048]{1,0:T(8,128)(2,1)S(1)}, u32[]{:S(2)}, u32[]{:S(2)}) collective-permute-start(bf16[160,2048]{1,0:T(8,128)(2,1)S(1)} %get-tuple-element.47), channel_id=1, source_target_pairs={{4,0},{17,1},{6,2},{19,3},{0,4},{21,5},{2,6},{23,7},{12,8},{25,9},... | collective-permute-start | bytes 1966088 | tf_op jit(solution)/shard_map/ppermute | solution.py:233
  55.7 15.7 %collective-permute-start.16 = (bf16[160,2048]{1,0:T(8,128)(2,1)S(1)}, bf16[160,2048]{1,0:T(8,128)(2,1)S(1)}, u32[]{:S(2)}, u32[]{:S(2)}) collective-permute-start(bf16[160,2048]{1,0:T(8,128)(2,1)S(1)} %get-tuple-element.48), channel_id=1, source_target_pairs={{5,0},{16,1},{7,2},{18,3},{1,4},{20,5},{3,6},{22,7},{13,8},{24,9},... | collective-permute-start | bytes 1966088 | tf_op jit(solution)/shard_map/ppermute | solution.py:233
  58.9 23.9 %collective-permute-start.11 = (bf16[160,2048]{1,0:T(8,128)(2,1)S(1)}, bf16[160,2048]{1,0:T(8,128)(2,1)S(1)}, u32[]{:S(2)}, u32[]{:S(2)}) collective-permute-start(bf16[160,2048]{1,0:T(8,128)(2,1)S(1)} %get-tuple-element.43), channel_id=1, source_target_pairs={{6,0},{25,1},{0,2},{27,3},{2,4},{29,5},{4,6},{31,7},{14,8},{1,9},{... | collective-permute-start | bytes 1966088 | tf_op jit(solution)/shard_map/ppermute | solution.py:233
  59.6 24.4 %collective-permute-start.12 = (bf16[160,2048]{1,0:T(8,128)(2,1)S(1)}, bf16[160,2048]{1,0:T(8,128)(2,1)S(1)}, u32[]{:S(2)}, u32[]{:S(2)}) collective-permute-start(bf16[160,2048]{1,0:T(8,128)(2,1)S(1)} %get-tuple-element.44), channel_id=1, source_target_pairs={{7,0},{24,1},{1,2},{26,3},{3,4},{28,5},{5,6},{30,7},{15,8},{0,9},{... | collective-permute-start | bytes 1966088 | tf_op jit(solution)/shard_map/ppermute | solution.py:233
  65.8 18.2 %collective-permute-start.7 = (bf16[160,2048]{1,0:T(8,128)(2,1)S(1)}, bf16[160,2048]{1,0:T(8,128)(2,1)S(1)}, u32[]{:S(2)}, u32[]{:S(2)}) collective-permute-start(bf16[160,2048]{1,0:T(8,128)(2,1)S(1)} %get-tuple-element.39), channel_id=1, source_target_pairs={{2,0},{9,1},{4,2},{11,3},{6,4},{13,5},{0,6},{15,7},{10,8},{17,9},{... | collective-permute-start | bytes 1966088 | tf_op jit(solution)/shard_map/ppermute | solution.py:233
  69.5 14.6 %collective-permute-start.8 = (bf16[160,2048]{1,0:T(8,128)(2,1)S(1)}, bf16[160,2048]{1,0:T(8,128)(2,1)S(1)}, u32[]{:S(2)}, u32[]{:S(2)}) collective-permute-start(bf16[160,2048]{1,0:T(8,128)(2,1)S(1)} %get-tuple-element.40), channel_id=1, source_target_pairs={{3,0},{8,1},{5,2},{10,3},{7,4},{12,5},{1,6},{14,7},{11,8},{16,9},{... | collective-permute-start | bytes 1966088 | tf_op jit(solution)/shard_map/ppermute | solution.py:233
  71.4 12.7 %collective-permute-start.4 = (bf16[160,2048]{1,0:T(8,128)(2,1)S(1)}, bf16[160,2048]{1,0:T(8,128)(2,1)S(1)}, u32[]{:S(2)}, u32[]{:S(2)}) collective-permute-start(bf16[160,2048]{1,0:T(8,128)(2,1)S(1)} %get-tuple-element.36), channel_id=1, source_target_pairs={{1,0},{0,1},{3,2},{2,3},{5,4},{4,5},{7,6},{6,7},{9,8},{8,9},{11,10... | collective-permute-start | bytes 1966088 | tf_op jit(solution)/shard_map/ppermute | solution.py:233
  85.1 7.6 %collective-permute-start.17 = (bf16[128,1024]{1,0:T(8,128)(2,1)S(1)}, bf16[128,1024]{1,0:T(8,128)(2,1)S(1)}, u32[]{:S(2)}, u32[]{:S(2)}) collective-permute-start(bf16[128,1024]{1,0:T(8,128)(2,1)S(1)} %get-tuple-element.50), channel_id=1, source_target_pairs={{8,0},{3,1},{10,2},{5,3},{12,4},{7,5},{14,6},{1,7},{16,8},{11,9},{... | collective-permute-start | bytes 786440 | tf_op jit(solution)/shard_map/ppermute | solution.py:233
  87.4 10.4 %collective-permute-start.18 = (bf16[128,1024]{1,0:T(8,128)(2,1)S(1)}, bf16[128,1024]{1,0:T(8,128)(2,1)S(1)}, u32[]{:S(2)}, u32[]{:S(2)}) collective-permute-start(bf16[128,1024]{1,0:T(8,128)(2,1)S(1)} %get-tuple-element.51), channel_id=1, source_target_pairs={{24,0},{7,1},{26,2},{1,3},{28,4},{3,5},{30,6},{5,7},{0,8},{15,9},{... | collective-permute-start | bytes 786440 | tf_op jit(solution)/shard_map/ppermute | solution.py:233
  87.4 10.4 %collective-permute-start.19 = (bf16[128,1024]{1,0:T(8,128)(2,1)S(1)}, bf16[128,1024]{1,0:T(8,128)(2,1)S(1)}, u32[]{:S(2)}, u32[]{:S(2)}) collective-permute-start(bf16[128,1024]{1,0:T(8,128)(2,1)S(1)} %get-tuple-element.52), channel_id=1, source_target_pairs={{16,0},{5,1},{18,2},{7,3},{20,4},{1,5},{22,6},{3,7},{24,8},{13,9},... | collective-permute-start | bytes 786440 | tf_op jit(solution)/shard_map/ppermute | solution.py:233
  90.4 9.5 %collective-permute-start.21 = (bf16[128,1024]{1,0:T(8,128)(2,1)S(1)}, bf16[128,1024]{1,0:T(8,128)(2,1)S(1)}, u32[]{:S(2)}, u32[]{:S(2)}) collective-permute-start(bf16[128,1024]{1,0:T(8,128)(2,1)S(1)} %get-tuple-element.54), channel_id=1, source_target_pairs={{8,0},{3,1},{10,2},{5,3},{12,4},{7,5},{14,6},{1,7},{16,8},{11,9},{... | collective-permute-start | bytes 786440 | tf_op jit(solution)/shard_map/ppermute | solution.py:233
  92.3 11.1 %collective-permute-start.22 = (bf16[128,1024]{1,0:T(8,128)(2,1)S(1)}, bf16[128,1024]{1,0:T(8,128)(2,1)S(1)}, u32[]{:S(2)}, u32[]{:S(2)}) collective-permute-start(bf16[128,1024]{1,0:T(8,128)(2,1)S(1)} %get-tuple-element.55), channel_id=1, source_target_pairs={{24,0},{7,1},{26,2},{1,3},{28,4},{3,5},{30,6},{5,7},{0,8},{15,9},{... | collective-permute-start | bytes 786440 | tf_op jit(solution)/shard_map/ppermute | solution.py:233
  92.6 10.8 %collective-permute-start.23 = (bf16[128,1024]{1,0:T(8,128)(2,1)S(1)}, bf16[128,1024]{1,0:T(8,128)(2,1)S(1)}, u32[]{:S(2)}, u32[]{:S(2)}) collective-permute-start(bf16[128,1024]{1,0:T(8,128)(2,1)S(1)} %get-tuple-element.56), channel_id=1, source_target_pairs={{16,0},{5,1},{18,2},{7,3},{20,4},{1,5},{22,6},{3,7},{24,8},{13,9},... | collective-permute-start | bytes 786440 | tf_op jit(solution)/shard_map/ppermute | solution.py:233
  98.0 12.9 %collective-permute-start.20 = (bf16[128,1024]{1,0:T(8,128)(2,1)S(1)}, bf16[128,1024]{1,0:T(8,128)(2,1)S(1)}, u32[]{:S(2)}, u32[]{:S(2)}) collective-permute-start(bf16[128,1024]{1,0:T(8,128)(2,1)S(1)} %finish.2), channel_id=1, source_target_pairs={{224,0},{0,32},{32,64},{64,96},{96,128},{128,160},{160,192},{192,2... | collective-permute-start | bytes 786440 | tf_op jit(solution)/shard_map/ppermute | solution.py:289
  103.6 10.3 %collective-permute-start.24 = (bf16[128,1024]{1,0:T(8,128)(2,1)S(1)}, bf16[128,1024]{1,0:T(8,128)(2,1)S(1)}, u32[]{:S(2)}, u32[]{:S(2)}) collective-permute-start(bf16[128,1024]{1,0:T(8,128)(2,1)S(1)} %finish.3), channel_id=1, source_target_pairs={{224,0},{0,32},{32,64},{64,96},{96,128},{128,160},{160,192},{192,2... | collective-permute-start | bytes 786440 | tf_op jit(solution)/shard_map/ppermute | solution.py:289

commit v3 on v2

--- a/solution.py
+++ b/solution.py
@@ -14,7 +14,7 @@
 TOP = 8
 D = 2048
 FF = 768
-HALF = 1024
+PARTS = (0, 1024, D)
 TILE = 256
 PAIR = 2 * CAP
 STEPS = (1, 3, 2)
@@ -22,6 +22,7 @@
 VMEM = pl.BlockSpec(memory_space=pltpu.VMEM)
 SMEM = pl.BlockSpec(memory_space=pltpu.SMEM)
 ANY = pl.BlockSpec(memory_space=pl.ANY)
+HBM = pl.BlockSpec(memory_space=pltpu.HBM)
 
 
 def place(x, y, core):
@@ -170,8 +171,7 @@
 
 
 def expert_kernel(*refs):
-    n = (len(refs) - 4) // 2
-    rows, (w_gate, w_up, w_down), outs, hidden = refs[:n], refs[n : n + 3], refs[n + 3 : -1], refs[-1]
+    rows, (w_gate, w_up, w_down), outs, hidden = refs[:2], refs[2:5], refs[5:7], refs[7]
     for f in range(FF // TILE):
         cut = pl.ds(f * TILE, TILE)
         block = jnp.concatenate([r[...] for r in rows], axis=0)
@@ -181,44 +181,45 @@
     for t in range(D // (2 * TILE)):
         cut = pl.ds(t * 2 * TILE, 2 * TILE)
         done = jnp.dot(hidden[...], w_down[:, cut], preferred_element_type=jnp.float32)
-        at = 0
-        for out in outs:
-            out[:, cut] = done[at : at + out.shape[0]].astype(jnp.bfloat16)
-            at += out.shape[0]
+        for i in range(2):
+            outs[i][:, cut] = done[i * 2 * PAIR : (i + 1) * 2 * PAIR].astype(jnp.bfloat16)
 
 
 def expert_forward(rows, weights, after=()):
-    total = sum(r.shape[0] for r in rows)
-    scratch = [pltpu.VMEM((total, FF), jnp.bfloat16)]
-    outs = [bf16(*r.shape) for r in rows]
-    flops = 6 * total * D * FF
+    scratch = [pltpu.VMEM((4 * PAIR, FF), jnp.bfloat16)]
+    outs = [bf16(2 * PAIR, D)] * 2
+    flops = 24 * PAIR * D * FF
     return call(expert_kernel, "expert", outs, (*rows, *weights), scratch, after, flops)
 
 
-def combine_kernel(half, *refs):
+def combine_kernel(part, *refs):
     weights, rows, outs, gathered = refs[0], refs[1:9], refs[9:13], refs[13]
+    first, last = PARTS[part], PARTS[part + 1]
     for pair in range(2):
-        for t in range(HALF // (2 * TILE)):
-            cut = pl.ds(t * 2 * TILE, 2 * TILE)
-            source = pl.ds(half * HALF + t * 2 * TILE, 2 * TILE)
+        for at in range(first, last, 2 * TILE):
+            width = min(2 * TILE, last - at)
             for i in range(len(TARGETS)):
-                gathered[i * PAIR : (i + 1) * PAIR, :] = rows[i][
-                    pair * PAIR : (pair + 1) * PAIR, source
+                gathered[i * PAIR : (i + 1) * PAIR, 0:width] = rows[i][
+                    pair * PAIR : (pair + 1) * PAIR, pl.ds(at, width)
                 ]
-            mixed = jnp.dot(weights[pair], gathered[...], preferred_element_type=jnp.float32)
+            mixed = jnp.dot(
+                weights[pair], gathered[:, 0:width], preferred_element_type=jnp.float32
+            )
+            cut = pl.ds(at - first, width)
             outs[2 * pair][:, cut] = mixed[0:TOK].astype(jnp.bfloat16)
             outs[2 * pair + 1][:, cut] = mixed[TOK : 2 * TOK].astype(jnp.bfloat16)
 
 
-def combine(weights, rows, half, after=()):
-    kernel = functools.partial(combine_kernel, half)
+def combine(weights, rows, part, after=()):
+    kernel = functools.partial(combine_kernel, part)
     scratch = [pltpu.VMEM((len(TARGETS) * PAIR, 2 * TILE), jnp.bfloat16)]
-    return call(kernel, "combine", [bf16(TOK, HALF)] * 4, (weights, *rows), scratch, after)
-
-
-def finish_kernel(half, own, *refs):
+    outs = [bf16(TOK, PARTS[part + 1] - PARTS[part])] * 4
+    return call(kernel, "combine", outs, (weights, *rows), scratch, after)
+
+
+def finish_kernel(part, own, *refs):
     blocks, out = refs[:4], refs[4]
-    mixed = own[:, half * HALF : (half + 1) * HALF].astype(jnp.float32)
+    mixed = own[:, PARTS[part] : PARTS[part + 1]].astype(jnp.float32)
     for block in blocks:
         mixed = mixed + block[...].astype(jnp.float32)
     out[...] = mixed.astype(jnp.bfloat16)
@@ -232,10 +233,11 @@
     def send(block, route):
         return lax.ppermute(block, "expert", route)
 
+    given = (own, routes_a[0].T, gates_a[0].T)
     packed = pl.pallas_call(
         pack_kernel,
         out_shape=bf16(TOK, D + TOK),
-        in_specs=[ANY] * 3,
+        in_specs=[HBM] * 3,
         out_specs=VMEM,
         scratch_shapes=[
             pltpu.VMEM((TOP, TOK), jnp.int32),
@@ -244,7 +246,7 @@
         ],
         compiler_params=pltpu.CompilerParams(vmem_limit_bytes=16 << 20),
         name="pack",
-    )(own, routes_a[0].T, gates_a[0].T)
+    )(*[pltpu.with_memory_space_constraint(a, pltpu.HBM) for a in given])
     tokens = [packed] + [send(packed, gather_route(d)) for d in STEPS]
     spread, slots = call(
         slots_kernel,
@@ -260,34 +262,57 @@
         return send(block, back(slot_route(*TARGETS[i])))
 
     results = [None] * len(TARGETS)
-    near_rows = fill_slots(spread, tokens, 2, 4)
+    far_rows = fill_slots(spread, tokens, 6, 2)
+    far = [out(i + 6, block) for i, block in enumerate(far_rows)]
+    near_rows = fill_slots(spread, tokens, 2, 4, after=(far_rows[0],))
     near = [out(i + 2, block) for i, block in enumerate(near_rows)]
-    far = fill_slots(spread, tokens, 6, 2, after=(near_rows[0],))
-    far = [out(i + 6, block) for i, block in enumerate(far)]
     here = list(fill_slots(spread, tokens, 0, 2))
     here[1] = out(1, here[1])
     weights = call(weights_kernel, "weights", bf16(2, 2 * TOK, len(TARGETS) * PAIR), (ids, slots))
-    after = ()
-    for n, rows in ((2, near[0:2]), (4, near[2:4]), (6, far), (0, here)):
-        done = expert_forward(rows, expert, after)
+    for n, rows in ((6, far), (4, near[2:4]), (2, near[0:2]), (0, here)):
+        done = expert_forward(rows, expert)
         results[n : n + 2] = [
             block if n + i == 0 else home(n + i, block) for i, block in enumerate(done)
         ]
     count = lax.axis_size("section")
     onward = [((i - 1) % count, i) for i in range(count)]
     moved, after = [], ()
-    for half in range(2):
-        partial = combine(weights, results, half, after)
+    for part in range(len(PARTS) - 1):
+        partial = combine(weights, results, part, after)
         after = (partial[0],)
         arrived = [send(block, back(gather_route(d))) for d, block in zip(STEPS, partial[1:])]
         layer_a = call(
-            functools.partial(finish_kernel, half),
+            functools.partial(finish_kernel, part),
             "finish",
-            bf16(TOK, HALF),
+            bf16(TOK, PARTS[part + 1] - PARTS[part]),
             (packed, partial[0], *arrived),
         )
         moved.append(lax.ppermute(layer_a, "section", onward))
-    return jnp.concatenate(moved, axis=1)[None]
+    joined = None
+    for part, block in enumerate(moved):
+        joined = join(block, part, joined)
+    return joined[None]
+
+
+def join_kernel(part, block, *refs):
+    out, sem = refs[-2:]
+    copy = pltpu.make_async_copy(block, out.at[:, pl.ds(PARTS[part], PARTS[part + 1] - PARTS[part])], sem)
+    copy.start()
+    copy.wait()
+
+
+def join(block, part, joined):
+    args = (block,) if joined is None else (block, joined)
+    return pl.pallas_call(
+        functools.partial(join_kernel, part),
+        out_shape=bf16(TOK, D),
+        in_specs=[VMEM, HBM][: len(args)],
+        out_specs=HBM,
+        scratch_shapes=[pltpu.SemaphoreType.DMA(())],
+        input_output_aliases={} if joined is None else {1: 0},
+        compiler_params=pltpu.CompilerParams(vmem_limit_bytes=16 << 20),
+        name="join",
+    )(*args)
 
 
 def solution(mesh):

time: 115 us -> 113 us (0.983)
  Pallas kernels: 18.6 us -> 21.1 us
  local copies, waits for them, and re-layouts: 2.51 us -> 0.1 us
  waiting for transfers between devices: 59.4 us -> 57.8 us
    pallas_call x1 -> x3, Pallas kernels: 0.08 us -> 2.52 us  [the longest x2 1.42 us: join(): pl.pallas_call(functools.partial(join_kernel, part), out_shape=bf16(TOK,...]
    unnamed x12 -> x6, local copies, waits for them, and re-layouts: 2.43 us -> 0.01 us
  transfers between devices with their start and end apart: 25 -> 25, of which waited for: 14 -> 14; matrix products, arithmetic and copies ran while one was open for 0% -> 0% of each run, Pallas kernels for 13% -> 15%
where the time goes in v3:
time: 113 us; the launch traced here: 112 us
  waiting for transfers between devices  57.8 us (51%)
  starting transfers between devices  33.2 us (29%)
  Pallas kernels  21.1 us (19%)
    ppermute x23, waiting for transfers between devices, send(): return lax.ppermute(block, 'expert', route)  50.2 us
    ppermute x23, starting transfers between devices, send(): return lax.ppermute(block, 'expert', route)  29.2 us
    pallas_call x13, Pallas kernels, call(): pl.pallas_call(body, out_shape=out_shape, in_specs=[SMEM if a.dtype == jn...  18.6 us
    ppermute x2, waiting for transfers between devices, on_device(): moved.append(lax.ppermute(layer_a, 'section', onward))  7.57 us
    ppermute x2, starting transfers between devices, on_device(): moved.append(lax.ppermute(layer_a, 'section', onward))  3.99 us
  transfers between devices with their start and end apart: 25, of which 14 were waited for; matrix products, arithmetic and copies ran while one was open for 0% of the time, Pallas kernels for 15%

profile of v3, /device:TPU:8, one launch (start us, length us, event | category | flops | bytes accessed | tf_op | source)
XLA Modules:
  0.0 112.5 jit_solution(693069699031757635)
XLA Ops:
  1.1 1.6 %collective-permute-start = (bf16[128,2176]{1,0:T(8,128)(2,1)S(1)}, bf16[128,2176]{1,0:T(8,128)(2,1)S(1)}, u32[]{:S(2)}, u32[]{:S(2)}) collective-permute-start(bf16[128,2176]{1,0:T(8,128)(2,1)S(1)} %pack.1.refs_1_.refs_0_), channel_id=1, source_target_pairs={{0,8},{1,3},{2,10},{3,5},{4,12},{5,7},{6,14},{7,1},{8,16},{9,11},{... | collective-permute-start | bytes 1671176 | tf_op jit(solution)/shard_map/ppermute | solution.py:234
  2.7 1.7 %collective-permute-start.1 = (bf16[128,2176]{1,0:T(8,128)(2,1)S(1)}, bf16[128,2176]{1,0:T(8,128)(2,1)S(1)}, u32[]{:S(2)}, u32[]{:S(2)}) collective-permute-start(bf16[128,2176]{1,0:T(8,128)(2,1)S(1)} %pack.1.refs_1_.refs_0_), channel_id=1, source_target_pairs={{0,24},{1,7},{2,26},{3,1},{4,28},{5,3},{6,30},{7,5},{8,0},{9,15},{... | collective-permute-start | bytes 1671176 | tf_op jit(solution)/shard_map/ppermute | solution.py:234
  4.4 1.8 %collective-permute-start.2 = (bf16[128,2176]{1,0:T(8,128)(2,1)S(1)}, bf16[128,2176]{1,0:T(8,128)(2,1)S(1)}, u32[]{:S(2)}, u32[]{:S(2)}) collective-permute-start(bf16[128,2176]{1,0:T(8,128)(2,1)S(1)} %pack.1.refs_1_.refs_0_), channel_id=1, source_target_pairs={{0,16},{1,5},{2,18},{3,7},{4,20},{5,1},{6,22},{7,3},{8,24},{9,13},... | collective-permute-start | bytes 1671176 | tf_op jit(solution)/shard_map/ppermute | solution.py:234
  6.3 5.6 %collective-permute-done.refs_2_ = bf16[128,2176]{1,0:T(8,128)(2,1)S(1)} collective-permute-done((bf16[128,2176]{1,0:T(8,128)(2,1)S(1)}, bf16[128,2176]{1,0:T(8,128)(2,1)S(1)}, u32[]{:S(2)}, u32[]{:S(2)}) %collective-permute-start) | collective-permute-done | bytes 557088 | tf_op jit(solution)/shard_map/ppermute | solution.py:234
  11.9 5.5 %collective-permute-done.1.refs_3_ = bf16[128,2176]{1,0:T(8,128)(2,1)S(1)} collective-permute-done((bf16[128,2176]{1,0:T(8,128)(2,1)S(1)}, bf16[128,2176]{1,0:T(8,128)(2,1)S(1)}, u32[]{:S(2)}, u32[]{:S(2)}) %collective-permute-start.1) | collective-permute-done | bytes 557088 | tf_op jit(solution)/shard_map/ppermute | solution.py:234
  17.5 1.4 %collective-permute-done.2.refs_4_ = bf16[128,2176]{1,0:T(8,128)(2,1)S(1)} collective-permute-done((bf16[128,2176]{1,0:T(8,128)(2,1)S(1)}, bf16[128,2176]{1,0:T(8,128)(2,1)S(1)}, u32[]{:S(2)}, u32[]{:S(2)}) %collective-permute-start.2) | collective-permute-done | bytes 557088 | tf_op jit(solution)/shard_map/ppermute | solution.py:234
  20.2 2.4 %collective-permute-start.13 = (bf16[160,2048]{1,0:T(8,128)(2,1)S(1)}, bf16[160,2048]{1,0:T(8,128)(2,1)S(1)}, u32[]{:S(2)}, u32[]{:S(2)}) collective-permute-start(bf16[160,2048]{1,0:T(8,128)(2,1)S(1)} %get-tuple-element.37.refs_5_), channel_id=1, source_target_pairs={{0,4},{1,17},{2,6},{3,19},{4,0},{5,21},{6,2},{7,23},{8,12},{9,25},... | collective-permute-start | bytes 1966088 | tf_op jit(solution)/shard_map/ppermute | solution.py:234
  23.7 1.7 %collective-permute-start.10 = (bf16[160,2048]{1,0:T(8,128)(2,1)S(1)}, bf16[160,2048]{1,0:T(8,128)(2,1)S(1)}, u32[]{:S(2)}, u32[]{:S(2)}) collective-permute-start(bf16[160,2048]{1,0:T(8,128)(2,1)S(1)} %get-tuple-element.43), channel_id=1, source_target_pairs={{0,7},{1,24},{2,1},{3,26},{4,3},{5,28},{6,5},{7,30},{8,15},{9,0},{... | collective-permute-start | bytes 1966088 | tf_op jit(solution)/shard_map/ppermute | solution.py:234
  27.4 5.0 %collective-permute-done.13.refs_0_ = bf16[160,2048]{1,0:T(8,128)(2,1)S(1)} collective-permute-done((bf16[160,2048]{1,0:T(8,128)(2,1)S(1)}, bf16[160,2048]{1,0:T(8,128)(2,1)S(1)}, u32[]{:S(2)}, u32[]{:S(2)}) %collective-permute-start.13) | collective-permute-done | bytes 655392 | tf_op jit(solution)/shard_map/ppermute | solution.py:234
  33.0 4.8 %collective-permute-done.14.refs_1_ = bf16[160,2048]{1,0:T(8,128)(2,1)S(1)} collective-permute-done((bf16[160,2048]{1,0:T(8,128)(2,1)S(1)}, bf16[160,2048]{1,0:T(8,128)(2,1)S(1)}, u32[]{:S(2)}, u32[]{:S(2)}) %collective-permute-start.14) | collective-permute-done | bytes 655392 | tf_op jit(solution)/shard_map/ppermute | solution.py:234
  37.7 1.6 %collective-permute-start.3 = (bf16[160,2048]{1,0:T(8,128)(2,1)S(1)}, bf16[160,2048]{1,0:T(8,128)(2,1)S(1)}, u32[]{:S(2)}, u32[]{:S(2)}) collective-permute-start(bf16[160,2048]{1,0:T(8,128)(2,1)S(1)} %get-tuple-element.34), channel_id=1, source_target_pairs={{0,1},{1,0},{2,3},{3,2},{4,5},{5,4},{6,7},{7,6},{8,9},{9,8},{10,11... | collective-permute-start | bytes 1966088 | tf_op jit(solution)/shard_map/ppermute | solution.py:234
  39.3 3.2 %expert.7 = (bf16[160,2048]{1,0:T(8,128)(2,1)S(1)}, bf16[160,2048]{1,0:T(8,128)(2,1)S(1)}) custom-call(bf16[160,2048]{1,0:T(8,128)(2,1)S(1)} %collective-permute-done.13.refs_0_, bf16[160,2048]{1,0:T(8,128)(2,1)S(1)} %collective-permute-done.14.refs_1_, bf16[2048,768]{1,0:T(8,128)(2,1)S(1)} %bitcast.19, bf16[2048,768]{1,0:T(8,128)(2,1)S(1)} %bitcast.23, ...), custom_call_target="tpu_custom_call" | custom-call | flops 3019898880 | tf_op jit(solution)/shard_map/expert/pallas_call | solution.py:73
  42.5 2.2 %collective-permute-done.10.refs_1_ = bf16[160,2048]{1,0:T(8,128)(2,1)S(1)} collective-permute-done((bf16[160,2048]{1,0:T(8,128)(2,1)S(1)}, bf16[160,2048]{1,0:T(8,128)(2,1)S(1)}, u32[]{:S(2)}, u32[]{:S(2)}) %collective-permute-start.10) | collective-permute-done | bytes 655392 | tf_op jit(solution)/shard_map/ppermute | solution.py:234
  44.8 1.2 %collective-permute-start.15 = (bf16[160,2048]{1,0:T(8,128)(2,1)S(1)}, bf16[160,2048]{1,0:T(8,128)(2,1)S(1)}, u32[]{:S(2)}, u32[]{:S(2)}) collective-permute-start(bf16[160,2048]{1,0:T(8,128)(2,1)S(1)} %get-tuple-element.47), channel_id=1, source_target_pairs={{4,0},{17,1},{6,2},{19,3},{0,4},{21,5},{2,6},{23,7},{12,8},{25,9},... | collective-permute-start | bytes 1966088 | tf_op jit(solution)/shard_map/ppermute | solution.py:234
  46.0 7.4 %collective-permute-done.9.refs_0_ = bf16[160,2048]{1,0:T(8,128)(2,1)S(1)} collective-permute-done((bf16[160,2048]{1,0:T(8,128)(2,1)S(1)}, bf16[160,2048]{1,0:T(8,128)(2,1)S(1)}, u32[]{:S(2)}, u32[]{:S(2)}) %collective-permute-start.9) | collective-permute-done | bytes 655392 | tf_op jit(solution)/shard_map/ppermute | solution.py:234
  53.4 3.2 %expert.6 = (bf16[160,2048]{1,0:T(8,128)(2,1)S(1)}, bf16[160,2048]{1,0:T(8,128)(2,1)S(1)}) custom-call(bf16[160,2048]{1,0:T(8,128)(2,1)S(1)} %collective-permute-done.9.refs_0_, bf16[160,2048]{1,0:T(8,128)(2,1)S(1)} %collective-permute-done.10.refs_1_, bf16[2048,768]{1,0:T(8,128)(2,1)S(1)} %bitcast.20, bf16[2048,768]{1,0:T(8,128)(2,1)S(1)} %bitcast.24, ...), custom_call_target="tpu_custom_call" | custom-call | flops 3019898880 | tf_op jit(solution)/shard_map/expert/pallas_call | solution.py:73
  57.4 2.9 %collective-permute-start.12 = (bf16[160,2048]{1,0:T(8,128)(2,1)S(1)}, bf16[160,2048]{1,0:T(8,128)(2,1)S(1)}, u32[]{:S(2)}, u32[]{:S(2)}) collective-permute-start(bf16[160,2048]{1,0:T(8,128)(2,1)S(1)} %get-tuple-element.45), channel_id=1, source_target_pairs={{7,0},{24,1},{1,2},{26,3},{3,4},{28,5},{5,6},{30,7},{15,8},{0,9},{... | collective-permute-start | bytes 1966088 | tf_op jit(solution)/shard_map/ppermute | solution.py:234
  60.3 3.2 %expert.5 = (bf16[160,2048]{1,0:T(8,128)(2,1)S(1)}, bf16[160,2048]{1,0:T(8,128)(2,1)S(1)}) custom-call(bf16[160,2048]{1,0:T(8,128)(2,1)S(1)} %collective-permute-done.5.refs_0_, bf16[160,2048]{1,0:T(8,128)(2,1)S(1)} %collective-permute-done.6.refs_1_, bf16[2048,768]{1,0:T(8,128)(2,1)S(1)} %bitcast.21, bf16[2048,768]{1,0:T(8,128)(2,1)S(1)} %bitcast.25, ...), custom_call_target="tpu_custom_call" | custom-call | flops 3019898880 | tf_op jit(solution)/shard_map/expert/pallas_call | solution.py:73
  64.0 3.2 %expert.4 = (bf16[160,2048]{1,0:T(8,128)(2,1)S(1)}, bf16[160,2048]{1,0:T(8,128)(2,1)S(1)}) custom-call(bf16[160,2048]{1,0:T(8,128)(2,1)S(1)} %get-tuple-element.33.refs_0_, bf16[160,2048]{1,0:T(8,128)(2,1)S(1)} %collective-permute-done.3.refs_1_, bf16[2048,768]{1,0:T(8,128)(2,1)S(1)} %bitcast.22, bf16[2048,768]{1,0:T(8,128)(2,1)S(1)} %bitcast.26, ...), custom_call_target="tpu_custom_call" | custom-call | flops 3019898880 | tf_op jit(solution)/shard_map/expert/pallas_call | solution.py:73
  67.2 1.9 %collective-permute-start.8 = (bf16[160,2048]{1,0:T(8,128)(2,1)S(1)}, bf16[160,2048]{1,0:T(8,128)(2,1)S(1)}, u32[]{:S(2)}, u32[]{:S(2)}) collective-permute-start(bf16[160,2048]{1,0:T(8,128)(2,1)S(1)} %get-tuple-element.41), channel_id=1, source_target_pairs={{3,0},{8,1},{5,2},{10,3},{7,4},{12,5},{1,6},{14,7},{11,8},{16,9},{... | collective-permute-start | bytes 1966088 | tf_op jit(solution)/shard_map/ppermute | solution.py:234
  70.2 10.3 %collective-permute-done.11.refs_5_ = bf16[160,2048]{1,0:T(8,128)(2,1)S(1)} collective-permute-done((bf16[160,2048]{1,0:T(8,128)(2,1)S(1)}, bf16[160,2048]{1,0:T(8,128)(2,1)S(1)}, u32[]{:S(2)}, u32[]{:S(2)}) %collective-permute-start.11) | collective-permute-done | bytes 655392 | tf_op jit(solution)/shard_map/ppermute | solution.py:234
  80.6 1.2 %collective-permute-done.12.refs_6_ = bf16[160,2048]{1,0:T(8,128)(2,1)S(1)} collective-permute-done((bf16[160,2048]{1,0:T(8,128)(2,1)S(1)}, bf16[160,2048]{1,0:T(8,128)(2,1)S(1)}, u32[]{:S(2)}, u32[]{:S(2)}) %collective-permute-start.12) | collective-permute-done | bytes 655392 | tf_op jit(solution)/shard_map/ppermute | solution.py:234
  82.8 2.3 %collective-permute-start.21 = (bf16[128,1024]{1,0:T(8,128)(2,1)S(1)}, bf16[128,1024]{1,0:T(8,128)(2,1)S(1)}, u32[]{:S(2)}, u32[]{:S(2)}) collective-permute-start(bf16[128,1024]{1,0:T(8,128)(2,1)S(1)} %get-tuple-element.54), channel_id=1, source_target_pairs={{8,0},{3,1},{10,2},{5,3},{12,4},{7,5},{14,6},{1,7},{16,8},{11,9},{... | collective-permute-start | bytes 786440 | tf_op jit(solution)/shard_map/ppermute | solution.py:234
  85.1 2.1 %collective-permute-start.23 = (bf16[128,1024]{1,0:T(8,128)(2,1)S(1)}, bf16[128,1024]{1,0:T(8,128)(2,1)S(1)}, u32[]{:S(2)}, u32[]{:S(2)}) collective-permute-start(bf16[128,1024]{1,0:T(8,128)(2,1)S(1)} %get-tuple-element.56), channel_id=1, source_target_pairs={{16,0},{5,1},{18,2},{7,3},{20,4},{1,5},{22,6},{3,7},{24,8},{13,9},... | collective-permute-start | bytes 786440 | tf_op jit(solution)/shard_map/ppermute | solution.py:234
  88.2 1.9 %collective-permute-start.17 = (bf16[128,1024]{1,0:T(8,128)(2,1)S(1)}, bf16[128,1024]{1,0:T(8,128)(2,1)S(1)}, u32[]{:S(2)}, u32[]{:S(2)}) collective-permute-start(bf16[128,1024]{1,0:T(8,128)(2,1)S(1)} %get-tuple-element.51), channel_id=1, source_target_pairs={{8,0},{3,1},{10,2},{5,3},{12,4},{7,5},{14,6},{1,7},{16,8},{11,9},{... | collective-permute-start | bytes 786440 | tf_op jit(solution)/shard_map/ppermute | solution.py:234
  90.4 2.0 %collective-permute-start.19 = (bf16[128,1024]{1,0:T(8,128)(2,1)S(1)}, bf16[128,1024]{1,0:T(8,128)(2,1)S(1)}, u32[]{:S(2)}, u32[]{:S(2)}) collective-permute-start(bf16[128,1024]{1,0:T(8,128)(2,1)S(1)} %get-tuple-element.53), channel_id=1, source_target_pairs={{16,0},{5,1},{18,2},{7,3},{20,4},{1,5},{22,6},{3,7},{24,8},{13,9},... | collective-permute-start | bytes 786440 | tf_op jit(solution)/shard_map/ppermute | solution.py:234
  92.4 3.2 %collective-permute-done.22.refs_3_ = bf16[128,1024]{1,0:T(8,128)(2,1)S(1)} collective-permute-done((bf16[128,1024]{1,0:T(8,128)(2,1)S(1)}, bf16[128,1024]{1,0:T(8,128)(2,1)S(1)}, u32[]{:S(2)}, u32[]{:S(2)}) %collective-permute-start.22) | collective-permute-done | bytes 262176 | tf_op jit(solution)/shard_map/ppermute | solution.py:234
  95.7 2.0 %collective-permute-start.24 = (bf16[128,1024]{1,0:T(8,128)(2,1)S(1)}, bf16[128,1024]{1,0:T(8,128)(2,1)S(1)}, u32[]{:S(2)}, u32[]{:S(2)}) collective-permute-start(bf16[128,1024]{1,0:T(8,128)(2,1)S(1)} %finish.3), channel_id=1, source_target_pairs={{224,0},{0,32},{32,64},{64,96},{96,128},{128,160},{160,192},{192,2... | collective-permute-start | bytes 786440 | tf_op jit(solution)/shard_map/ppermute | solution.py:290
  97.7 3.4 %collective-permute-done.18.refs_3_ = bf16[128,1024]{1,0:T(8,128)(2,1)S(1)} collective-permute-done((bf16[128,1024]{1,0:T(8,128)(2,1)S(1)}, bf16[128,1024]{1,0:T(8,128)(2,1)S(1)}, u32[]{:S(2)}, u32[]{:S(2)}) %collective-permute-start.18) | collective-permute-done | bytes 262176 | tf_op jit(solution)/shard_map/ppermute | solution.py:234
  101.3 2.0 %collective-permute-start.20 = (bf16[128,1024]{1,0:T(8,128)(2,1)S(1)}, bf16[128,1024]{1,0:T(8,128)(2,1)S(1)}, u32[]{:S(2)}, u32[]{:S(2)}) collective-permute-start(bf16[128,1024]{1,0:T(8,128)(2,1)S(1)} %finish.2), channel_id=1, source_target_pairs={{224,0},{0,32},{32,64},{64,96},{96,128},{128,160},{160,192},{192,2... | collective-permute-start | bytes 786440 | tf_op jit(solution)/shard_map/ppermute | solution.py:290
  103.3 5.3 %collective-permute-done.24.block = bf16[128,1024]{1,0:T(8,128)(2,1)S(1)} collective-permute-done((bf16[128,1024]{1,0:T(8,128)(2,1)S(1)}, bf16[128,1024]{1,0:T(8,128)(2,1)S(1)}, u32[]{:S(2)}, u32[]{:S(2)}) %collective-permute-start.24) | collective-permute-done | bytes 262176 | tf_op jit(solution)/shard_map/ppermute | solution.py:290
  109.3 2.2 %collective-permute-done.20.block = bf16[128,1024]{1,0:T(8,128)(2,1)S(1)} collective-permute-done((bf16[128,1024]{1,0:T(8,128)(2,1)S(1)}, bf16[128,1024]{1,0:T(8,128)(2,1)S(1)}, u32[]{:S(2)}, u32[]{:S(2)}) %collective-permute-start.20) | collective-permute-done | bytes 262176 | tf_op jit(solution)/shard_map/ppermute | solution.py:290
  (41 shorter events, 12.5 us)
Async XLA Ops:
  1.1 10.8 %collective-permute-start = (bf16[128,2176]{1,0:T(8,128)(2,1)S(1)}, bf16[128,2176]{1,0:T(8,128)(2,1)S(1)}, u32[]{:S(2)}, u32[]{:S(2)}) collective-permute-start(bf16[128,2176]{1,0:T(8,128)(2,1)S(1)} %pack.1.refs_1_.refs_0_), channel_id=1, source_target_pairs={{0,8},{1,3},{2,10},{3,5},{4,12},{5,7},{6,14},{7,1},{8,16},{9,11},{... | collective-permute-start | bytes 1671176 | tf_op jit(solution)/shard_map/ppermute | solution.py:234
  2.7 14.8 %collective-permute-start.1 = (bf16[128,2176]{1,0:T(8,128)(2,1)S(1)}, bf16[128,2176]{1,0:T(8,128)(2,1)S(1)}, u32[]{:S(2)}, u32[]{:S(2)}) collective-permute-start(bf16[128,2176]{1,0:T(8,128)(2,1)S(1)} %pack.1.refs_1_.refs_0_), channel_id=1, source_target_pairs={{0,24},{1,7},{2,26},{3,1},{4,28},{5,3},{6,30},{7,5},{8,0},{9,15},{... | collective-permute-start | bytes 1671176 | tf_op jit(solution)/shard_map/ppermute | solution.py:234
  4.4 14.5 %collective-permute-start.2 = (bf16[128,2176]{1,0:T(8,128)(2,1)S(1)}, bf16[128,2176]{1,0:T(8,128)(2,1)S(1)}, u32[]{:S(2)}, u32[]{:S(2)}) collective-permute-start(bf16[128,2176]{1,0:T(8,128)(2,1)S(1)} %pack.1.refs_1_.refs_0_), channel_id=1, source_target_pairs={{0,16},{1,5},{2,18},{3,7},{4,20},{5,1},{6,22},{7,3},{8,24},{9,13},... | collective-permute-start | bytes 1671176 | tf_op jit(solution)/shard_map/ppermute | solution.py:234
  18.9 20.4 %copy-start.2 = (bf16[1,1,768,2048]{3,2,1,0:T(8,128)(2,1)S(1)}, bf16[1,1,768,2048]{3,2,1,0:T(8,128)(2,1)}, u32[]{:S(2)}) copy-start(bf16[1,1,768,2048]{3,2,1,0:T(8,128)(2,1)} %param.11) | copy-start | bytes 9437188
  20.2 12.3 %collective-permute-start.13 = (bf16[160,2048]{1,0:T(8,128)(2,1)S(1)}, bf16[160,2048]{1,0:T(8,128)(2,1)S(1)}, u32[]{:S(2)}, u32[]{:S(2)}) collective-permute-start(bf16[160,2048]{1,0:T(8,128)(2,1)S(1)} %get-tuple-element.37.refs_5_), channel_id=1, source_target_pairs={{0,4},{1,17},{2,6},{3,19},{4,0},{5,21},{6,2},{7,23},{8,12},{9,25},... | collective-permute-start | bytes 1966088 | tf_op jit(solution)/shard_map/ppermute | solution.py:234
  22.6 16.7 %copy-start = (bf16[1,1,2048,768]{3,2,1,0:T(8,128)(2,1)S(1)}, bf16[1,1,2048,768]{3,2,1,0:T(8,128)(2,1)}, u32[]{:S(2)}) copy-start(bf16[1,1,2048,768]{3,2,1,0:T(8,128)(2,1)} %param.9) | copy-start | bytes 9437188
  22.6 16.7 %copy-start.1 = (bf16[1,1,2048,768]{3,2,1,0:T(8,128)(2,1)S(1)}, bf16[1,1,2048,768]{3,2,1,0:T(8,128)(2,1)}, u32[]{:S(2)}) copy-start(bf16[1,1,2048,768]{3,2,1,0:T(8,128)(2,1)} %param.10) | copy-start | bytes 9437188
  22.6 15.2 %collective-permute-start.14 = (bf16[160,2048]{1,0:T(8,128)(2,1)S(1)}, bf16[160,2048]{1,0:T(8,128)(2,1)S(1)}, u32[]{:S(2)}, u32[]{:S(2)}) collective-permute-start(bf16[160,2048]{1,0:T(8,128)(2,1)S(1)} %get-tuple-element.46), channel_id=1, source_target_pairs={{0,5},{1,16},{2,7},{3,18},{4,1},{5,20},{6,3},{7,22},{8,13},{9,24},... | collective-permute-start | bytes 1966088 | tf_op jit(solution)/shard_map/ppermute | solution.py:234
  23.7 21.1 %collective-permute-start.10 = (bf16[160,2048]{1,0:T(8,128)(2,1)S(1)}, bf16[160,2048]{1,0:T(8,128)(2,1)S(1)}, u32[]{:S(2)}, u32[]{:S(2)}) collective-permute-start(bf16[160,2048]{1,0:T(8,128)(2,1)S(1)} %get-tuple-element.43), channel_id=1, source_target_pairs={{0,7},{1,24},{2,1},{3,26},{4,3},{5,28},{6,5},{7,30},{8,15},{9,0},{... | collective-permute-start | bytes 1966088 | tf_op jit(solution)/shard_map/ppermute | solution.py:234
  25.4 28.0 %collective-permute-start.9 = (bf16[160,2048]{1,0:T(8,128)(2,1)S(1)}, bf16[160,2048]{1,0:T(8,128)(2,1)S(1)}, u32[]{:S(2)}, u32[]{:S(2)}) collective-permute-start(bf16[160,2048]{1,0:T(8,128)(2,1)S(1)} %get-tuple-element.42), channel_id=1, source_target_pairs={{0,6},{1,25},{2,0},{3,27},{4,2},{5,29},{6,4},{7,31},{8,14},{9,1},{... | collective-permute-start | bytes 1966088 | tf_op jit(solution)/shard_map/ppermute | solution.py:234
  26.4 30.2 %collective-permute-start.5 = (bf16[160,2048]{1,0:T(8,128)(2,1)S(1)}, bf16[160,2048]{1,0:T(8,128)(2,1)S(1)}, u32[]{:S(2)}, u32[]{:S(2)}) collective-permute-start(bf16[160,2048]{1,0:T(8,128)(2,1)S(1)} %get-tuple-element.38), channel_id=1, source_target_pairs={{0,2},{1,9},{2,4},{3,11},{4,6},{5,13},{6,0},{7,15},{8,10},{9,17},{... | collective-permute-start | bytes 1966088 | tf_op jit(solution)/shard_map/ppermute | solution.py:234
  32.5 24.9 %collective-permute-start.6 = (bf16[160,2048]{1,0:T(8,128)(2,1)S(1)}, bf16[160,2048]{1,0:T(8,128)(2,1)S(1)}, u32[]{:S(2)}, u32[]{:S(2)}) collective-permute-start(bf16[160,2048]{1,0:T(8,128)(2,1)S(1)} %get-tuple-element.39), channel_id=1, source_target_pairs={{0,3},{1,8},{2,5},{3,10},{4,7},{5,12},{6,1},{7,14},{8,11},{9,16},{... | collective-permute-start | bytes 1966088 | tf_op jit(solution)/shard_map/ppermute | solution.py:234
  37.7 25.8 %collective-permute-start.3 = (bf16[160,2048]{1,0:T(8,128)(2,1)S(1)}, bf16[160,2048]{1,0:T(8,128)(2,1)S(1)}, u32[]{:S(2)}, u32[]{:S(2)}) collective-permute-start(bf16[160,2048]{1,0:T(8,128)(2,1)S(1)} %get-tuple-element.34), channel_id=1, source_target_pairs={{0,1},{1,0},{2,3},{3,2},{4,5},{5,4},{6,7},{7,6},{8,9},{9,8},{10,11... | collective-permute-start | bytes 1966088 | tf_op jit(solution)/shard_map/ppermute | solution.py:234
  44.8 22.4 %collective-permute-start.15 = (bf16[160,2048]{1,0:T(8,128)(2,1)S(1)}, bf16[160,2048]{1,0:T(8,128)(2,1)S(1)}, u32[]{:S(2)}, u32[]{:S(2)}) collective-permute-start(bf16[160,2048]{1,0:T(8,128)(2,1)S(1)} %get-tuple-element.47), channel_id=1, source_target_pairs={{4,0},{17,1},{6,2},{19,3},{0,4},{21,5},{2,6},{23,7},{12,8},{25,9},... | collective-permute-start | bytes 1966088 | tf_op jit(solution)/shard_map/ppermute | solution.py:234
  53.4 15.7 %collective-permute-start.16 = (bf16[160,2048]{1,0:T(8,128)(2,1)S(1)}, bf16[160,2048]{1,0:T(8,128)(2,1)S(1)}, u32[]{:S(2)}, u32[]{:S(2)}) collective-permute-start(bf16[160,2048]{1,0:T(8,128)(2,1)S(1)} %get-tuple-element.48), channel_id=1, source_target_pairs={{5,0},{16,1},{7,2},{18,3},{1,4},{20,5},{3,6},{22,7},{13,8},{24,9},... | collective-permute-start | bytes 1966088 | tf_op jit(solution)/shard_map/ppermute | solution.py:234
  56.7 23.9 %collective-permute-start.11 = (bf16[160,2048]{1,0:T(8,128)(2,1)S(1)}, bf16[160,2048]{1,0:T(8,128)(2,1)S(1)}, u32[]{:S(2)}, u32[]{:S(2)}) collective-permute-start(bf16[160,2048]{1,0:T(8,128)(2,1)S(1)} %get-tuple-element.44), channel_id=1, source_target_pairs={{6,0},{25,1},{0,2},{27,3},{2,4},{29,5},{4,6},{31,7},{14,8},{1,9},{... | collective-permute-start | bytes 1966088 | tf_op jit(solution)/shard_map/ppermute | solution.py:234
  57.4 24.4 %collective-permute-start.12 = (bf16[160,2048]{1,0:T(8,128)(2,1)S(1)}, bf16[160,2048]{1,0:T(8,128)(2,1)S(1)}, u32[]{:S(2)}, u32[]{:S(2)}) collective-permute-start(bf16[160,2048]{1,0:T(8,128)(2,1)S(1)} %get-tuple-element.45), channel_id=1, source_target_pairs={{7,0},{24,1},{1,2},{26,3},{3,4},{28,5},{5,6},{30,7},{15,8},{0,9},{... | collective-permute-start | bytes 1966088 | tf_op jit(solution)/shard_map/ppermute | solution.py:234
  63.5 18.2 %collective-permute-start.7 = (bf16[160,2048]{1,0:T(8,128)(2,1)S(1)}, bf16[160,2048]{1,0:T(8,128)(2,1)S(1)}, u32[]{:S(2)}, u32[]{:S(2)}) collective-permute-start(bf16[160,2048]{1,0:T(8,128)(2,1)S(1)} %get-tuple-element.40), channel_id=1, source_target_pairs={{2,0},{9,1},{4,2},{11,3},{6,4},{13,5},{0,6},{15,7},{10,8},{17,9},{... | collective-permute-start | bytes 1966088 | tf_op jit(solution)/shard_map/ppermute | solution.py:234
  67.2 14.6 %collective-permute-start.8 = (bf16[160,2048]{1,0:T(8,128)(2,1)S(1)}, bf16[160,2048]{1,0:T(8,128)(2,1)S(1)}, u32[]{:S(2)}, u32[]{:S(2)}) collective-permute-start(bf16[160,2048]{1,0:T(8,128)(2,1)S(1)} %get-tuple-element.41), channel_id=1, source_target_pairs={{3,0},{8,1},{5,2},{10,3},{7,4},{12,5},{1,6},{14,7},{11,8},{16,9},{... | collective-permute-start | bytes 1966088 | tf_op jit(solution)/shard_map/ppermute | solution.py:234
  69.1 12.7 %collective-permute-start.4 = (bf16[160,2048]{1,0:T(8,128)(2,1)S(1)}, bf16[160,2048]{1,0:T(8,128)(2,1)S(1)}, u32[]{:S(2)}, u32[]{:S(2)}) collective-permute-start(bf16[160,2048]{1,0:T(8,128)(2,1)S(1)} %get-tuple-element.36), channel_id=1, source_target_pairs={{1,0},{0,1},{3,2},{2,3},{5,4},{4,5},{7,6},{6,7},{9,8},{8,9},{11,10... | collective-permute-start | bytes 1966088 | tf_op jit(solution)/shard_map/ppermute | solution.py:234
  82.8 7.6 %collective-permute-start.21 = (bf16[128,1024]{1,0:T(8,128)(2,1)S(1)}, bf16[128,1024]{1,0:T(8,128)(2,1)S(1)}, u32[]{:S(2)}, u32[]{:S(2)}) collective-permute-start(bf16[128,1024]{1,0:T(8,128)(2,1)S(1)} %get-tuple-element.54), channel_id=1, source_target_pairs={{8,0},{3,1},{10,2},{5,3},{12,4},{7,5},{14,6},{1,7},{16,8},{11,9},{... | collective-permute-start | bytes 786440 | tf_op jit(solution)/shard_map/ppermute | solution.py:234
  85.1 10.4 %collective-permute-start.22 = (bf16[128,1024]{1,0:T(8,128)(2,1)S(1)}, bf16[128,1024]{1,0:T(8,128)(2,1)S(1)}, u32[]{:S(2)}, u32[]{:S(2)}) collective-permute-start(bf16[128,1024]{1,0:T(8,128)(2,1)S(1)} %get-tuple-element.55), channel_id=1, source_target_pairs={{24,0},{7,1},{26,2},{1,3},{28,4},{3,5},{30,6},{5,7},{0,8},{15,9},{... | collective-permute-start | bytes 786440 | tf_op jit(solution)/shard_map/ppermute | solution.py:234
  85.1 10.4 %collective-permute-start.23 = (bf16[128,1024]{1,0:T(8,128)(2,1)S(1)}, bf16[128,1024]{1,0:T(8,128)(2,1)S(1)}, u32[]{:S(2)}, u32[]{:S(2)}) collective-permute-start(bf16[128,1024]{1,0:T(8,128)(2,1)S(1)} %get-tuple-element.56), channel_id=1, source_target_pairs={{16,0},{5,1},{18,2},{7,3},{20,4},{1,5},{22,6},{3,7},{24,8},{13,9},... | collective-permute-start | bytes 786440 | tf_op jit(solution)/shard_map/ppermute | solution.py:234
  88.2 9.5 %collective-permute-start.17 = (bf16[128,1024]{1,0:T(8,128)(2,1)S(1)}, bf16[128,1024]{1,0:T(8,128)(2,1)S(1)}, u32[]{:S(2)}, u32[]{:S(2)}) collective-permute-start(bf16[128,1024]{1,0:T(8,128)(2,1)S(1)} %get-tuple-element.51), channel_id=1, source_target_pairs={{8,0},{3,1},{10,2},{5,3},{12,4},{7,5},{14,6},{1,7},{16,8},{11,9},{... | collective-permute-start | bytes 786440 | tf_op jit(solution)/shard_map/ppermute | solution.py:234
  90.1 11.1 %collective-permute-start.18 = (bf16[128,1024]{1,0:T(8,128)(2,1)S(1)}, bf16[128,1024]{1,0:T(8,128)(2,1)S(1)}, u32[]{:S(2)}, u32[]{:S(2)}) collective-permute-start(bf16[128,1024]{1,0:T(8,128)(2,1)S(1)} %get-tuple-element.52), channel_id=1, source_target_pairs={{24,0},{7,1},{26,2},{1,3},{28,4},{3,5},{30,6},{5,7},{0,8},{15,9},{... | collective-permute-start | bytes 786440 | tf_op jit(solution)/shard_map/ppermute | solution.py:234
  90.4 10.8 %collective-permute-start.19 = (bf16[128,1024]{1,0:T(8,128)(2,1)S(1)}, bf16[128,1024]{1,0:T(8,128)(2,1)S(1)}, u32[]{:S(2)}, u32[]{:S(2)}) collective-permute-start(bf16[128,1024]{1,0:T(8,128)(2,1)S(1)} %get-tuple-element.53), channel_id=1, source_target_pairs={{16,0},{5,1},{18,2},{7,3},{20,4},{1,5},{22,6},{3,7},{24,8},{13,9},... | collective-permute-start | bytes 786440 | tf_op jit(solution)/shard_map/ppermute | solution.py:234
  95.7 12.9 %collective-permute-start.24 = (bf16[128,1024]{1,0:T(8,128)(2,1)S(1)}, bf16[128,1024]{1,0:T(8,128)(2,1)S(1)}, u32[]{:S(2)}, u32[]{:S(2)}) collective-permute-start(bf16[128,1024]{1,0:T(8,128)(2,1)S(1)} %finish.3), channel_id=1, source_target_pairs={{224,0},{0,32},{32,64},{64,96},{96,128},{128,160},{160,192},{192,2... | collective-permute-start | bytes 786440 | tf_op jit(solution)/shard_map/ppermute | solution.py:290
  101.3 10.3 %collective-permute-start.20 = (bf16[128,1024]{1,0:T(8,128)(2,1)S(1)}, bf16[128,1024]{1,0:T(8,128)(2,1)S(1)}, u32[]{:S(2)}, u32[]{:S(2)}) collective-permute-start(bf16[128,1024]{1,0:T(8,128)(2,1)S(1)} %finish.2), channel_id=1, source_target_pairs={{224,0},{0,32},{32,64},{64,96},{96,128},{128,160},{160,192},{192,2... | collective-permute-start | bytes 786440 | tf_op jit(solution)/shard_map/ppermute | solution.py:290

commit v4 on v3

--- a/solution.py
+++ b/solution.py
@@ -214,7 +214,7 @@
     kernel = functools.partial(combine_kernel, part)
     scratch = [pltpu.VMEM((len(TARGETS) * PAIR, 2 * TILE), jnp.bfloat16)]
     outs = [bf16(TOK, PARTS[part + 1] - PARTS[part])] * 4
-    return call(kernel, "combine", outs, (weights, *rows), scratch, after)
+    return call(kernel, "combine", outs, (weights, *rows), scratch, after, 1 << 30)
 
 
 def finish_kernel(part, own, *refs):

time: 113 us -> 113 us (level)
  no operation moved by 1% of the time
where the time goes in v4:
time: 113 us; the launch traced here: 112 us
  waiting for transfers between devices  57.8 us (51%)
  starting transfers between devices  33.2 us (29%)
  Pallas kernels  21.1 us (19%)
    ppermute x23, waiting for transfers between devices, send(): return lax.ppermute(block, 'expert', route)  50.2 us
    ppermute x23, starting transfers between devices, send(): return lax.ppermute(block, 'expert', route)  29.2 us
    pallas_call x13, Pallas kernels, call(): pl.pallas_call(body, out_shape=out_shape, in_specs=[SMEM if a.dtype == jn...  18.6 us
    ppermute x2, waiting for transfers between devices, on_device(): moved.append(lax.ppermute(layer_a, 'section', onward))  7.57 us
    ppermute x2, starting transfers between devices, on_device(): moved.append(lax.ppermute(layer_a, 'section', onward))  3.99 us
  transfers between devices with their start and end apart: 25, of which 14 were waited for; matrix products, arithmetic and copies ran while one was open for 0% of the time, Pallas kernels for 15%

profile of v4, /device:TPU:8, one launch (start us, length us, event | category | flops | bytes accessed | tf_op | source)
XLA Modules:
  0.0 112.5 jit_solution(693069699031757635)
XLA Ops:
  1.1 1.6 %collective-permute-start = (bf16[128,2176]{1,0:T(8,128)(2,1)S(1)}, bf16[128,2176]{1,0:T(8,128)(2,1)S(1)}, u32[]{:S(2)}, u32[]{:S(2)}) collective-permute-start(bf16[128,2176]{1,0:T(8,128)(2,1)S(1)} %pack.1.refs_1_.refs_0_), channel_id=1, source_target_pairs={{0,8},{1,3},{2,10},{3,5},{4,12},{5,7},{6,14},{7,1},{8,16},{9,11},{... | collective-permute-start | bytes 1671176 | tf_op jit(solution)/shard_map/ppermute | solution.py:234
  2.7 1.7 %collective-permute-start.1 = (bf16[128,2176]{1,0:T(8,128)(2,1)S(1)}, bf16[128,2176]{1,0:T(8,128)(2,1)S(1)}, u32[]{:S(2)}, u32[]{:S(2)}) collective-permute-start(bf16[128,2176]{1,0:T(8,128)(2,1)S(1)} %pack.1.refs_1_.refs_0_), channel_id=1, source_target_pairs={{0,24},{1,7},{2,26},{3,1},{4,28},{5,3},{6,30},{7,5},{8,0},{9,15},{... | collective-permute-start | bytes 1671176 | tf_op jit(solution)/shard_map/ppermute | solution.py:234
  4.4 1.8 %collective-permute-start.2 = (bf16[128,2176]{1,0:T(8,128)(2,1)S(1)}, bf16[128,2176]{1,0:T(8,128)(2,1)S(1)}, u32[]{:S(2)}, u32[]{:S(2)}) collective-permute-start(bf16[128,2176]{1,0:T(8,128)(2,1)S(1)} %pack.1.refs_1_.refs_0_), channel_id=1, source_target_pairs={{0,16},{1,5},{2,18},{3,7},{4,20},{5,1},{6,22},{7,3},{8,24},{9,13},... | collective-permute-start | bytes 1671176 | tf_op jit(solution)/shard_map/ppermute | solution.py:234
  6.3 5.6 %collective-permute-done.refs_2_ = bf16[128,2176]{1,0:T(8,128)(2,1)S(1)} collective-permute-done((bf16[128,2176]{1,0:T(8,128)(2,1)S(1)}, bf16[128,2176]{1,0:T(8,128)(2,1)S(1)}, u32[]{:S(2)}, u32[]{:S(2)}) %collective-permute-start) | collective-permute-done | bytes 557088 | tf_op jit(solution)/shard_map/ppermute | solution.py:234
  11.9 5.5 %collective-permute-done.1.refs_3_ = bf16[128,2176]{1,0:T(8,128)(2,1)S(1)} collective-permute-done((bf16[128,2176]{1,0:T(8,128)(2,1)S(1)}, bf16[128,2176]{1,0:T(8,128)(2,1)S(1)}, u32[]{:S(2)}, u32[]{:S(2)}) %collective-permute-start.1) | collective-permute-done | bytes 557088 | tf_op jit(solution)/shard_map/ppermute | solution.py:234
  17.5 1.4 %collective-permute-done.2.refs_4_ = bf16[128,2176]{1,0:T(8,128)(2,1)S(1)} collective-permute-done((bf16[128,2176]{1,0:T(8,128)(2,1)S(1)}, bf16[128,2176]{1,0:T(8,128)(2,1)S(1)}, u32[]{:S(2)}, u32[]{:S(2)}) %collective-permute-start.2) | collective-permute-done | bytes 557088 | tf_op jit(solution)/shard_map/ppermute | solution.py:234
  20.2 2.4 %collective-permute-start.13 = (bf16[160,2048]{1,0:T(8,128)(2,1)S(1)}, bf16[160,2048]{1,0:T(8,128)(2,1)S(1)}, u32[]{:S(2)}, u32[]{:S(2)}) collective-permute-start(bf16[160,2048]{1,0:T(8,128)(2,1)S(1)} %get-tuple-element.37.refs_5_), channel_id=1, source_target_pairs={{0,4},{1,17},{2,6},{3,19},{4,0},{5,21},{6,2},{7,23},{8,12},{9,25},... | collective-permute-start | bytes 1966088 | tf_op jit(solution)/shard_map/ppermute | solution.py:234
  23.7 1.7 %collective-permute-start.10 = (bf16[160,2048]{1,0:T(8,128)(2,1)S(1)}, bf16[160,2048]{1,0:T(8,128)(2,1)S(1)}, u32[]{:S(2)}, u32[]{:S(2)}) collective-permute-start(bf16[160,2048]{1,0:T(8,128)(2,1)S(1)} %get-tuple-element.43), channel_id=1, source_target_pairs={{0,7},{1,24},{2,1},{3,26},{4,3},{5,28},{6,5},{7,30},{8,15},{9,0},{... | collective-permute-start | bytes 1966088 | tf_op jit(solution)/shard_map/ppermute | solution.py:234
  27.4 5.0 %collective-permute-done.13.refs_0_ = bf16[160,2048]{1,0:T(8,128)(2,1)S(1)} collective-permute-done((bf16[160,2048]{1,0:T(8,128)(2,1)S(1)}, bf16[160,2048]{1,0:T(8,128)(2,1)S(1)}, u32[]{:S(2)}, u32[]{:S(2)}) %collective-permute-start.13) | collective-permute-done | bytes 655392 | tf_op jit(solution)/shard_map/ppermute | solution.py:234
  33.0 4.8 %collective-permute-done.14.refs_1_ = bf16[160,2048]{1,0:T(8,128)(2,1)S(1)} collective-permute-done((bf16[160,2048]{1,0:T(8,128)(2,1)S(1)}, bf16[160,2048]{1,0:T(8,128)(2,1)S(1)}, u32[]{:S(2)}, u32[]{:S(2)}) %collective-permute-start.14) | collective-permute-done | bytes 655392 | tf_op jit(solution)/shard_map/ppermute | solution.py:234
  37.7 1.6 %collective-permute-start.3 = (bf16[160,2048]{1,0:T(8,128)(2,1)S(1)}, bf16[160,2048]{1,0:T(8,128)(2,1)S(1)}, u32[]{:S(2)}, u32[]{:S(2)}) collective-permute-start(bf16[160,2048]{1,0:T(8,128)(2,1)S(1)} %get-tuple-element.34), channel_id=1, source_target_pairs={{0,1},{1,0},{2,3},{3,2},{4,5},{5,4},{6,7},{7,6},{8,9},{9,8},{10,11... | collective-permute-start | bytes 1966088 | tf_op jit(solution)/shard_map/ppermute | solution.py:234
  39.3 3.2 %expert.7 = (bf16[160,2048]{1,0:T(8,128)(2,1)S(1)}, bf16[160,2048]{1,0:T(8,128)(2,1)S(1)}) custom-call(bf16[160,2048]{1,0:T(8,128)(2,1)S(1)} %collective-permute-done.13.refs_0_, bf16[160,2048]{1,0:T(8,128)(2,1)S(1)} %collective-permute-done.14.refs_1_, bf16[2048,768]{1,0:T(8,128)(2,1)S(1)} %bitcast.19, bf16[2048,768]{1,0:T(8,128)(2,1)S(1)} %bitcast.23, ...), custom_call_target="tpu_custom_call" | custom-call | flops 3019898880 | tf_op jit(solution)/shard_map/expert/pallas_call | solution.py:73
  42.5 2.2 %collective-permute-done.10.refs_1_ = bf16[160,2048]{1,0:T(8,128)(2,1)S(1)} collective-permute-done((bf16[160,2048]{1,0:T(8,128)(2,1)S(1)}, bf16[160,2048]{1,0:T(8,128)(2,1)S(1)}, u32[]{:S(2)}, u32[]{:S(2)}) %collective-permute-start.10) | collective-permute-done | bytes 655392 | tf_op jit(solution)/shard_map/ppermute | solution.py:234
  44.8 1.2 %collective-permute-start.15 = (bf16[160,2048]{1,0:T(8,128)(2,1)S(1)}, bf16[160,2048]{1,0:T(8,128)(2,1)S(1)}, u32[]{:S(2)}, u32[]{:S(2)}) collective-permute-start(bf16[160,2048]{1,0:T(8,128)(2,1)S(1)} %get-tuple-element.47), channel_id=1, source_target_pairs={{4,0},{17,1},{6,2},{19,3},{0,4},{21,5},{2,6},{23,7},{12,8},{25,9},... | collective-permute-start | bytes 1966088 | tf_op jit(solution)/shard_map/ppermute | solution.py:234
  46.0 7.4 %collective-permute-done.9.refs_0_ = bf16[160,2048]{1,0:T(8,128)(2,1)S(1)} collective-permute-done((bf16[160,2048]{1,0:T(8,128)(2,1)S(1)}, bf16[160,2048]{1,0:T(8,128)(2,1)S(1)}, u32[]{:S(2)}, u32[]{:S(2)}) %collective-permute-start.9) | collective-permute-done | bytes 655392 | tf_op jit(solution)/shard_map/ppermute | solution.py:234
  53.4 3.2 %expert.6 = (bf16[160,2048]{1,0:T(8,128)(2,1)S(1)}, bf16[160,2048]{1,0:T(8,128)(2,1)S(1)}) custom-call(bf16[160,2048]{1,0:T(8,128)(2,1)S(1)} %collective-permute-done.9.refs_0_, bf16[160,2048]{1,0:T(8,128)(2,1)S(1)} %collective-permute-done.10.refs_1_, bf16[2048,768]{1,0:T(8,128)(2,1)S(1)} %bitcast.20, bf16[2048,768]{1,0:T(8,128)(2,1)S(1)} %bitcast.24, ...), custom_call_target="tpu_custom_call" | custom-call | flops 3019898880 | tf_op jit(solution)/shard_map/expert/pallas_call | solution.py:73
  57.4 2.9 %collective-permute-start.12 = (bf16[160,2048]{1,0:T(8,128)(2,1)S(1)}, bf16[160,2048]{1,0:T(8,128)(2,1)S(1)}, u32[]{:S(2)}, u32[]{:S(2)}) collective-permute-start(bf16[160,2048]{1,0:T(8,128)(2,1)S(1)} %get-tuple-element.45), channel_id=1, source_target_pairs={{7,0},{24,1},{1,2},{26,3},{3,4},{28,5},{5,6},{30,7},{15,8},{0,9},{... | collective-permute-start | bytes 1966088 | tf_op jit(solution)/shard_map/ppermute | solution.py:234
  60.3 3.2 %expert.5 = (bf16[160,2048]{1,0:T(8,128)(2,1)S(1)}, bf16[160,2048]{1,0:T(8,128)(2,1)S(1)}) custom-call(bf16[160,2048]{1,0:T(8,128)(2,1)S(1)} %collective-permute-done.5.refs_0_, bf16[160,2048]{1,0:T(8,128)(2,1)S(1)} %collective-permute-done.6.refs_1_, bf16[2048,768]{1,0:T(8,128)(2,1)S(1)} %bitcast.21, bf16[2048,768]{1,0:T(8,128)(2,1)S(1)} %bitcast.25, ...), custom_call_target="tpu_custom_call" | custom-call | flops 3019898880 | tf_op jit(solution)/shard_map/expert/pallas_call | solution.py:73
  64.0 3.2 %expert.4 = (bf16[160,2048]{1,0:T(8,128)(2,1)S(1)}, bf16[160,2048]{1,0:T(8,128)(2,1)S(1)}) custom-call(bf16[160,2048]{1,0:T(8,128)(2,1)S(1)} %get-tuple-element.33.refs_0_, bf16[160,2048]{1,0:T(8,128)(2,1)S(1)} %collective-permute-done.3.refs_1_, bf16[2048,768]{1,0:T(8,128)(2,1)S(1)} %bitcast.22, bf16[2048,768]{1,0:T(8,128)(2,1)S(1)} %bitcast.26, ...), custom_call_target="tpu_custom_call" | custom-call | flops 3019898880 | tf_op jit(solution)/shard_map/expert/pallas_call | solution.py:73
  67.2 1.9 %collective-permute-start.8 = (bf16[160,2048]{1,0:T(8,128)(2,1)S(1)}, bf16[160,2048]{1,0:T(8,128)(2,1)S(1)}, u32[]{:S(2)}, u32[]{:S(2)}) collective-permute-start(bf16[160,2048]{1,0:T(8,128)(2,1)S(1)} %get-tuple-element.41), channel_id=1, source_target_pairs={{3,0},{8,1},{5,2},{10,3},{7,4},{12,5},{1,6},{14,7},{11,8},{16,9},{... | collective-permute-start | bytes 1966088 | tf_op jit(solution)/shard_map/ppermute | solution.py:234
  70.2 10.3 %collective-permute-done.11.refs_5_ = bf16[160,2048]{1,0:T(8,128)(2,1)S(1)} collective-permute-done((bf16[160,2048]{1,0:T(8,128)(2,1)S(1)}, bf16[160,2048]{1,0:T(8,128)(2,1)S(1)}, u32[]{:S(2)}, u32[]{:S(2)}) %collective-permute-start.11) | collective-permute-done | bytes 655392 | tf_op jit(solution)/shard_map/ppermute | solution.py:234
  80.6 1.2 %collective-permute-done.12.refs_6_ = bf16[160,2048]{1,0:T(8,128)(2,1)S(1)} collective-permute-done((bf16[160,2048]{1,0:T(8,128)(2,1)S(1)}, bf16[160,2048]{1,0:T(8,128)(2,1)S(1)}, u32[]{:S(2)}, u32[]{:S(2)}) %collective-permute-start.12) | collective-permute-done | bytes 655392 | tf_op jit(solution)/shard_map/ppermute | solution.py:234
  82.8 2.3 %collective-permute-start.21 = (bf16[128,1024]{1,0:T(8,128)(2,1)S(1)}, bf16[128,1024]{1,0:T(8,128)(2,1)S(1)}, u32[]{:S(2)}, u32[]{:S(2)}) collective-permute-start(bf16[128,1024]{1,0:T(8,128)(2,1)S(1)} %get-tuple-element.54), channel_id=1, source_target_pairs={{8,0},{3,1},{10,2},{5,3},{12,4},{7,5},{14,6},{1,7},{16,8},{11,9},{... | collective-permute-start | bytes 786440 | tf_op jit(solution)/shard_map/ppermute | solution.py:234
  85.1 2.1 %collective-permute-start.23 = (bf16[128,1024]{1,0:T(8,128)(2,1)S(1)}, bf16[128,1024]{1,0:T(8,128)(2,1)S(1)}, u32[]{:S(2)}, u32[]{:S(2)}) collective-permute-start(bf16[128,1024]{1,0:T(8,128)(2,1)S(1)} %get-tuple-element.56), channel_id=1, source_target_pairs={{16,0},{5,1},{18,2},{7,3},{20,4},{1,5},{22,6},{3,7},{24,8},{13,9},... | collective-permute-start | bytes 786440 | tf_op jit(solution)/shard_map/ppermute | solution.py:234
  88.2 1.9 %collective-permute-start.17 = (bf16[128,1024]{1,0:T(8,128)(2,1)S(1)}, bf16[128,1024]{1,0:T(8,128)(2,1)S(1)}, u32[]{:S(2)}, u32[]{:S(2)}) collective-permute-start(bf16[128,1024]{1,0:T(8,128)(2,1)S(1)} %get-tuple-element.51), channel_id=1, source_target_pairs={{8,0},{3,1},{10,2},{5,3},{12,4},{7,5},{14,6},{1,7},{16,8},{11,9},{... | collective-permute-start | bytes 786440 | tf_op jit(solution)/shard_map/ppermute | solution.py:234
  90.4 2.0 %collective-permute-start.19 = (bf16[128,1024]{1,0:T(8,128)(2,1)S(1)}, bf16[128,1024]{1,0:T(8,128)(2,1)S(1)}, u32[]{:S(2)}, u32[]{:S(2)}) collective-permute-start(bf16[128,1024]{1,0:T(8,128)(2,1)S(1)} %get-tuple-element.53), channel_id=1, source_target_pairs={{16,0},{5,1},{18,2},{7,3},{20,4},{1,5},{22,6},{3,7},{24,8},{13,9},... | collective-permute-start | bytes 786440 | tf_op jit(solution)/shard_map/ppermute | solution.py:234
  92.4 3.2 %collective-permute-done.22.refs_3_ = bf16[128,1024]{1,0:T(8,128)(2,1)S(1)} collective-permute-done((bf16[128,1024]{1,0:T(8,128)(2,1)S(1)}, bf16[128,1024]{1,0:T(8,128)(2,1)S(1)}, u32[]{:S(2)}, u32[]{:S(2)}) %collective-permute-start.22) | collective-permute-done | bytes 262176 | tf_op jit(solution)/shard_map/ppermute | solution.py:234
  95.7 2.0 %collective-permute-start.24 = (bf16[128,1024]{1,0:T(8,128)(2,1)S(1)}, bf16[128,1024]{1,0:T(8,128)(2,1)S(1)}, u32[]{:S(2)}, u32[]{:S(2)}) collective-permute-start(bf16[128,1024]{1,0:T(8,128)(2,1)S(1)} %finish.3), channel_id=1, source_target_pairs={{224,0},{0,32},{32,64},{64,96},{96,128},{128,160},{160,192},{192,2... | collective-permute-start | bytes 786440 | tf_op jit(solution)/shard_map/ppermute | solution.py:290
  97.7 3.4 %collective-permute-done.18.refs_3_ = bf16[128,1024]{1,0:T(8,128)(2,1)S(1)} collective-permute-done((bf16[128,1024]{1,0:T(8,128)(2,1)S(1)}, bf16[128,1024]{1,0:T(8,128)(2,1)S(1)}, u32[]{:S(2)}, u32[]{:S(2)}) %collective-permute-start.18) | collective-permute-done | bytes 262176 | tf_op jit(solution)/shard_map/ppermute | solution.py:234
  101.3 2.0 %collective-permute-start.20 = (bf16[128,1024]{1,0:T(8,128)(2,1)S(1)}, bf16[128,1024]{1,0:T(8,128)(2,1)S(1)}, u32[]{:S(2)}, u32[]{:S(2)}) collective-permute-start(bf16[128,1024]{1,0:T(8,128)(2,1)S(1)} %finish.2), channel_id=1, source_target_pairs={{224,0},{0,32},{32,64},{64,96},{96,128},{128,160},{160,192},{192,2... | collective-permute-start | bytes 786440 | tf_op jit(solution)/shard_map/ppermute | solution.py:290
  103.3 5.3 %collective-permute-done.24.block = bf16[128,1024]{1,0:T(8,128)(2,1)S(1)} collective-permute-done((bf16[128,1024]{1,0:T(8,128)(2,1)S(1)}, bf16[128,1024]{1,0:T(8,128)(2,1)S(1)}, u32[]{:S(2)}, u32[]{:S(2)}) %collective-permute-start.24) | collective-permute-done | bytes 262176 | tf_op jit(solution)/shard_map/ppermute | solution.py:290
  109.3 2.2 %collective-permute-done.20.block = bf16[128,1024]{1,0:T(8,128)(2,1)S(1)} collective-permute-done((bf16[128,1024]{1,0:T(8,128)(2,1)S(1)}, bf16[128,1024]{1,0:T(8,128)(2,1)S(1)}, u32[]{:S(2)}, u32[]{:S(2)}) %collective-permute-start.20) | collective-permute-done | bytes 262176 | tf_op jit(solution)/shard_map/ppermute | solution.py:290
  (41 shorter events, 12.5 us)
Async XLA Ops:
  1.1 10.8 %collective-permute-start = (bf16[128,2176]{1,0:T(8,128)(2,1)S(1)}, bf16[128,2176]{1,0:T(8,128)(2,1)S(1)}, u32[]{:S(2)}, u32[]{:S(2)}) collective-permute-start(bf16[128,2176]{1,0:T(8,128)(2,1)S(1)} %pack.1.refs_1_.refs_0_), channel_id=1, source_target_pairs={{0,8},{1,3},{2,10},{3,5},{4,12},{5,7},{6,14},{7,1},{8,16},{9,11},{... | collective-permute-start | bytes 1671176 | tf_op jit(solution)/shard_map/ppermute | solution.py:234
  2.7 14.8 %collective-permute-start.1 = (bf16[128,2176]{1,0:T(8,128)(2,1)S(1)}, bf16[128,2176]{1,0:T(8,128)(2,1)S(1)}, u32[]{:S(2)}, u32[]{:S(2)}) collective-permute-start(bf16[128,2176]{1,0:T(8,128)(2,1)S(1)} %pack.1.refs_1_.refs_0_), channel_id=1, source_target_pairs={{0,24},{1,7},{2,26},{3,1},{4,28},{5,3},{6,30},{7,5},{8,0},{9,15},{... | collective-permute-start | bytes 1671176 | tf_op jit(solution)/shard_map/ppermute | solution.py:234
  4.4 14.5 %collective-permute-start.2 = (bf16[128,2176]{1,0:T(8,128)(2,1)S(1)}, bf16[128,2176]{1,0:T(8,128)(2,1)S(1)}, u32[]{:S(2)}, u32[]{:S(2)}) collective-permute-start(bf16[128,2176]{1,0:T(8,128)(2,1)S(1)} %pack.1.refs_1_.refs_0_), channel_id=1, source_target_pairs={{0,16},{1,5},{2,18},{3,7},{4,20},{5,1},{6,22},{7,3},{8,24},{9,13},... | collective-permute-start | bytes 1671176 | tf_op jit(solution)/shard_map/ppermute | solution.py:234
  18.9 20.4 %copy-start.2 = (bf16[1,1,768,2048]{3,2,1,0:T(8,128)(2,1)S(1)}, bf16[1,1,768,2048]{3,2,1,0:T(8,128)(2,1)}, u32[]{:S(2)}) copy-start(bf16[1,1,768,2048]{3,2,1,0:T(8,128)(2,1)} %param.11) | copy-start | bytes 9437188
  20.2 12.3 %collective-permute-start.13 = (bf16[160,2048]{1,0:T(8,128)(2,1)S(1)}, bf16[160,2048]{1,0:T(8,128)(2,1)S(1)}, u32[]{:S(2)}, u32[]{:S(2)}) collective-permute-start(bf16[160,2048]{1,0:T(8,128)(2,1)S(1)} %get-tuple-element.37.refs_5_), channel_id=1, source_target_pairs={{0,4},{1,17},{2,6},{3,19},{4,0},{5,21},{6,2},{7,23},{8,12},{9,25},... | collective-permute-start | bytes 1966088 | tf_op jit(solution)/shard_map/ppermute | solution.py:234
  22.6 16.7 %copy-start = (bf16[1,1,2048,768]{3,2,1,0:T(8,128)(2,1)S(1)}, bf16[1,1,2048,768]{3,2,1,0:T(8,128)(2,1)}, u32[]{:S(2)}) copy-start(bf16[1,1,2048,768]{3,2,1,0:T(8,128)(2,1)} %param.9) | copy-start | bytes 9437188
  22.6 16.7 %copy-start.1 = (bf16[1,1,2048,768]{3,2,1,0:T(8,128)(2,1)S(1)}, bf16[1,1,2048,768]{3,2,1,0:T(8,128)(2,1)}, u32[]{:S(2)}) copy-start(bf16[1,1,2048,768]{3,2,1,0:T(8,128)(2,1)} %param.10) | copy-start | bytes 9437188
  22.6 15.2 %collective-permute-start.14 = (bf16[160,2048]{1,0:T(8,128)(2,1)S(1)}, bf16[160,2048]{1,0:T(8,128)(2,1)S(1)}, u32[]{:S(2)}, u32[]{:S(2)}) collective-permute-start(bf16[160,2048]{1,0:T(8,128)(2,1)S(1)} %get-tuple-element.46), channel_id=1, source_target_pairs={{0,5},{1,16},{2,7},{3,18},{4,1},{5,20},{6,3},{7,22},{8,13},{9,24},... | collective-permute-start | bytes 1966088 | tf_op jit(solution)/shard_map/ppermute | solution.py:234
  23.7 21.1 %collective-permute-start.10 = (bf16[160,2048]{1,0:T(8,128)(2,1)S(1)}, bf16[160,2048]{1,0:T(8,128)(2,1)S(1)}, u32[]{:S(2)}, u32[]{:S(2)}) collective-permute-start(bf16[160,2048]{1,0:T(8,128)(2,1)S(1)} %get-tuple-element.43), channel_id=1, source_target_pairs={{0,7},{1,24},{2,1},{3,26},{4,3},{5,28},{6,5},{7,30},{8,15},{9,0},{... | collective-permute-start | bytes 1966088 | tf_op jit(solution)/shard_map/ppermute | solution.py:234
  25.4 28.0 %collective-permute-start.9 = (bf16[160,2048]{1,0:T(8,128)(2,1)S(1)}, bf16[160,2048]{1,0:T(8,128)(2,1)S(1)}, u32[]{:S(2)}, u32[]{:S(2)}) collective-permute-start(bf16[160,2048]{1,0:T(8,128)(2,1)S(1)} %get-tuple-element.42), channel_id=1, source_target_pairs={{0,6},{1,25},{2,0},{3,27},{4,2},{5,29},{6,4},{7,31},{8,14},{9,1},{... | collective-permute-start | bytes 1966088 | tf_op jit(solution)/shard_map/ppermute | solution.py:234
  26.4 30.2 %collective-permute-start.5 = (bf16[160,2048]{1,0:T(8,128)(2,1)S(1)}, bf16[160,2048]{1,0:T(8,128)(2,1)S(1)}, u32[]{:S(2)}, u32[]{:S(2)}) collective-permute-start(bf16[160,2048]{1,0:T(8,128)(2,1)S(1)} %get-tuple-element.38), channel_id=1, source_target_pairs={{0,2},{1,9},{2,4},{3,11},{4,6},{5,13},{6,0},{7,15},{8,10},{9,17},{... | collective-permute-start | bytes 1966088 | tf_op jit(solution)/shard_map/ppermute | solution.py:234
  32.5 24.9 %collective-permute-start.6 = (bf16[160,2048]{1,0:T(8,128)(2,1)S(1)}, bf16[160,2048]{1,0:T(8,128)(2,1)S(1)}, u32[]{:S(2)}, u32[]{:S(2)}) collective-permute-start(bf16[160,2048]{1,0:T(8,128)(2,1)S(1)} %get-tuple-element.39), channel_id=1, source_target_pairs={{0,3},{1,8},{2,5},{3,10},{4,7},{5,12},{6,1},{7,14},{8,11},{9,16},{... | collective-permute-start | bytes 1966088 | tf_op jit(solution)/shard_map/ppermute | solution.py:234
  37.7 25.8 %collective-permute-start.3 = (bf16[160,2048]{1,0:T(8,128)(2,1)S(1)}, bf16[160,2048]{1,0:T(8,128)(2,1)S(1)}, u32[]{:S(2)}, u32[]{:S(2)}) collective-permute-start(bf16[160,2048]{1,0:T(8,128)(2,1)S(1)} %get-tuple-element.34), channel_id=1, source_target_pairs={{0,1},{1,0},{2,3},{3,2},{4,5},{5,4},{6,7},{7,6},{8,9},{9,8},{10,11... | collective-permute-start | bytes 1966088 | tf_op jit(solution)/shard_map/ppermute | solution.py:234
  44.8 22.4 %collective-permute-start.15 = (bf16[160,2048]{1,0:T(8,128)(2,1)S(1)}, bf16[160,2048]{1,0:T(8,128)(2,1)S(1)}, u32[]{:S(2)}, u32[]{:S(2)}) collective-permute-start(bf16[160,2048]{1,0:T(8,128)(2,1)S(1)} %get-tuple-element.47), channel_id=1, source_target_pairs={{4,0},{17,1},{6,2},{19,3},{0,4},{21,5},{2,6},{23,7},{12,8},{25,9},... | collective-permute-start | bytes 1966088 | tf_op jit(solution)/shard_map/ppermute | solution.py:234
  53.4 15.7 %collective-permute-start.16 = (bf16[160,2048]{1,0:T(8,128)(2,1)S(1)}, bf16[160,2048]{1,0:T(8,128)(2,1)S(1)}, u32[]{:S(2)}, u32[]{:S(2)}) collective-permute-start(bf16[160,2048]{1,0:T(8,128)(2,1)S(1)} %get-tuple-element.48), channel_id=1, source_target_pairs={{5,0},{16,1},{7,2},{18,3},{1,4},{20,5},{3,6},{22,7},{13,8},{24,9},... | collective-permute-start | bytes 1966088 | tf_op jit(solution)/shard_map/ppermute | solution.py:234
  56.7 23.9 %collective-permute-start.11 = (bf16[160,2048]{1,0:T(8,128)(2,1)S(1)}, bf16[160,2048]{1,0:T(8,128)(2,1)S(1)}, u32[]{:S(2)}, u32[]{:S(2)}) collective-permute-start(bf16[160,2048]{1,0:T(8,128)(2,1)S(1)} %get-tuple-element.44), channel_id=1, source_target_pairs={{6,0},{25,1},{0,2},{27,3},{2,4},{29,5},{4,6},{31,7},{14,8},{1,9},{... | collective-permute-start | bytes 1966088 | tf_op jit(solution)/shard_map/ppermute | solution.py:234
  57.4 24.4 %collective-permute-start.12 = (bf16[160,2048]{1,0:T(8,128)(2,1)S(1)}, bf16[160,2048]{1,0:T(8,128)(2,1)S(1)}, u32[]{:S(2)}, u32[]{:S(2)}) collective-permute-start(bf16[160,2048]{1,0:T(8,128)(2,1)S(1)} %get-tuple-element.45), channel_id=1, source_target_pairs={{7,0},{24,1},{1,2},{26,3},{3,4},{28,5},{5,6},{30,7},{15,8},{0,9},{... | collective-permute-start | bytes 1966088 | tf_op jit(solution)/shard_map/ppermute | solution.py:234
  63.5 18.2 %collective-permute-start.7 = (bf16[160,2048]{1,0:T(8,128)(2,1)S(1)}, bf16[160,2048]{1,0:T(8,128)(2,1)S(1)}, u32[]{:S(2)}, u32[]{:S(2)}) collective-permute-start(bf16[160,2048]{1,0:T(8,128)(2,1)S(1)} %get-tuple-element.40), channel_id=1, source_target_pairs={{2,0},{9,1},{4,2},{11,3},{6,4},{13,5},{0,6},{15,7},{10,8},{17,9},{... | collective-permute-start | bytes 1966088 | tf_op jit(solution)/shard_map/ppermute | solution.py:234
  67.2 14.6 %collective-permute-start.8 = (bf16[160,2048]{1,0:T(8,128)(2,1)S(1)}, bf16[160,2048]{1,0:T(8,128)(2,1)S(1)}, u32[]{:S(2)}, u32[]{:S(2)}) collective-permute-start(bf16[160,2048]{1,0:T(8,128)(2,1)S(1)} %get-tuple-element.41), channel_id=1, source_target_pairs={{3,0},{8,1},{5,2},{10,3},{7,4},{12,5},{1,6},{14,7},{11,8},{16,9},{... | collective-permute-start | bytes 1966088 | tf_op jit(solution)/shard_map/ppermute | solution.py:234
  69.1 12.7 %collective-permute-start.4 = (bf16[160,2048]{1,0:T(8,128)(2,1)S(1)}, bf16[160,2048]{1,0:T(8,128)(2,1)S(1)}, u32[]{:S(2)}, u32[]{:S(2)}) collective-permute-start(bf16[160,2048]{1,0:T(8,128)(2,1)S(1)} %get-tuple-element.36), channel_id=1, source_target_pairs={{1,0},{0,1},{3,2},{2,3},{5,4},{4,5},{7,6},{6,7},{9,8},{8,9},{11,10... | collective-permute-start | bytes 1966088 | tf_op jit(solution)/shard_map/ppermute | solution.py:234
  82.8 7.6 %collective-permute-start.21 = (bf16[128,1024]{1,0:T(8,128)(2,1)S(1)}, bf16[128,1024]{1,0:T(8,128)(2,1)S(1)}, u32[]{:S(2)}, u32[]{:S(2)}) collective-permute-start(bf16[128,1024]{1,0:T(8,128)(2,1)S(1)} %get-tuple-element.54), channel_id=1, source_target_pairs={{8,0},{3,1},{10,2},{5,3},{12,4},{7,5},{14,6},{1,7},{16,8},{11,9},{... | collective-permute-start | bytes 786440 | tf_op jit(solution)/shard_map/ppermute | solution.py:234
  85.1 10.4 %collective-permute-start.22 = (bf16[128,1024]{1,0:T(8,128)(2,1)S(1)}, bf16[128,1024]{1,0:T(8,128)(2,1)S(1)}, u32[]{:S(2)}, u32[]{:S(2)}) collective-permute-start(bf16[128,1024]{1,0:T(8,128)(2,1)S(1)} %get-tuple-element.55), channel_id=1, source_target_pairs={{24,0},{7,1},{26,2},{1,3},{28,4},{3,5},{30,6},{5,7},{0,8},{15,9},{... | collective-permute-start | bytes 786440 | tf_op jit(solution)/shard_map/ppermute | solution.py:234
  85.1 10.4 %collective-permute-start.23 = (bf16[128,1024]{1,0:T(8,128)(2,1)S(1)}, bf16[128,1024]{1,0:T(8,128)(2,1)S(1)}, u32[]{:S(2)}, u32[]{:S(2)}) collective-permute-start(bf16[128,1024]{1,0:T(8,128)(2,1)S(1)} %get-tuple-element.56), channel_id=1, source_target_pairs={{16,0},{5,1},{18,2},{7,3},{20,4},{1,5},{22,6},{3,7},{24,8},{13,9},... | collective-permute-start | bytes 786440 | tf_op jit(solution)/shard_map/ppermute | solution.py:234
  88.2 9.5 %collective-permute-start.17 = (bf16[128,1024]{1,0:T(8,128)(2,1)S(1)}, bf16[128,1024]{1,0:T(8,128)(2,1)S(1)}, u32[]{:S(2)}, u32[]{:S(2)}) collective-permute-start(bf16[128,1024]{1,0:T(8,128)(2,1)S(1)} %get-tuple-element.51), channel_id=1, source_target_pairs={{8,0},{3,1},{10,2},{5,3},{12,4},{7,5},{14,6},{1,7},{16,8},{11,9},{... | collective-permute-start | bytes 786440 | tf_op jit(solution)/shard_map/ppermute | solution.py:234
  90.1 11.1 %collective-permute-start.18 = (bf16[128,1024]{1,0:T(8,128)(2,1)S(1)}, bf16[128,1024]{1,0:T(8,128)(2,1)S(1)}, u32[]{:S(2)}, u32[]{:S(2)}) collective-permute-start(bf16[128,1024]{1,0:T(8,128)(2,1)S(1)} %get-tuple-element.52), channel_id=1, source_target_pairs={{24,0},{7,1},{26,2},{1,3},{28,4},{3,5},{30,6},{5,7},{0,8},{15,9},{... | collective-permute-start | bytes 786440 | tf_op jit(solution)/shard_map/ppermute | solution.py:234
  90.4 10.8 %collective-permute-start.19 = (bf16[128,1024]{1,0:T(8,128)(2,1)S(1)}, bf16[128,1024]{1,0:T(8,128)(2,1)S(1)}, u32[]{:S(2)}, u32[]{:S(2)}) collective-permute-start(bf16[128,1024]{1,0:T(8,128)(2,1)S(1)} %get-tuple-element.53), channel_id=1, source_target_pairs={{16,0},{5,1},{18,2},{7,3},{20,4},{1,5},{22,6},{3,7},{24,8},{13,9},... | collective-permute-start | bytes 786440 | tf_op jit(solution)/shard_map/ppermute | solution.py:234
  95.7 12.9 %collective-permute-start.24 = (bf16[128,1024]{1,0:T(8,128)(2,1)S(1)}, bf16[128,1024]{1,0:T(8,128)(2,1)S(1)}, u32[]{:S(2)}, u32[]{:S(2)}) collective-permute-start(bf16[128,1024]{1,0:T(8,128)(2,1)S(1)} %finish.3), channel_id=1, source_target_pairs={{224,0},{0,32},{32,64},{64,96},{96,128},{128,160},{160,192},{192,2... | collective-permute-start | bytes 786440 | tf_op jit(solution)/shard_map/ppermute | solution.py:290
  101.3 10.3 %collective-permute-start.20 = (bf16[128,1024]{1,0:T(8,128)(2,1)S(1)}, bf16[128,1024]{1,0:T(8,128)(2,1)S(1)}, u32[]{:S(2)}, u32[]{:S(2)}) collective-permute-start(bf16[128,1024]{1,0:T(8,128)(2,1)S(1)} %finish.2), channel_id=1, source_target_pairs={{224,0},{0,32},{32,64},{64,96},{96,128},{128,160},{160,192},{192,2... | collective-permute-start | bytes 786440 | tf_op jit(solution)/shard_map/ppermute | solution.py:290
